TPU v7x, 32 devices: a whole 2x2x4 slice. The times are simulated.
32 devices in a mesh: row: 4 (over z), col: 8 (over y, x, core).
Axes of the slice: x: 2, y: 2, z: 4, core: 2. Of those that a mesh axis runs over, the one named last changes fastest.
Arguments:
- three_index: float32 [32, 512, 1024], P('col', None, 'row'), may hold values from -1.2 to 1.2
- occ_energy: float32 [32], replicated, may hold values from -2 to -0.5
- vir_energy: float32 [512], replicated, may hold values from 0.5 to 3
- block_mask: int32 [32, 8, 16], replicated, may hold values from 0 to 1, as said below
- pair_list: int32 [32, 4], P('col'), may hold values from -1 to 3, as said below
Outputs:
- response_density: float32 [32, 512, 1024], P('col', None, 'row')
- virtual_density: float32 [512, 512], replicated
Inputs may be any that keep to these rules, and one draw needn't show every extreme that they name: `block_mask`: each orbital keeps between 32 and 64 of its 128 blocks; some orbital keeps exactly 64. `pair_list`: in each row the live entries come first and are distinct, then -1; every orbital lists at least one partner class; some orbital lists 4.
All inputs are finite; a program needn't handle non-finite values.
Results may differ from a plain program's by a relative error of at most 0.0003.
Values sent between devices are 32-bit elements; how exact they have to be, the bound alone decides.
No kernel may reach another device: no remote copies, remote signals or barrier semaphores. Data moves between devices by JAX's collectives and lax.ppermute only.
A program may use at most 128 MiB of HBM per device.

v0:
```python
import functools

import jax
import jax.numpy as jnp
from jax import lax
from jax.experimental import pallas as pl
from jax.experimental.pallas import tpu as pltpu
from jax.sharding import PartitionSpec as P

BLOCK = 64
NPANEL = 4
CHUNKS = 4
TILE = 256
VMEM_LIMIT = 48 * 1024 * 1024
SMEM = pl.BlockSpec(memory_space=pltpu.SMEM)
VMEM = pl.BlockSpec(memory_space=pltpu.VMEM)
NT = (((1,), (1,)), ((), ()))


def call(kernel, name, outs, operands, flops, scratch=(), scalars=0):
    size = sum(at.size * at.dtype.itemsize for at in [*outs, *operands])
    return pl.pallas_call(
        kernel,
        out_shape=outs,
        in_specs=[SMEM] * scalars + [VMEM] * (len(operands) - scalars),
        out_specs=[VMEM] * len(outs),
        scratch_shapes=list(scratch),
        compiler_params=pltpu.CompilerParams(vmem_limit_bytes=VMEM_LIMIT),
        cost_estimate=pl.CostEstimate(flops=flops, bytes_accessed=size, transcendentals=0),
        name=name,
    )(*operands)


def shape(*sizes, kind=jnp.float32):
    return jax.ShapeDtypeStruct(sizes, kind)


def halves(value):
    high = value.astype(jnp.bfloat16)
    return high, (value - high.astype(jnp.float32)).astype(jnp.bfloat16)


def dot(left, right):
    return jnp.dot(left, right, preferred_element_type=jnp.float32)


def dot_nt(left, right):
    return lax.dot_general(left, right, NT, preferred_element_type=jnp.float32)


def split_rows(chunks, mask, high, low):
    for chunk, rows in enumerate(chunks):
        parts, count, width = rows.shape
        for start in range(0, count, BLOCK):
            at = chunk * count + start
            for part in range(parts):
                cols = slice(part * width, (part + 1) * width)
                kept = mask[at // BLOCK : at // BLOCK + 1, cols]
                value = rows[part, start : start + BLOCK, :] * kept
                high[at : at + BLOCK, cols], low[at : at + BLOCK, cols] = halves(value)


def amplitudes(energy, live, vir_col, vir_row, own, panel, amp, a_parts, w_parts):
    nvir = amp.shape[0]
    for start in range(0, nvir, TILE):
        cols = slice(start, start + TILE)
        cross = dot_nt(own[0][...], panel[0][cols, :])
        cross += dot_nt(own[0][...], panel[1][cols, :])
        cross += dot_nt(own[1][...], panel[0][cols, :])
        value = cross / (energy - vir_col[...] - vir_row[:, cols]) * live
        amp[:, cols] = value
        a_parts[0][:, cols], a_parts[1][:, cols] = halves(value)
    for above in range(0, nvir, TILE):
        rows = slice(above, above + TILE)
        for start in range(0, nvir, TILE):
            cols = slice(start, start + TILE)
            value = 2.0 * amp[rows, cols] - amp[cols, rows].T
            w_parts[0][rows, cols], w_parts[1][rows, cols] = halves(value)


def respond(rows, w_parts, panel, cols):
    value = dot(w_parts[0][rows, :], panel[0][:, cols])
    value += dot(w_parts[0][rows, :], panel[1][:, cols])
    return value + dot(w_parts[1][rows, :], panel[0][:, cols])


def density_tile(cols, w_parts, a_parts):
    value = dot_nt(w_parts[0][...], a_parts[0][cols, :])
    value += dot_nt(w_parts[0][...], a_parts[1][cols, :])
    return value + dot_nt(w_parts[1][...], a_parts[0][cols, :])


def early_kernel(scalars, vir_col, vir_row, masks, *refs):
    own, near, twin = (refs[at * CHUNKS : (at + 1) * CHUNKS] for at in range(3))
    refs = refs[3 * CHUNKS :]
    own_high, own_low, response, density = refs[:4]
    m_high, m_low, amp, a_high, a_low, w_high, w_low = refs[4:]
    split_rows(own, masks.at[0], own_high, own_low)
    nvir = amp.shape[0]
    parts, _, width = response.shape
    panel, a_parts, w_parts = (m_high, m_low), (a_high, a_low), (w_high, w_low)
    for turn, chunks in enumerate((near, twin)):
        split_rows(chunks, masks.at[1 + turn], m_high, m_low)
        amplitudes(
            scalars[2 * turn], scalars[2 * turn + 1], vir_col, vir_row,
            (own_high, own_low), panel, amp, a_parts, w_parts,
        )
        for part in range(parts):
            cols = slice(part * width, (part + 1) * width)
            value = respond(slice(0, nvir), w_parts, panel, cols)
            response[part] = value if turn == 0 else response[part] + value
        for start in range(0, nvir, TILE):
            cols = slice(start, start + TILE)
            value = density_tile(cols, w_parts, a_parts)
            density[:, cols] = value if turn == 0 else density[:, cols] + value


def early(scalars, virtual, masks, own, near, twin):
    parts, rows, width = own[0].shape
    nvir, naux = rows * CHUNKS, parts * width
    half = jnp.bfloat16
    outs = [shape(nvir, naux, kind=half)] * 2 + [shape(parts, nvir, width), shape(nvir, nvir)]
    scratch = [pltpu.VMEM((nvir, naux), half)] * 2
    scratch += [pltpu.VMEM((nvir, nvir), jnp.float32)]
    scratch += [pltpu.VMEM((nvir, nvir), half)] * 4
    operands = [scalars, virtual[:, None], virtual[None, :], masks, *own, *near, *twin]
    flops = 2 * 3 * 2 * nvir * nvir * (2 * naux + nvir)
    return call(early_kernel, "early", outs, operands, flops, scratch, 1)


def late_kernel(scalars, vir_col, vir_row, masks, own_high, own_low, *refs):
    sources = refs[:CHUNKS], refs[CHUNKS : 2 * CHUNKS]
    refs = refs[2 * CHUNKS :]
    for turn, chunks in enumerate(sources):
        m_high, m_low, a_high, a_low, w_high, w_low = refs[6 * turn : 6 * turn + 6]
        split_rows(chunks, masks.at[turn], m_high, m_low)
        amplitudes(
            scalars[2 * turn], scalars[2 * turn + 1], vir_col, vir_row,
            (own_high, own_low), (m_high, m_low), refs[12], (a_high, a_low), (w_high, w_low),
        )


def late(scalars, virtual, masks, own, far, twin):
    nvir, naux = own[0].shape
    half = jnp.bfloat16
    outs = ([shape(nvir, naux, kind=half)] * 2 + [shape(nvir, nvir, kind=half)] * 4) * 2
    operands = [scalars, virtual[:, None], virtual[None, :], masks, *own, *far, *twin]
    flops = 2 * 3 * 2 * nvir * nvir * naux
    scratch = [pltpu.VMEM((nvir, nvir), jnp.float32)]
    outs = call(late_kernel, "late", outs, operands, flops, scratch, 1)
    return outs[:6], outs[6:]


def response_kernel(first, before, *refs):
    pieces = refs[8:]
    for piece in pieces:
        parts, count, width = piece.shape
        rows = slice(first, first + count)
        for part in range(parts):
            cols = slice(part * width, (part + 1) * width)
            value = before[part, rows, :]
            for at in (0, 4):
                value += respond(rows, refs[at + 2 : at + 4], refs[at : at + 2], cols)
            piece[part] = value
        first += count


def responses(first, counts, before, panels):
    parts, nvir, width = before.shape
    outs = [shape(parts, count, width) for count in counts]
    operands = [before]
    for m_high, m_low, _, _, w_high, w_low in panels:
        operands += [m_high, m_low, w_high, w_low]
    flops = 2 * 3 * 2 * sum(counts) * nvir * parts * width
    return call(functools.partial(response_kernel, first), "response", outs, operands, flops)


def density_kernel(scale, before, *refs):
    total = refs[8]
    for start in range(0, before.shape[0], TILE):
        cols = slice(start, start + TILE)
        value = before[:, cols]
        for at in (0, 4):
            value += density_tile(cols, refs[at + 2 : at + 4], refs[at : at + 2])
        total[:, cols] = value * scale


def densities(scale, before, panels):
    nvir = before.shape[0]
    operands = [before]
    for _, _, *squares in panels:
        operands += squares
    kernel = functools.partial(density_kernel, scale)
    return call(kernel, "density", [shape(nvir, nvir)], operands, 2 * 3 * 2 * nvir**3)[0]


def exchange(value, axis, bit):
    size = lax.axis_size(axis)
    return lax.ppermute(value, axis, [(at, at ^ bit) for at in range(size)])


def swap_parts(value):
    return lax.all_to_all(value, "row", split_axis=0, concat_axis=0, tiled=True)


def bits(axis):
    size = lax.axis_size(axis)
    return [1 << at for at in range(size.bit_length() - 1)]


def scatter_plane(value):
    for bit in bits("col"):
        half = value.shape[0] // 2
        side = (lax.axis_index("col") // bit) % 2
        kept = lax.dynamic_slice_in_dim(value, side * half, half, 0)
        sent = lax.dynamic_slice_in_dim(value, (1 - side) * half, half, 0)
        value = kept + exchange(sent, "col", bit)
    return value


def sum_row(value):
    terms = [value] + [exchange(value, "row", bit) for bit in range(1, lax.axis_size("row"))]
    while len(terms) > 1:
        terms = [terms[at] + terms[at + 1] for at in range(0, len(terms), 2)]
    return terms[0]


def gather_plane(value):
    for bit in reversed(bits("col")):
        side = (lax.axis_index("col") // bit) % 2
        other = exchange(value, "col", bit)
        value = jnp.where(
            side == 0, jnp.concatenate([value, other]), jnp.concatenate([other, value])
        )
    return value


def on_device(three_index, occ_energy, vir_energy, block_mask, pair_list):
    row = lax.axis_index("row")
    col = lax.axis_index("col")
    row_count = lax.axis_size("row")
    col_count = lax.axis_size("col")
    position = col % NPANEL
    group = col // NPANEL
    groups = col_count // NPANEL
    nvir = three_index.shape[1]
    step = nvir // CHUNKS

    own, near, far, near_twin, far_twin = [], [], [], [], []
    for chunk in range(CHUNKS):
        rows = swap_parts(three_index[:, chunk * step : (chunk + 1) * step, :])
        own.append(rows)
        reach = 1
        while reach < groups:
            count = min(reach, groups - reach) * NPANEL
            links = [(at, at + reach * NPANEL) for at in range(count)]
            got = lax.ppermute(rows, "col", links)
            rows = jnp.where((group >= reach) & (group < 2 * reach), got, rows)
            reach *= 2
        near.append(rows)
        far.append(exchange(rows, "col", 2))
        near_twin.append(exchange(rows, "col", 1))
        far_twin.append(exchange(far[-1], "col", 1))

    own_orbital = col * row_count + row
    panels = [position ^ turn for turn in range(NPANEL)]
    orbitals = jnp.stack([own_orbital] + [at * row_count + row for at in panels])
    masks = jnp.repeat(block_mask[orbitals].astype(jnp.float32), BLOCK, axis=-1)
    lists = pair_list[row]
    scalars = []
    for turn in range(NPANEL):
        live = jnp.any(lists == panels[turn]).astype(jnp.float32)
        scalars += [occ_energy[own_orbital] + occ_energy[orbitals[1 + turn]], live]
    first, second = jnp.stack(scalars[:4]), jnp.stack(scalars[4:])

    own_high, own_low, response, density = early(
        first, vir_energy, masks[:3], own, near, near_twin
    )
    last = late(second, vir_energy, masks[3:], (own_high, own_low), far, far_twin)
    half, quarter = nvir // 2, nvir // 4
    head = responses(0, [half], response, last)
    middle, tail = responses(half, [quarter, quarter], response, last)
    density = densities(1.0 / (row_count * col_count), density, last)

    returned = [swap_parts(head[0])]
    piece = scatter_plane(density)
    piece, middle = lax.optimization_barrier((piece, middle))
    returned.append(swap_parts(middle))
    piece = sum_row(piece)
    piece, tail = lax.optimization_barrier((piece, tail))
    returned.append(swap_parts(tail))
    return jnp.concatenate(returned, axis=1), gather_plane(piece)


def solution(mesh):
    placed = (P("col", None, "row"), P(), P(), P(), P("col", None))
    return jax.shard_map(
        on_device,
        mesh=mesh,
        in_specs=placed,
        out_specs=(P("col", None, "row"), P()),
        check_vma=False,
    )
```

profile of v0, /device:TPU:0, one launch (start us, length us, event | category | flops | bytes accessed | tf_op | source)
XLA Modules:
  0.0 260.4 jit_solution(8130734036293072597)
XLA Ops:
  0.6 2.5 fusion.1
  3.1 20.6 %all_to_all.35.refs_2_ = f32[4,128,256]{2,1,0:T(8,128)S(1)} all-to-all(f32[4,128,256]{2,1,0:T(8,128)S(1)} %get-tuple-element.53), channel_id=1, replica_groups=mesh['row'=4,'col'=8] {'row'}, dimensions={0} | all-to-all | bytes 1048576 | tf_op jit(solution)/shard_map/all_to_all | solution.py:203
  23.7 16.5 %all_to_all.36.refs_3_ = f32[4,128,256]{2,1,0:T(8,128)S(1)} all-to-all(f32[4,128,256]{2,1,0:T(8,128)S(1)} %get-tuple-element.50), channel_id=1, replica_groups=mesh['row'=4,'col'=8] {'row'}, dimensions={0} | all-to-all | bytes 1048576 | tf_op jit(solution)/shard_map/all_to_all | solution.py:203
  40.2 16.6 %all_to_all.37.refs_1_ = f32[4,128,256]{2,1,0:T(8,128)S(1)} all-to-all(f32[4,128,256]{2,1,0:T(8,128)S(1)} %get-tuple-element.51), channel_id=1, replica_groups=mesh['row'=4,'col'=8] {'row'}, dimensions={0} | all-to-all | bytes 1048576 | tf_op jit(solution)/shard_map/all_to_all | solution.py:203
  56.8 3.5 %all-to-all-start = ((f32[4,128,256]{2,1,0:T(8,128)}), f32[4,128,256]{2,1,0:T(8,128)S(1)}, u32[]{:S(2)}, u32[]{:S(2)}) async-start(f32[4,128,256]{2,1,0:T(8,128)} %get-tuple-element.52), calls=%async_computation | async-start | bytes 1048576 | tf_op jit(solution)/shard_map/all_to_all | solution.py:203
  60.3 3.5 %collective-permute-start.2 = (f32[4,128,256]{2,1,0:T(8,128)S(1)}, f32[4,128,256]{2,1,0:T(8,128)S(1)}, u32[]{:S(2)}, u32[]{:S(2)}) collective-permute-start(f32[4,128,256]{2,1,0:T(8,128)S(1)} %all_to_all.35.refs_2_), channel_id=1, source_target_pairs={{0,4},{1,5},{2,6},{3,7},{8,12},{9,13},{10,14},{11,15},{16,20},{17,... | collective-permute-start | bytes 1572872 | tf_op jit(solution)/shard_map/ppermute | solution.py:257
  63.7 2.1 collective-permute-start.3
  65.8 2.2 collective-permute-start.1
  68.1 5.7 %all-to-all-done.refs_0_ = f32[4,128,256]{2,1,0:T(8,128)S(1)} async-done(((f32[4,128,256]{2,1,0:T(8,128)}), f32[4,128,256]{2,1,0:T(8,128)S(1)}, u32[]{:S(2)}, u32[]{:S(2)}) %all-to-all-start) | async-done | bytes 524320 | tf_op jit(solution)/shard_map/all_to_all | solution.py:203
  73.8 4.2 %collective-permute-start = (f32[4,128,256]{2,1,0:T(8,128)S(1)}, f32[4,128,256]{2,1,0:T(8,128)}, u32[]{:S(2)}, u32[]{:S(2)}) collective-permute-start(f32[4,128,256]{2,1,0:T(8,128)S(1)} %all-to-all-done.refs_0_), channel_id=1, source_target_pairs={{0,4},{1,5},{2,6},{3,7},{8,12},{9,13},{10,14},{11,15},{16,20},{17,... | collective-permute-start | bytes 1572872 | tf_op jit(solution)/shard_map/ppermute | solution.py:257
  78.1 9.2 %collective-permute-done.3 = f32[4,128,256]{2,1,0:T(8,128)} collective-permute-done((f32[4,128,256]{2,1,0:T(8,128)S(1)}, f32[4,128,256]{2,1,0:T(8,128)}, u32[]{:S(2)}, u32[]{:S(2)}) %collective-permute-start.3) | collective-permute-done | bytes 524320 | tf_op jit(solution)/shard_map/ppermute | solution.py:257
  87.5 11.1 %collective-permute-done.1 = f32[4,128,256]{2,1,0:T(8,128)} collective-permute-done((f32[4,128,256]{2,1,0:T(8,128)S(1)}, f32[4,128,256]{2,1,0:T(8,128)}, u32[]{:S(2)}, u32[]{:S(2)}) %collective-permute-start.1) | collective-permute-done | bytes 524320 | tf_op jit(solution)/shard_map/ppermute | solution.py:257
  98.5 0.9 broadcast_select_fusion.2.refs_5_
  99.4 0.1 copy.9
  99.6 1.5 collective-permute-start.10
  101.1 6.2 %collective-permute-done = f32[4,128,256]{2,1,0:T(8,128)} collective-permute-done((f32[4,128,256]{2,1,0:T(8,128)S(1)}, f32[4,128,256]{2,1,0:T(8,128)}, u32[]{:S(2)}, u32[]{:S(2)}) %collective-permute-start) | collective-permute-done | bytes 524320 | tf_op jit(solution)/shard_map/ppermute | solution.py:257
  107.3 1.5 collective-permute-start.11
  108.8 0.9 broadcast_select_fusion.3.refs_4_
  109.7 0.5 collective-permute-start.9
  110.2 1.6 collective-permute-start.8
  111.8 0.6 gather_fusion
  112.5 0.1 slice.27.masks
  112.7 0.6 fusion.2
  115.9 1.4 compare_reduce_fusion.1
  118.4 0.1 copy.10.vir_col
  118.6 0.8 broadcast_in_dim.17
  119.4 1.6 slice.33.masks
  124.9 0.2 collective-permute-start.14
  125.1 0.6 collective-permute-done.11.refs_3_
  125.7 11.2 %collective-permute-done.9.refs_1_ = f32[4,128,256]{2,1,0:T(8,128)} collective-permute-done((f32[4,128,256]{2,1,0:T(8,128)}, f32[4,128,256]{2,1,0:T(8,128)}, u32[]{:S(2)}, u32[]{:S(2)}) %collective-permute-start.9) | collective-permute-done | bytes 524320 | tf_op jit(solution)/shard_map/ppermute | solution.py:199
  136.9 10.8 %collective-permute-done.8.refs_0_ = f32[4,128,256]{2,1,0:T(8,128)} collective-permute-done((f32[4,128,256]{2,1,0:T(8,128)}, f32[4,128,256]{2,1,0:T(8,128)}, u32[]{:S(2)}, u32[]{:S(2)}) %collective-permute-start.8) | collective-permute-done | bytes 524320 | tf_op jit(solution)/shard_map/ppermute | solution.py:199
  147.8 11.5 %early.1 = (bf16[512,1024]{1,0:T(8,128)(2,1)}, bf16[512,1024]{1,0:T(8,128)(2,1)}, f32[4,512,256]{2,1,0:T(8,128)}, f32[512,512]{1,0:T(8,128)}) custom-call(f32[4]{0:T(128)S(1)} %pad_maximum_fusion.1.scalars, f32[512,1]{1,0:T(8,128)S(1)} %copy.10.vir_col, f32[1,512]{1,0:T(1,128)S(1)} %bitcast.18, f32[3,8,1024]{2,1,0:T(8,128)S(1)} %slice.27.masks, ...), custom_call_target="tpu_custom_call" | custom-call | flops 8053063680 | bytes 11636752 | tf_op jit(solution)/shard_map/early/pallas_call | solution.py:22
  159.4 0.7 copy-done.10
  160.1 0.2 copy-done.11
  160.3 0.2 copy-done.12
  160.5 0.2 copy-done.13
  160.7 7.5 %late.1 = (bf16[512,1024]{1,0:T(8,128)(2,1)}, bf16[512,1024]{1,0:T(8,128)(2,1)}, bf16[512,512]{1,0:T(8,128)(2,1)S(1)}, bf16[512,512]{1,0:T(8,128)(2,1)S(1)}, bf1...) custom-call(f32[4]{0:T(128)S(1)} %pad_maximum_fusion.2.scalars, ...), custom_call_target="tpu_custom_call" | custom-call | flops 3221225472 | bytes 14749712 | tf_op jit(solution)/shard_map/late/pallas_call | solution.py:22
  168.2 3.4 %density.1 = f32[512,512]{1,0:T(8,128)S(1)} custom-call(f32[512,512]{1,0:T(8,128)} %get-tuple-element.35.before, bf16[512,512]{1,0:T(8,128)(2,1)S(1)} %get-tuple-element.36.refs_0_, bf16[512,512]{1,0:T(8,128)(2,1)S(1)} %get-tuple-element.37.refs_1_, bf16[512,512]{1,0:T(8,128)(2,1)S(1)} %get-tuple-element.29.refs_2_, ...), custom_call_target="tpu_custom_call" | custom-call | flops 1610612736 | bytes 6291456 | tf_op jit(solution)/shard_map/density/pallas_call | solution.py:22
  171.6 0.8 constant_dynamic-slice_fusion.2
  172.4 0.5 collective-permute-start.16
  172.9 5.0 %response.2 = f32[4,256,256]{2,1,0:T(8,128)} custom-call(f32[4,512,256]{2,1,0:T(8,128)} %get-tuple-element.24.before, bf16[512,1024]{1,0:T(8,128)(2,1)S(1)} %copy-done, bf16[512,1024]{1,0:T(8,128)(2,1)S(1)} %copy-done.2, bf16[512,512]{1,0:T(8,128)(2,1)S(1)} %get-tuple-element.29.refs_2_, bf16[512,512]{1,0:T(8,128)(2,1)S(1)} %get-tuple-element.30.refs_3_, ...), custom_call_target="tpu_custom_call" | custom-call | flops 1610612736 | bytes 9437184 | tf_op jit(solution)/shard_map/response/pallas_call | solution.py:22
  177.9 5.0 %all-to-all-start.4 = ((f32[4,256,256]{2,1,0:T(8,128)}), f32[4,256,256]{2,1,0:T(8,128)}, u32[]{:S(2)}, u32[]{:S(2)}) async-start(f32[4,256,256]{2,1,0:T(8,128)} %response.2), calls=%async_computation.4 | async-start | bytes 2097152 | tf_op jit(solution)/shard_map/all_to_all | solution.py:203
  182.9 1.1 dynamic-slice_add_fusion
  184.0 0.8 copy-done.7
  184.8 1.6 collective-permute-start.17
  186.4 6.6 %collective-permute-done.17 = f32[128,512]{1,0:T(8,128)} collective-permute-done((f32[128,512]{1,0:T(8,128)S(1)}, f32[128,512]{1,0:T(8,128)}, u32[]{:S(2)}, u32[]{:S(2)}) %collective-permute-start.17) | collective-permute-done | bytes 262176 | tf_op jit(solution)/shard_map/ppermute | solution.py:199
  193.0 1.1 dynamic-slice_add_fusion.1
  194.0 3.7 %collective-permute-start.18 = (f32[64,512]{1,0:T(8,128)S(1)}, f32[64,512]{1,0:T(8,128)S(1)}, u32[]{:S(2)}, u32[]{:S(2)}) collective-permute-start(f32[64,512]{1,0:T(8,128)S(1)} %constant_dynamic-slice_fusion), channel_id=1, source_target_pairs={{0,4},{1,5},{2,6},{3,7},{4,0},{5,1},{6,2},{7,3},{8,12},{9,13},{10,... | collective-permute-start | bytes 393224 | tf_op jit(solution)/shard_map/ppermute | solution.py:199
  197.7 1.2 copy-done.3
  199.0 4.8 %response.3 = (f32[4,128,256]{2,1,0:T(8,128)S(1)}, f32[4,128,256]{2,1,0:T(8,128)}) custom-call(f32[4,512,256]{2,1,0:T(8,128)} %get-tuple-element.24.before, bf16[512,1024]{1,0:T(8,128)(2,1)S(1)} %copy-done.1, bf16[512,1024]{1,0:T(8,128)(2,1)S(1)} %copy-done.3, bf16[512,512]{1,0:T(8,128)(2,1)S(1)} %get-tuple-element.29.refs_2_, ...), custom_call_target="tpu_custom_call" | custom-call | flops 1610612736 | bytes 9437184 | tf_op jit(solution)/shard_map/response/pallas_call | solution.py:22
  203.7 0.8 copy-done.4
  204.6 4.4 %all-to-all-done.4 = f32[4,256,256]{2,1,0:T(8,128)} async-done(((f32[4,256,256]{2,1,0:T(8,128)}), f32[4,256,256]{2,1,0:T(8,128)}, u32[]{:S(2)}, u32[]{:S(2)}) %all-to-all-start.4) | async-done | bytes 1048608 | tf_op jit(solution)/shard_map/all_to_all | solution.py:203
  208.9 3.5 %all-to-all-start.5 = ((f32[4,128,256]{2,1,0:T(8,128)}), f32[4,128,256]{2,1,0:T(8,128)S(1)}, u32[]{:S(2)}, u32[]{:S(2)}) async-start(f32[4,128,256]{2,1,0:T(8,128)} %copy-done.4), calls=%async_computation.5 | async-start | bytes 1048576 | tf_op jit(solution)/shard_map/all_to_all | solution.py:203
  212.4 2.0 collective-permute-start.19
  214.4 2.4 collective-permute-start.20
  216.9 8.1 %collective-permute-done.19 = f32[64,512]{1,0:T(8,128)S(1)} collective-permute-done((f32[64,512]{1,0:T(8,128)S(1)}, f32[64,512]{1,0:T(8,128)S(1)}, u32[]{:S(2)}, u32[]{:S(2)}) %collective-permute-start.19) | collective-permute-done | bytes 131104 | tf_op jit(solution)/shard_map/ppermute | solution.py:199
  225.0 10.9 %collective-permute-done.20 = f32[64,512]{1,0:T(8,128)S(1)} collective-permute-done((f32[64,512]{1,0:T(8,128)S(1)}, f32[64,512]{1,0:T(8,128)S(1)}, u32[]{:S(2)}, u32[]{:S(2)}) %collective-permute-start.20) | collective-permute-done | bytes 131104 | tf_op jit(solution)/shard_map/ppermute | solution.py:199
  235.9 3.7 %collective-permute-start.22 = (f32[64,512]{1,0:T(8,128)S(1)}, f32[64,512]{1,0:T(8,128)S(1)}, u32[]{:S(2)}, u32[]{:S(2)}) collective-permute-start(f32[64,512]{1,0:T(8,128)S(1)} %add_add_fusion), channel_id=1, source_target_pairs={{0,4},{1,5},{2,6},{3,7},{4,0},{5,1},{6,2},{7,3},{8,12},{9,13},{10,... | collective-permute-start | bytes 393224 | tf_op jit(solution)/shard_map/ppermute | solution.py:199
  239.6 3.6 %all-to-all-start.6 = ((f32[4,128,256]{2,1,0:T(8,128)}), f32[4,128,256]{2,1,0:T(8,128)S(1)}, u32[]{:S(2)}, u32[]{:S(2)}) async-start(f32[4,128,256]{2,1,0:T(8,128)} %get-tuple-element.44), calls=%async_computation.6 | async-start | bytes 1048576 | tf_op jit(solution)/shard_map/all_to_all | solution.py:203
  243.2 1.6 collective-permute-start.23
  244.8 5.2 %collective-permute-done.23 = f32[128,512]{1,0:T(8,128)S(1)} collective-permute-done((f32[128,512]{1,0:T(8,128)S(1)}, f32[128,512]{1,0:T(8,128)S(1)}, u32[]{:S(2)}, u32[]{:S(2)}) %collective-permute-start.23) | collective-permute-done | bytes 262176 | tf_op jit(solution)/shard_map/ppermute | solution.py:199
  250.1 6.5 %all-to-all-done.6 = f32[4,128,256]{2,1,0:T(8,128)S(1)} async-done(((f32[4,128,256]{2,1,0:T(8,128)}), f32[4,128,256]{2,1,0:T(8,128)S(1)}, u32[]{:S(2)}, u32[]{:S(2)}) %all-to-all-start.6) | async-done | bytes 524320 | tf_op jit(solution)/shard_map/all_to_all | solution.py:203
  256.6 2.7 %pad_maximum_fusion = f32[4,512,256]{2,1,0:T(8,128)} fusion(f32[4,128,256]{2,1,0:T(8,128)S(1)} %all-to-all-done.6, f32[4,128,256]{2,1,0:T(8,128)S(1)} %all-to-all-done.5, f32[4,256,256]{2,1,0:T(8,128)} %all-to-all-done.4), kind=kLoop, calls=%fused_computation.1 | loop fusion | flops 1048576 | bytes 4194304 | tf_op jit(solution)/shard_map/concatenate | solution.py:292
  259.3 1.1 maximum_select_fusion
  (63 shorter events, 1.1 us)
Async XLA Ops:
  56.8 17.0 %all-to-all-start = ((f32[4,128,256]{2,1,0:T(8,128)}), f32[4,128,256]{2,1,0:T(8,128)S(1)}, u32[]{:S(2)}, u32[]{:S(2)}) async-start(f32[4,128,256]{2,1,0:T(8,128)} %get-tuple-element.52), calls=%async_computation | async-start | bytes 1048576 | tf_op jit(solution)/shard_map/all_to_all | solution.py:203
  60.3 17.7 %collective-permute-start.2 = (f32[4,128,256]{2,1,0:T(8,128)S(1)}, f32[4,128,256]{2,1,0:T(8,128)S(1)}, u32[]{:S(2)}, u32[]{:S(2)}) collective-permute-start(f32[4,128,256]{2,1,0:T(8,128)S(1)} %all_to_all.35.refs_2_), channel_id=1, source_target_pairs={{0,4},{1,5},{2,6},{3,7},{8,12},{9,13},{10,14},{11,15},{16,20},{17,... | collective-permute-start | bytes 1572872 | tf_op jit(solution)/shard_map/ppermute | solution.py:257
  63.7 23.6 %collective-permute-start.3 = (f32[4,128,256]{2,1,0:T(8,128)S(1)}, f32[4,128,256]{2,1,0:T(8,128)}, u32[]{:S(2)}, u32[]{:S(2)}) collective-permute-start(f32[4,128,256]{2,1,0:T(8,128)S(1)} %all_to_all.36.refs_3_), channel_id=1, source_target_pairs={{0,4},{1,5},{2,6},{3,7},{8,12},{9,13},{10,14},{11,15},{16,20},{17,... | collective-permute-start | bytes 1572872 | tf_op jit(solution)/shard_map/ppermute | solution.py:257
  65.8 33.6 %copy-start.8 = (s32[32,8,16]{0,2,1:T(8,128)S(1)}, s32[32,8,16]{0,2,1:T(8,128)}, u32[]{:S(2)}) copy-start(s32[32,8,16]{0,2,1:T(8,128)} %param.8) | copy-start | bytes 49156
  65.8 32.7 %collective-permute-start.1 = (f32[4,128,256]{2,1,0:T(8,128)S(1)}, f32[4,128,256]{2,1,0:T(8,128)}, u32[]{:S(2)}, u32[]{:S(2)}) collective-permute-start(f32[4,128,256]{2,1,0:T(8,128)S(1)} %all_to_all.37.refs_1_), channel_id=1, source_target_pairs={{0,4},{1,5},{2,6},{3,7},{8,12},{9,13},{10,14},{11,15},{16,20},{17,... | collective-permute-start | bytes 1572872 | tf_op jit(solution)/shard_map/ppermute | solution.py:257
  73.8 33.6 %collective-permute-start = (f32[4,128,256]{2,1,0:T(8,128)S(1)}, f32[4,128,256]{2,1,0:T(8,128)}, u32[]{:S(2)}, u32[]{:S(2)}) collective-permute-start(f32[4,128,256]{2,1,0:T(8,128)S(1)} %all-to-all-done.refs_0_), channel_id=1, source_target_pairs={{0,4},{1,5},{2,6},{3,7},{8,12},{9,13},{10,14},{11,15},{16,20},{17,... | collective-permute-start | bytes 1572872 | tf_op jit(solution)/shard_map/ppermute | solution.py:257
  78.1 31.6 %collective-permute-start.6 = (f32[4,128,256]{2,1,0:T(8,128)S(1)}, f32[4,128,256]{2,1,0:T(8,128)}, u32[]{:S(2)}, u32[]{:S(2)}) collective-permute-start(f32[4,128,256]{2,1,0:T(8,128)S(1)} %broadcast_select_fusion.1.refs_6_), channel_id=1, source_target_pairs={{0,1},{1,0},{2,3},{3,2},{4,5},{5,4},{6,7},{7,6},{8,9},{9,8},{10,11... | collective-permute-start | bytes 1572872 | tf_op jit(solution)/shard_map/ppermute | solution.py:199
  87.4 25.3 %copy-start.9 = (f32[32]{0:T(128)S(1)}, f32[32]{0:T(128)}, u32[]{:S(2)}) copy-start(f32[32]{0:T(128)} %param.6) | copy-start | bytes 388
  87.4 31.1 %copy-start.6 = (f32[512]{0:T(512)S(1)}, f32[512]{0:T(512)}, u32[]{:S(2)}) copy-start(f32[512]{0:T(512)} %param.7) | copy-start | bytes 6148
  87.4 22.9 %collective-permute-start.7 = (f32[4,128,256]{2,1,0:T(8,128)S(1)}, f32[4,128,256]{2,1,0:T(8,128)}, u32[]{:S(2)}, u32[]{:S(2)}) collective-permute-start(f32[4,128,256]{2,1,0:T(8,128)S(1)} %broadcast_select_fusion.refs_7_), channel_id=1, source_target_pairs={{0,1},{1,0},{2,3},{3,2},{4,5},{5,4},{6,7},{7,6},{8,9},{9,8},{10,11... | collective-permute-start | bytes 1572872 | tf_op jit(solution)/shard_map/ppermute | solution.py:199
  99.4 10.8 %collective-permute-start.5 = (f32[4,128,256]{2,1,0:T(8,128)}, f32[4,128,256]{2,1,0:T(8,128)}, u32[]{:S(2)}, u32[]{:S(2)}) collective-permute-start(f32[4,128,256]{2,1,0:T(8,128)} %broadcast_select_fusion.2.refs_5_), channel_id=1, source_target_pairs={{0,1},{1,0},{2,3},{3,2},{4,5},{5,4},{6,7},{7,6},{8,9},{9,8},{10,11... | collective-permute-start | bytes 1572872 | tf_op jit(solution)/shard_map/ppermute | solution.py:199
  99.6 25.3 %collective-permute-start.10 = (f32[4,128,256]{2,1,0:T(8,128)S(1)}, f32[4,128,256]{2,1,0:T(8,128)}, u32[]{:S(2)}, u32[]{:S(2)}) collective-permute-start(f32[4,128,256]{2,1,0:T(8,128)S(1)} %broadcast_select_fusion.1.refs_6_), channel_id=1, source_target_pairs={{0,2},{1,3},{2,0},{3,1},{4,6},{5,7},{6,4},{7,5},{8,10},{9,11},{10,... | collective-permute-start | bytes 1572872 | tf_op jit(solution)/shard_map/ppermute | solution.py:199
  107.3 18.3 %collective-permute-start.11 = (f32[4,128,256]{2,1,0:T(8,128)S(1)}, f32[4,128,256]{2,1,0:T(8,128)}, u32[]{:S(2)}, u32[]{:S(2)}) collective-permute-start(f32[4,128,256]{2,1,0:T(8,128)S(1)} %broadcast_select_fusion.refs_7_), channel_id=1, source_target_pairs={{0,2},{1,3},{2,0},{3,1},{4,6},{5,7},{6,4},{7,5},{8,10},{9,11},{10,... | collective-permute-start | bytes 1572872 | tf_op jit(solution)/shard_map/ppermute | solution.py:199
  109.7 27.2 %collective-permute-start.9 = (f32[4,128,256]{2,1,0:T(8,128)}, f32[4,128,256]{2,1,0:T(8,128)}, u32[]{:S(2)}, u32[]{:S(2)}) collective-permute-start(f32[4,128,256]{2,1,0:T(8,128)} %broadcast_select_fusion.2.refs_5_), channel_id=1, source_target_pairs={{0,2},{1,3},{2,0},{3,1},{4,6},{5,7},{6,4},{7,5},{8,10},{9,11},{10,... | collective-permute-start | bytes 1572872 | tf_op jit(solution)/shard_map/ppermute | solution.py:199
  110.2 37.5 %collective-permute-start.4 = (f32[4,128,256]{2,1,0:T(8,128)}, f32[4,128,256]{2,1,0:T(8,128)}, u32[]{:S(2)}, u32[]{:S(2)}) collective-permute-start(f32[4,128,256]{2,1,0:T(8,128)} %broadcast_select_fusion.3.refs_4_), channel_id=1, source_target_pairs={{0,1},{1,0},{2,3},{3,2},{4,5},{5,4},{6,7},{7,6},{8,9},{9,8},{10,11... | collective-permute-start | bytes 1572872 | tf_op jit(solution)/shard_map/ppermute | solution.py:199
  110.2 37.5 %collective-permute-start.8 = (f32[4,128,256]{2,1,0:T(8,128)}, f32[4,128,256]{2,1,0:T(8,128)}, u32[]{:S(2)}, u32[]{:S(2)}) collective-permute-start(f32[4,128,256]{2,1,0:T(8,128)} %broadcast_select_fusion.3.refs_4_), channel_id=1, source_target_pairs={{0,2},{1,3},{2,0},{3,1},{4,6},{5,7},{6,4},{7,5},{8,10},{9,11},{10,... | collective-permute-start | bytes 1572872 | tf_op jit(solution)/shard_map/ppermute | solution.py:199
  124.9 34.4 %collective-permute-start.14 = (f32[4,128,256]{2,1,0:T(8,128)}, f32[4,128,256]{2,1,0:T(8,128)S(1)}, u32[]{:S(2)}, u32[]{:S(2)}) collective-permute-start(f32[4,128,256]{2,1,0:T(8,128)} %collective-permute-done.10.refs_2_), channel_id=1, source_target_pairs={{0,1},{1,0},{2,3},{3,2},{4,5},{5,4},{6,7},{7,6},{8,9},{9,8},{10,11... | collective-permute-start | bytes 1572872 | tf_op jit(solution)/shard_map/ppermute | solution.py:199
  125.7 33.7 %collective-permute-start.15 = (f32[4,128,256]{2,1,0:T(8,128)}, f32[4,128,256]{2,1,0:T(8,128)S(1)}, u32[]{:S(2)}, u32[]{:S(2)}) collective-permute-start(f32[4,128,256]{2,1,0:T(8,128)} %collective-permute-done.11.refs_3_), channel_id=1, source_target_pairs={{0,1},{1,0},{2,3},{3,2},{4,5},{5,4},{6,7},{7,6},{8,9},{9,8},{10,11... | collective-permute-start | bytes 1572872 | tf_op jit(solution)/shard_map/ppermute | solution.py:199
  136.9 22.4 %collective-permute-start.13 = (f32[4,128,256]{2,1,0:T(8,128)}, f32[4,128,256]{2,1,0:T(8,128)S(1)}, u32[]{:S(2)}, u32[]{:S(2)}) collective-permute-start(f32[4,128,256]{2,1,0:T(8,128)} %collective-permute-done.9.refs_1_), channel_id=1, source_target_pairs={{0,1},{1,0},{2,3},{3,2},{4,5},{5,4},{6,7},{7,6},{8,9},{9,8},{10,11... | collective-permute-start | bytes 1572872 | tf_op jit(solution)/shard_map/ppermute | solution.py:199
  147.8 11.6 %collective-permute-start.12 = (f32[4,128,256]{2,1,0:T(8,128)}, f32[4,128,256]{2,1,0:T(8,128)S(1)}, u32[]{:S(2)}, u32[]{:S(2)}) collective-permute-start(f32[4,128,256]{2,1,0:T(8,128)} %collective-permute-done.8.refs_0_), channel_id=1, source_target_pairs={{0,1},{1,0},{2,3},{3,2},{4,5},{5,4},{6,7},{7,6},{8,9},{9,8},{10,11... | collective-permute-start | bytes 1572872 | tf_op jit(solution)/shard_map/ppermute | solution.py:199
  147.8 12.9 %copy-start.5 = (f32[2,8,1024]{2,1,0:T(8,128)S(1)}, f32[2,8,1024]{2,1,0:T(8,128)}, u32[]{:S(2)}) copy-start(f32[2,8,1024]{2,1,0:T(8,128)} %slice.33.masks) | copy-start | bytes 196612
  159.3 0.8 copy-start.10
  159.3 1.0 copy-start.11
  159.4 1.1 copy-start.12
  159.4 1.3 copy-start.13
  168.2 4.7 %copy-start = (bf16[512,1024]{1,0:T(8,128)(2,1)S(1)}, bf16[512,1024]{1,0:T(8,128)(2,1)}, u32[]{:S(2)}) copy-start(bf16[512,1024]{1,0:T(8,128)(2,1)} %get-tuple-element.27.refs_0_) | copy-start | bytes 3145732
  168.2 4.7 %copy-start.2 = (bf16[512,1024]{1,0:T(8,128)(2,1)S(1)}, bf16[512,1024]{1,0:T(8,128)(2,1)}, u32[]{:S(2)}) copy-start(bf16[512,1024]{1,0:T(8,128)(2,1)} %get-tuple-element.28.refs_1_) | copy-start | bytes 3145732
  172.4 10.5 %collective-permute-start.16 = (f32[256,512]{1,0:T(8,128)}, f32[256,512]{1,0:T(8,128)}, u32[]{:S(2)}, u32[]{:S(2)}) collective-permute-start(f32[256,512]{1,0:T(8,128)} %constant_dynamic-slice_fusion.2), channel_id=1, source_target_pairs={{0,1},{1,0},{2,3},{3,2},{4,5},{5,4},{6,7},{7,6},{8,9},{9,8},{10,11... | collective-permute-start | bytes 1572872 | tf_op jit(solution)/shard_map/ppermute | solution.py:199
  177.9 31.1 %all-to-all-start.4 = ((f32[4,256,256]{2,1,0:T(8,128)}), f32[4,256,256]{2,1,0:T(8,128)}, u32[]{:S(2)}, u32[]{:S(2)}) async-start(f32[4,256,256]{2,1,0:T(8,128)} %response.2), calls=%async_computation.4 | async-start | bytes 2097152 | tf_op jit(solution)/shard_map/all_to_all | solution.py:203
  184.0 0.8 copy-start.7
  184.8 12.9 %copy-start.1 = (bf16[512,1024]{1,0:T(8,128)(2,1)S(1)}, bf16[512,1024]{1,0:T(8,128)(2,1)}, u32[]{:S(2)}) copy-start(bf16[512,1024]{1,0:T(8,128)(2,1)} %get-tuple-element.27.refs_0_) | copy-start | bytes 3145732
  184.8 8.1 %collective-permute-start.17 = (f32[128,512]{1,0:T(8,128)S(1)}, f32[128,512]{1,0:T(8,128)}, u32[]{:S(2)}, u32[]{:S(2)}) collective-permute-start(f32[128,512]{1,0:T(8,128)S(1)} %constant_dynamic-slice_fusion.1), channel_id=1, source_target_pairs={{0,2},{1,3},{2,0},{3,1},{4,6},{5,7},{6,4},{7,5},{8,10},{9,11},{10,... | collective-permute-start | bytes 786440 | tf_op jit(solution)/shard_map/ppermute | solution.py:199
  194.0 10.5 %collective-permute-start.18 = (f32[64,512]{1,0:T(8,128)S(1)}, f32[64,512]{1,0:T(8,128)S(1)}, u32[]{:S(2)}, u32[]{:S(2)}) collective-permute-start(f32[64,512]{1,0:T(8,128)S(1)} %constant_dynamic-slice_fusion), channel_id=1, source_target_pairs={{0,4},{1,5},{2,6},{3,7},{4,0},{5,1},{6,2},{7,3},{8,12},{9,13},{10,... | collective-permute-start | bytes 393224 | tf_op jit(solution)/shard_map/ppermute | solution.py:199
  197.7 1.2 copy-start.3
  203.7 0.8 copy-start.4
  208.9 30.7 %all-to-all-start.5 = ((f32[4,128,256]{2,1,0:T(8,128)}), f32[4,128,256]{2,1,0:T(8,128)S(1)}, u32[]{:S(2)}, u32[]{:S(2)}) async-start(f32[4,128,256]{2,1,0:T(8,128)} %copy-done.4), calls=%async_computation.5 | async-start | bytes 1048576 | tf_op jit(solution)/shard_map/all_to_all | solution.py:203
  212.4 12.6 %collective-permute-start.19 = (f32[64,512]{1,0:T(8,128)S(1)}, f32[64,512]{1,0:T(8,128)S(1)}, u32[]{:S(2)}, u32[]{:S(2)}) collective-permute-start(f32[64,512]{1,0:T(8,128)S(1)} %dynamic-slice_add_fusion.2), channel_id=1, source_target_pairs={{0,8},{8,0},{16,24},{24,16},{1,9},{9,1},{17,25},{25,17},{2,10},{10... | collective-permute-start | bytes 393224 | tf_op jit(solution)/shard_map/ppermute | solution.py:199
  214.4 21.5 %collective-permute-start.20 = (f32[64,512]{1,0:T(8,128)S(1)}, f32[64,512]{1,0:T(8,128)S(1)}, u32[]{:S(2)}, u32[]{:S(2)}) collective-permute-start(f32[64,512]{1,0:T(8,128)S(1)} %dynamic-slice_add_fusion.2), channel_id=1, source_target_pairs={{0,16},{8,24},{16,0},{24,8},{1,17},{9,25},{17,1},{25,9},{2,18},{10... | collective-permute-start | bytes 393224 | tf_op jit(solution)/shard_map/ppermute | solution.py:199
  216.8 19.1 %collective-permute-start.21 = (f32[64,512]{1,0:T(8,128)S(1)}, f32[64,512]{1,0:T(8,128)S(1)}, u32[]{:S(2)}, u32[]{:S(2)}) collective-permute-start(f32[64,512]{1,0:T(8,128)S(1)} %dynamic-slice_add_fusion.2), channel_id=1, source_target_pairs={{0,24},{8,16},{16,8},{24,0},{1,25},{9,17},{17,9},{25,1},{2,26},{10... | collective-permute-start | bytes 393224 | tf_op jit(solution)/shard_map/ppermute | solution.py:199
  235.9 7.3 %collective-permute-start.22 = (f32[64,512]{1,0:T(8,128)S(1)}, f32[64,512]{1,0:T(8,128)S(1)}, u32[]{:S(2)}, u32[]{:S(2)}) collective-permute-start(f32[64,512]{1,0:T(8,128)S(1)} %add_add_fusion), channel_id=1, source_target_pairs={{0,4},{1,5},{2,6},{3,7},{4,0},{5,1},{6,2},{7,3},{8,12},{9,13},{10,... | collective-permute-start | bytes 393224 | tf_op jit(solution)/shard_map/ppermute | solution.py:199
  239.6 17.0 %all-to-all-start.6 = ((f32[4,128,256]{2,1,0:T(8,128)}), f32[4,128,256]{2,1,0:T(8,128)S(1)}, u32[]{:S(2)}, u32[]{:S(2)}) async-start(f32[4,128,256]{2,1,0:T(8,128)} %get-tuple-element.44), calls=%async_computation.6 | async-start | bytes 1048576 | tf_op jit(solution)/shard_map/all_to_all | solution.py:203
  243.2 6.8 %collective-permute-start.23 = (f32[128,512]{1,0:T(8,128)S(1)}, f32[128,512]{1,0:T(8,128)S(1)}, u32[]{:S(2)}, u32[]{:S(2)}) collective-permute-start(f32[128,512]{1,0:T(8,128)S(1)} %maximum_select_fusion.2), channel_id=1, source_target_pairs={{0,2},{1,3},{2,0},{3,1},{4,6},{5,7},{6,4},{7,5},{8,10},{9,11},{10,... | collective-permute-start | bytes 786440 | tf_op jit(solution)/shard_map/ppermute | solution.py:199
  250.0 9.3 %collective-permute-start.24 = (f32[256,512]{1,0:T(8,128)S(1)}, f32[256,512]{1,0:T(8,128)S(1)}, u32[]{:S(2)}, u32[]{:S(2)}) collective-permute-start(f32[256,512]{1,0:T(8,128)S(1)} %maximum_select_fusion.1), channel_id=1, source_target_pairs={{0,1},{1,0},{2,3},{3,2},{4,5},{5,4},{6,7},{7,6},{8,9},{9,8},{10,11... | collective-permute-start | bytes 1572872 | tf_op jit(solution)/shard_map/ppermute | solution.py:199
where the time goes:
time: 261 us; the launch traced here: 260 us
  waiting for transfers between devices  96.5 us (37%)
  blocking collectives  53.7 us (21%)
  starting transfers between devices  48.5 us (19%)
  Pallas kernels  32.1 us (12%)
  local copies, waits for them, and re-layouts  11.6 us (4%)
  other arithmetic  9.5 us (4%)
  between operations  8.48 us (3%)
    all_to_all x3, blocking collectives, swap_parts(): return lax.all_to_all(value, 'row', split_axis=0, concat_axis=0, tiled=True)  53.7 us
    ppermute x21, waiting for transfers between devices, exchange(): return lax.ppermute(value, axis, [(at, at ^ bit) for at in range(size)])  53.5 us
    pallas_call x5, Pallas kernels, call(): pl.pallas_call(kernel, out_shape=outs, in_specs=[SMEM] * scalars + [VMEM]...  32.1 us
    ppermute x4, waiting for transfers between devices, on_device(): got = lax.ppermute(rows, 'col', links)  26.4 us
    ppermute x21, starting transfers between devices, exchange(): return lax.ppermute(value, axis, [(at, at ^ bit) for at in range(size)])  20.9 us
    all_to_all x4, waiting for transfers between devices, swap_parts(): return lax.all_to_all(value, 'row', split_axis=0, concat_axis=0, tiled=True)  16.6 us
    all_to_all x4, starting transfers between devices, swap_parts(): return lax.all_to_all(value, 'row', split_axis=0, concat_axis=0, tiled=True)  15.6 us
    ppermute x4, starting transfers between devices, on_device(): got = lax.ppermute(rows, 'col', links)  12 us
  transfers between devices with their start and end apart: 29, of which 13 were waited for; matrix products, arithmetic and copies ran while one was open for 5% of the time, Pallas kernels for 8%

commit v1 on v0

--- a/solution.py
+++ b/solution.py
@@ -9,7 +9,6 @@
 
 BLOCK = 64
 NPANEL = 4
-CHUNKS = 4
 TILE = 256
 VMEM_LIMIT = 48 * 1024 * 1024
 SMEM = pl.BlockSpec(memory_space=pltpu.SMEM)
@@ -48,16 +47,15 @@
     return lax.dot_general(left, right, NT, preferred_element_type=jnp.float32)
 
 
-def split_rows(chunks, mask, high, low):
-    for chunk, rows in enumerate(chunks):
-        parts, count, width = rows.shape
+def split_rows(cuts, pieces, mask, high, low):
+    for (part, first, count), piece in zip(cuts, pieces):
+        width = piece.shape[1]
+        cols = slice(part * width, (part + 1) * width)
         for start in range(0, count, BLOCK):
-            at = chunk * count + start
-            for part in range(parts):
-                cols = slice(part * width, (part + 1) * width)
-                kept = mask[at // BLOCK : at // BLOCK + 1, cols]
-                value = rows[part, start : start + BLOCK, :] * kept
-                high[at : at + BLOCK, cols], low[at : at + BLOCK, cols] = halves(value)
+            at = first + start
+            kept = mask[at // BLOCK : at // BLOCK + 1, cols]
+            value = piece[start : start + BLOCK, :] * kept
+            high[at : at + BLOCK, cols], low[at : at + BLOCK, cols] = halves(value)
 
 
 def amplitudes(energy, live, vir_col, vir_row, own, panel, amp, a_parts, w_parts):
@@ -90,17 +88,18 @@
     return value + dot_nt(w_parts[1][...], a_parts[0][cols, :])
 
 
-def early_kernel(scalars, vir_col, vir_row, masks, *refs):
-    own, near, twin = (refs[at * CHUNKS : (at + 1) * CHUNKS] for at in range(3))
-    refs = refs[3 * CHUNKS :]
+def early_kernel(cuts, scalars, vir_col, vir_row, masks, *refs):
+    count = len(cuts)
+    own, near, twin = (refs[at * count : (at + 1) * count] for at in range(3))
+    refs = refs[3 * count :]
     own_high, own_low, response, density = refs[:4]
     m_high, m_low, amp, a_high, a_low, w_high, w_low = refs[4:]
-    split_rows(own, masks.at[0], own_high, own_low)
+    split_rows(cuts, own, masks.at[0], own_high, own_low)
     nvir = amp.shape[0]
     parts, _, width = response.shape
     panel, a_parts, w_parts = (m_high, m_low), (a_high, a_low), (w_high, w_low)
-    for turn, chunks in enumerate((near, twin)):
-        split_rows(chunks, masks.at[1 + turn], m_high, m_low)
+    for turn, pieces in enumerate((near, twin)):
+        split_rows(cuts, pieces, masks.at[1 + turn], m_high, m_low)
         amplitudes(
             scalars[2 * turn], scalars[2 * turn + 1], vir_col, vir_row,
             (own_high, own_low), panel, amp, a_parts, w_parts,
@@ -115,64 +114,65 @@
             density[:, cols] = value if turn == 0 else density[:, cols] + value
 
 
-def early(scalars, virtual, masks, own, near, twin):
-    parts, rows, width = own[0].shape
-    nvir, naux = rows * CHUNKS, parts * width
+def early(cuts, scalars, virtual, masks, own, near, twin):
+    nvir, width = own[0].shape
+    naux = masks.shape[2]
     half = jnp.bfloat16
-    outs = [shape(nvir, naux, kind=half)] * 2 + [shape(parts, nvir, width), shape(nvir, nvir)]
+    outs = [shape(nvir, naux, kind=half)] * 2
+    outs += [shape(naux // width, nvir, width), shape(nvir, nvir)]
     scratch = [pltpu.VMEM((nvir, naux), half)] * 2
     scratch += [pltpu.VMEM((nvir, nvir), jnp.float32)]
     scratch += [pltpu.VMEM((nvir, nvir), half)] * 4
     operands = [scalars, virtual[:, None], virtual[None, :], masks, *own, *near, *twin]
     flops = 2 * 3 * 2 * nvir * nvir * (2 * naux + nvir)
-    return call(early_kernel, "early", outs, operands, flops, scratch, 1)
-
-
-def late_kernel(scalars, vir_col, vir_row, masks, own_high, own_low, *refs):
-    sources = refs[:CHUNKS], refs[CHUNKS : 2 * CHUNKS]
-    refs = refs[2 * CHUNKS :]
-    for turn, chunks in enumerate(sources):
+    kernel = functools.partial(early_kernel, cuts)
+    return call(kernel, "early", outs, operands, flops, scratch, 1)
+
+
+def late_kernel(cuts, scalars, vir_col, vir_row, masks, own_high, own_low, *refs):
+    count = len(cuts)
+    sources = refs[:count], refs[count : 2 * count]
+    refs = refs[2 * count :]
+    for turn, pieces in enumerate(sources):
         m_high, m_low, a_high, a_low, w_high, w_low = refs[6 * turn : 6 * turn + 6]
-        split_rows(chunks, masks.at[turn], m_high, m_low)
+        split_rows(cuts, pieces, masks.at[turn], m_high, m_low)
         amplitudes(
             scalars[2 * turn], scalars[2 * turn + 1], vir_col, vir_row,
             (own_high, own_low), (m_high, m_low), refs[12], (a_high, a_low), (w_high, w_low),
         )
 
 
-def late(scalars, virtual, masks, own, far, twin):
+def late(cuts, scalars, virtual, masks, own, far, twin):
     nvir, naux = own[0].shape
     half = jnp.bfloat16
     outs = ([shape(nvir, naux, kind=half)] * 2 + [shape(nvir, nvir, kind=half)] * 4) * 2
     operands = [scalars, virtual[:, None], virtual[None, :], masks, *own, *far, *twin]
     flops = 2 * 3 * 2 * nvir * nvir * naux
     scratch = [pltpu.VMEM((nvir, nvir), jnp.float32)]
-    outs = call(late_kernel, "late", outs, operands, flops, scratch, 1)
+    kernel = functools.partial(late_kernel, cuts)
+    outs = call(kernel, "late", outs, operands, flops, scratch, 1)
     return outs[:6], outs[6:]
 
 
-def response_kernel(first, before, *refs):
-    pieces = refs[8:]
-    for piece in pieces:
-        parts, count, width = piece.shape
+def response_kernel(wanted, before, *refs):
+    for (part, first, count), piece in zip(wanted, refs[8:]):
         rows = slice(first, first + count)
-        for part in range(parts):
-            cols = slice(part * width, (part + 1) * width)
-            value = before[part, rows, :]
-            for at in (0, 4):
-                value += respond(rows, refs[at + 2 : at + 4], refs[at : at + 2], cols)
-            piece[part] = value
-        first += count
-
-
-def responses(first, counts, before, panels):
-    parts, nvir, width = before.shape
-    outs = [shape(parts, count, width) for count in counts]
+        width = piece.shape[1]
+        cols = slice(part * width, (part + 1) * width)
+        value = before[part, rows, :]
+        for at in (0, 4):
+            value += respond(rows, refs[at + 2 : at + 4], refs[at : at + 2], cols)
+        piece[...] = value
+
+
+def responses(wanted, before, panels):
+    _, nvir, width = before.shape
+    outs = [shape(count, width) for _, _, count in wanted]
     operands = [before]
     for m_high, m_low, _, _, w_high, w_low in panels:
         operands += [m_high, m_low, w_high, w_low]
-    flops = 2 * 3 * 2 * sum(counts) * nvir * parts * width
-    return call(functools.partial(response_kernel, first), "response", outs, operands, flops)
+    flops = 2 * 3 * 2 * sum(out.size for out in outs) * nvir
+    return call(functools.partial(response_kernel, wanted), "response", outs, operands, flops)
 
 
 def density_kernel(scale, before, *refs):
@@ -199,8 +199,8 @@
     return lax.ppermute(value, axis, [(at, at ^ bit) for at in range(size)])
 
 
-def swap_parts(value):
-    return lax.all_to_all(value, "row", split_axis=0, concat_axis=0, tiled=True)
+def after(value, *others):
+    return lax.optimization_barrier((value, *others))[0]
 
 
 def bits(axis):
@@ -219,10 +219,9 @@
 
 
 def sum_row(value):
-    terms = [value] + [exchange(value, "row", bit) for bit in range(1, lax.axis_size("row"))]
-    while len(terms) > 1:
-        terms = [terms[at] + terms[at + 1] for at in range(0, len(terms), 2)]
-    return terms[0]
+    for bit in bits("row"):
+        value = value + exchange(value, "row", bit)
+    return value
 
 
 def gather_plane(value):
@@ -233,6 +232,11 @@
             side == 0, jnp.concatenate([value, other]), jnp.concatenate([other, value])
         )
     return value
+
+
+def cut_list(nvir, row_count):
+    cuts = [(part, 0, nvir) for part in range(row_count - 1)]
+    return cuts + [(row_count - 1, at, nvir // 2) for at in (0, nvir // 2)]
 
 
 def on_device(three_index, occ_energy, vir_energy, block_mask, pair_list):
@@ -244,28 +248,37 @@
     group = col // NPANEL
     groups = col_count // NPANEL
     nvir = three_index.shape[1]
-    step = nvir // CHUNKS
-
-    own, near, far, near_twin, far_twin = [], [], [], [], []
-    for chunk in range(CHUNKS):
-        rows = swap_parts(three_index[:, chunk * step : (chunk + 1) * step, :])
+    cuts = cut_list(nvir, row_count)
+
+    own, near, far, near_twin = [], [], [], []
+    for at, (part, first, count) in enumerate(cuts):
+        rows = lax.dynamic_index_in_dim(three_index, row ^ part, 0, keepdims=False)
+        rows = rows[first : first + count]
+        if part:
+            if at > 2:
+                rows = after(rows, own[at - 2])
+            rows = exchange(rows, "row", part)
         own.append(rows)
+        if at > 1:
+            rows = after(rows, near[at - 2])
         reach = 1
         while reach < groups:
-            count = min(reach, groups - reach) * NPANEL
-            links = [(at, at + reach * NPANEL) for at in range(count)]
+            span = min(reach, groups - reach) * NPANEL
+            links = [(one, one + reach * NPANEL) for one in range(span)]
             got = lax.ppermute(rows, "col", links)
             rows = jnp.where((group >= reach) & (group < 2 * reach), got, rows)
             reach *= 2
         near.append(rows)
-        far.append(exchange(rows, "col", 2))
+        sent = after(rows, far[at - 2]) if at > 1 else rows
+        far.append(exchange(sent, "col", 2))
         near_twin.append(exchange(rows, "col", 1))
-        far_twin.append(exchange(far[-1], "col", 1))
 
     own_orbital = col * row_count + row
     panels = [position ^ turn for turn in range(NPANEL)]
     orbitals = jnp.stack([own_orbital] + [at * row_count + row for at in panels])
-    masks = jnp.repeat(block_mask[orbitals].astype(jnp.float32), BLOCK, axis=-1)
+    kept = block_mask[orbitals].reshape(NPANEL + 1, block_mask.shape[1], row_count, -1)
+    kept = kept[:, :, row ^ jnp.arange(row_count), :].reshape(NPANEL + 1, kept.shape[1], -1)
+    masks = jnp.repeat(kept.astype(jnp.float32), BLOCK, axis=-1)
     lists = pair_list[row]
     scalars = []
     for turn in range(NPANEL):
@@ -274,22 +287,29 @@
     first, second = jnp.stack(scalars[:4]), jnp.stack(scalars[4:])
 
     own_high, own_low, response, density = early(
-        first, vir_energy, masks[:3], own, near, near_twin
+        cuts, first, vir_energy, masks[:3], own, near, near_twin
     )
-    last = late(second, vir_energy, masks[3:], (own_high, own_low), far, far_twin)
-    half, quarter = nvir // 2, nvir // 4
-    head = responses(0, [half], response, last)
-    middle, tail = responses(half, [quarter, quarter], response, last)
+    far_twin = [exchange(piece, "col", 1) for piece in far[:-2]]
+    far_twin += [exchange(after(piece, response), "col", 1) for piece in far[-2:]]
+    last = late(cuts, second, vir_energy, masks[3:], (own_high, own_low), far, far_twin)
+
+    middle = row_count // 2
+    head = [(middle, 0, nvir)]
+    rest = [(at, 0, nvir) for at in range(row_count) if at != middle]
+    pieces = list(responses(head, response, last))
+    density = after(density, pieces[0])
     density = densities(1.0 / (row_count * col_count), density, last)
-
-    returned = [swap_parts(head[0])]
-    piece = scatter_plane(density)
-    piece, middle = lax.optimization_barrier((piece, middle))
-    returned.append(swap_parts(middle))
-    piece = sum_row(piece)
-    piece, tail = lax.optimization_barrier((piece, tail))
-    returned.append(swap_parts(tail))
-    return jnp.concatenate(returned, axis=1), gather_plane(piece)
+    response = after(response, density)
+    pieces += responses(rest, response, last)
+    total = sum_row(scatter_plane(density))
+    pieces[-1] = after(pieces[-1], total)
+
+    returned = jnp.zeros_like(three_index)
+    for (part, _, _), piece in zip(head + rest, pieces):
+        if part:
+            piece = exchange(piece, "row", part)
+        returned = lax.dynamic_update_index_in_dim(returned, piece, row ^ part, 0)
+    return returned, gather_plane(total)
 
 
 def solution(mesh):

time: 261 us -> 208 us (0.80)
  blocking collectives: 53.7 us -> 0 us
  local copies, waits for them, and re-layouts: 11.6 us -> 24.7 us
  waiting for transfers between devices: 96.5 us -> 86.5 us
  Pallas kernels: 32.1 us -> 24.9 us
  other arithmetic: 9.5 us -> 12.8 us
    all_to_all x3 -> x0, blocking collectives: 53.7 us -> none  [swap_parts(): return lax.all_to_all(value, 'row', split_axis=0, concat_axis=0, tiled=True)]
    ppermute x21 -> x30, waiting for transfers between devices: 53.5 us -> 74.1 us  [exchange(): return lax.ppermute(value, axis, [(at, at ^ bit) for at in range(size)])]
    all_to_all x4 -> x0, waiting for transfers between devices: 16.6 us -> none  [swap_parts(): return lax.all_to_all(value, 'row', split_axis=0, concat_axis=0, tiled=True)]
    all_to_all x4 -> x0, starting transfers between devices: 15.6 us -> none  [swap_parts(): return lax.all_to_all(value, 'row', split_axis=0, concat_axis=0, tiled=True)]
    ppermute x4 -> x5, waiting for transfers between devices: 26.4 us -> 12.4 us  [on_device(): got = lax.ppermute(rows, 'col', links)]
    ppermute x21 -> x30, starting transfers between devices: 20.9 us -> 29.3 us  [exchange(): return lax.ppermute(value, axis, [(at, at ^ bit) for at in range(size)])]
    unnamed x29 -> x41, local copies, waits for them, and re-layouts: 4.25 us -> 12.1 us
    ppermute x4 -> x5, starting transfers between devices: 12 us -> 19.7 us  [on_device(): got = lax.ppermute(rows, 'col', links)]
  transfers between devices with their start and end apart: 29 -> 35, of which waited for: 13 -> 14; matrix products, arithmetic and copies ran while one was open for 5% -> 10% of each run, Pallas kernels for 8% -> 6%
where the time goes in v1:
time: 208 us; the launch traced here: 206 us
  waiting for transfers between devices  86.5 us (42%)
  starting transfers between devices  49 us (24%)
  Pallas kernels  24.9 us (12%)
  local copies, waits for them, and re-layouts  24.7 us (12%)
  other arithmetic  12.8 us (6%)
  between operations  8.62 us (4%)
    ppermute x30, waiting for transfers between devices, exchange(): return lax.ppermute(value, axis, [(at, at ^ bit) for at in range(size)])  74.1 us
    ppermute x30, starting transfers between devices, exchange(): return lax.ppermute(value, axis, [(at, at ^ bit) for at in range(size)])  29.3 us
    pallas_call x4, Pallas kernels, call(): pl.pallas_call(kernel, out_shape=outs, in_specs=[SMEM] * scalars + [VMEM]...  24.9 us
    ppermute x5, starting transfers between devices, on_device(): got = lax.ppermute(rows, 'col', links)  19.7 us
    ppermute x5, waiting for transfers between devices, on_device(): got = lax.ppermute(rows, 'col', links)  12.4 us
    unnamed x41, local copies, waits for them, and re-layouts  12.1 us
    pallas_call x1, other arithmetic, call(): pl.pallas_call(kernel, out_shape=outs, in_specs=[SMEM] * scalars + [VMEM]...  5.2 us
  transfers between devices with their start and end apart: 35, of which 14 were waited for; matrix products, arithmetic and copies ran while one was open for 10% of the time, Pallas kernels for 6%

profile of v1, /device:TPU:0, one launch (start us, length us, event | category | flops | bytes accessed | tf_op | source)
XLA Modules:
  0.0 206.4 jit_solution(12436331834647710331)
XLA Ops:
  0.6 1.5 dynamic-slice_bitcast_fusion
  2.1 5.7 %collective-permute-start.4 = (f32[512,256]{1,0:T(8,128)S(1)}, f32[512,256]{1,0:T(8,128)}, u32[]{:S(2)}, u32[]{:S(2)}) collective-permute-start(f32[512,256]{1,0:T(8,128)S(1)} %get-tuple-element.80.refs_0_), channel_id=1, source_target_pairs={{0,4},{1,5},{2,6},{3,7},{8,12},{9,13},{10,14},{11,15},{16,20},{17,... | collective-permute-start | bytes 1572872 | tf_op jit(solution)/shard_map/ppermute | solution.py:268
  7.8 2.6 %collective-permute-start.1 = (f32[512,256]{1,0:T(8,128)S(1)}, f32[512,256]{1,0:T(8,128)S(1)}, u32[]{:S(2)}, u32[]{:S(2)}) collective-permute-start(f32[512,256]{1,0:T(8,128)S(1)} %get-tuple-element.78), channel_id=1, source_target_pairs={{0,16},{8,24},{16,0},{24,8},{1,17},{9,25},{17,1},{25,9},{2,18},{10... | collective-permute-start | bytes 1572872 | tf_op jit(solution)/shard_map/ppermute | solution.py:199
  10.4 1.6 collective-permute-start
  12.1 6.1 %collective-permute-done.4 = f32[512,256]{1,0:T(8,128)} collective-permute-done((f32[512,256]{1,0:T(8,128)S(1)}, f32[512,256]{1,0:T(8,128)}, u32[]{:S(2)}, u32[]{:S(2)}) %collective-permute-start.4) | collective-permute-done | bytes 524320 | tf_op jit(solution)/shard_map/ppermute | solution.py:268
  18.2 15.2 %collective-permute-done.1.refs_2_ = f32[512,256]{1,0:T(8,128)S(1)} collective-permute-done((f32[512,256]{1,0:T(8,128)S(1)}, f32[512,256]{1,0:T(8,128)S(1)}, u32[]{:S(2)}, u32[]{:S(2)}) %collective-permute-start.1) | collective-permute-done | bytes 524320 | tf_op jit(solution)/shard_map/ppermute | solution.py:199
  33.4 2.1 %collective-permute-start.6 = (f32[512,256]{1,0:T(8,128)S(1)}, f32[512,256]{1,0:T(8,128)}, u32[]{:S(2)}, u32[]{:S(2)}) collective-permute-start(f32[512,256]{1,0:T(8,128)S(1)} %collective-permute-done.1.refs_2_), channel_id=1, source_target_pairs={{0,4},{1,5},{2,6},{3,7},{8,12},{9,13},{10,14},{11,15},{16,20},{17,... | collective-permute-start | bytes 1572872 | tf_op jit(solution)/shard_map/ppermute | solution.py:268
  35.5 1.5 collective-permute-start.14
  37.0 2.1 %collective-permute-start.5 = (f32[512,256]{1,0:T(8,128)S(1)}, f32[512,256]{1,0:T(8,128)}, u32[]{:S(2)}, u32[]{:S(2)}) collective-permute-start(f32[512,256]{1,0:T(8,128)S(1)} %collective-permute-done.refs_1_), channel_id=1, source_target_pairs={{0,4},{1,5},{2,6},{3,7},{8,12},{9,13},{10,14},{11,15},{16,20},{17,... | collective-permute-start | bytes 1572872 | tf_op jit(solution)/shard_map/ppermute | solution.py:268
  39.1 1.1 dynamic-slice_bitcast_fusion.3
  40.2 3.4 %collective-permute-start.3 = (f32[256,256]{1,0:T(8,128)S(1)}, f32[256,256]{1,0:T(8,128)S(1)}, u32[]{:S(2)}, u32[]{:S(2)}) collective-permute-start(f32[256,256]{1,0:T(8,128)S(1)} %get-tuple-element.35), channel_id=1, source_target_pairs={{0,24},{8,16},{16,8},{24,0},{1,25},{9,17},{17,9},{25,1},{2,26},{10... | collective-permute-start | bytes 786440 | tf_op jit(solution)/shard_map/ppermute | solution.py:199
  44.1 3.0 %collective-permute-done.6 = f32[512,256]{1,0:T(8,128)} collective-permute-done((f32[512,256]{1,0:T(8,128)S(1)}, f32[512,256]{1,0:T(8,128)}, u32[]{:S(2)}, u32[]{:S(2)}) %collective-permute-start.6) | collective-permute-done | bytes 524320 | tf_op jit(solution)/shard_map/ppermute | solution.py:268
  47.2 1.1 collective-permute-done.14.refs_0_
  48.3 1.5 collective-permute-start.16
  49.7 1.6 collective-permute-done.3.refs_4_
  51.4 3.6 %collective-permute-start.8 = (f32[256,256]{1,0:T(8,128)S(1)}, f32[256,256]{1,0:T(8,128)}, u32[]{:S(2)}, u32[]{:S(2)}) collective-permute-start(f32[256,256]{1,0:T(8,128)S(1)} %collective-permute-done.3.refs_4_), channel_id=1, source_target_pairs={{0,4},{1,5},{2,6},{3,7},{8,12},{9,13},{10,14},{11,15},{16,20},{17,... | collective-permute-start | bytes 786440 | tf_op jit(solution)/shard_map/ppermute | solution.py:268
  55.0 3.3 %collective-permute-done.5 = f32[512,256]{1,0:T(8,128)} collective-permute-done((f32[512,256]{1,0:T(8,128)S(1)}, f32[512,256]{1,0:T(8,128)}, u32[]{:S(2)}, u32[]{:S(2)}) %collective-permute-start.5) | collective-permute-done | bytes 524320 | tf_op jit(solution)/shard_map/ppermute | solution.py:268
  58.4 1.6 collective-permute-start.15
  59.9 6.2 %collective-permute-start.7 = (f32[256,256]{1,0:T(8,128)}, f32[256,256]{1,0:T(8,128)}, u32[]{:S(2)}, u32[]{:S(2)}) collective-permute-start(f32[256,256]{1,0:T(8,128)} %collective-permute-done.2.refs_3_), channel_id=1, source_target_pairs={{0,4},{1,5},{2,6},{3,7},{8,12},{9,13},{10,14},{11,15},{16,20},{17,... | collective-permute-start | bytes 786440 | tf_op jit(solution)/shard_map/ppermute | solution.py:268
  69.4 1.4 compare_reduce_fusion.1
  72.0 0.9 copy.12
  73.0 1.2 gather_fusion
  74.1 0.8 copy.13
  76.1 0.8 broadcast_select_fusion.3.refs_9_
  77.0 1.7 broadcast_select_fusion.4.refs_8_
  79.3 0.8 broadcast_in_dim.34
  80.1 1.0 slice.34.masks
  82.4 1.5 collective-permute-start.17
  84.4 0.9 copy-done.8
  85.3 11.4 %early.1 = (bf16[512,1024]{1,0:T(8,128)(2,1)}, bf16[512,1024]{1,0:T(8,128)(2,1)}, f32[4,512,256]{2,1,0:T(8,128)}, f32[512,512]{1,0:T(8,128)}) custom-call(f32[4]{0:T(128)S(1)} %pad_maximum_fusion.scalars, f32[512,1]{1,0:T(8,128)S(1)} %copy.16.vir_col, f32[1,512]{1,0:T(1,128)S(1)} %bitcast.43, f32[3,8,1024]{2,1,0:T(8,128)S(1)} %slice.34.masks, ...), custom_call_target="tpu_custom_call" | custom-call | flops 8053063680 | bytes 11636752 | tf_op jit(solution)/shard_map/early/pallas_call | solution.py:21
  101.5 0.7 copy-done.12
  102.2 0.7 copy-done.14
  102.9 1.0 copy-done.11
  104.0 0.9 copy-done.13
  104.9 0.9 copy-done.15
  105.9 7.2 %late.1 = (bf16[512,1024]{1,0:T(8,128)(2,1)}, bf16[512,1024]{1,0:T(8,128)(2,1)}, bf16[512,512]{1,0:T(8,128)(2,1)S(1)}, bf16[512,512]{1,0:T(8,128)(2,1)S(1)}, bf1...) custom-call(f32[4]{0:T(128)S(1)} %pad_maximum_fusion.1.scalars, ...), custom_call_target="tpu_custom_call" | custom-call | flops 3221225472 | bytes 14749712 | tf_op jit(solution)/shard_map/late/pallas_call | solution.py:21
  113.1 1.2 copy-done
  114.3 1.2 copy-done.2
  115.5 1.2 copy-done.4
  116.7 3.0 %response.2 = f32[512,256]{1,0:T(8,128)S(1)} custom-call(f32[4,512,256]{2,1,0:T(8,128)} %get-tuple-element.61.before, bf16[512,1024]{1,0:T(8,128)(2,1)S(1)} %copy-done, bf16[512,1024]{1,0:T(8,128)(2,1)S(1)} %copy-done.2, bf16[512,512]{1,0:T(8,128)(2,1)S(1)} %get-tuple-element.49.refs_2_, bf16[512,512]{1,0:T(8,128)(2,1)S(1)} %get-tuple-element.50.refs_3_, ...), custom_call_target="tpu_custom_call" | custom-call | flops 805306368 | bytes 8912896 | tf_op jit(solution)/shard_map/response/pallas_call | solution.py:21
  119.8 3.2 %density.1 = f32[512,512]{1,0:T(8,128)S(1)} custom-call(f32[512,512]{1,0:T(8,128)} %get-tuple-element.56.before, bf16[512,512]{1,0:T(8,128)(2,1)S(1)} %get-tuple-element.57.refs_0_, bf16[512,512]{1,0:T(8,128)(2,1)S(1)} %get-tuple-element.58.refs_1_, bf16[512,512]{1,0:T(8,128)(2,1)S(1)} %get-tuple-element.49.refs_2_, ...), custom_call_target="tpu_custom_call" | custom-call | flops 1610612736 | bytes 6291456 | tf_op jit(solution)/shard_map/density/pallas_call | solution.py:21
  123.0 0.8 constant_dynamic-slice_fusion.2
  123.9 2.2 %collective-permute-done.26 = f32[256,512]{1,0:T(8,128)} collective-permute-done((f32[256,512]{1,0:T(8,128)}, f32[256,512]{1,0:T(8,128)}, u32[]{:S(2)}, u32[]{:S(2)}) %collective-permute-start.26) | collective-permute-done | bytes 524320 | tf_op jit(solution)/shard_map/ppermute | solution.py:199
  126.1 1.1 dynamic-slice_add_fusion
  127.3 0.8 copy-done.18
  128.7 7.8 %collective-permute-done.27 = f32[128,512]{1,0:T(8,128)S(1)} collective-permute-done((f32[128,512]{1,0:T(8,128)S(1)}, f32[128,512]{1,0:T(8,128)S(1)}, u32[]{:S(2)}, u32[]{:S(2)}) %collective-permute-start.27) | collective-permute-done | bytes 262176 | tf_op jit(solution)/shard_map/ppermute | solution.py:199
  136.5 1.0 dynamic-slice_add_fusion.1
  138.2 1.3 collective-permute-start.24
  139.5 3.9 %collective-permute-done.28 = f32[64,512]{1,0:T(8,128)S(1)} collective-permute-done((f32[64,512]{1,0:T(8,128)}, f32[64,512]{1,0:T(8,128)S(1)}, u32[]{:S(2)}, u32[]{:S(2)}) %collective-permute-start.28) | collective-permute-done | bytes 131104 | tf_op jit(solution)/shard_map/ppermute | solution.py:199
  143.4 1.7 collective-permute-start.29
  145.0 8.2 %collective-permute-done.29 = f32[64,512]{1,0:T(8,128)S(1)} collective-permute-done((f32[64,512]{1,0:T(8,128)S(1)}, f32[64,512]{1,0:T(8,128)S(1)}, u32[]{:S(2)}, u32[]{:S(2)}) %collective-permute-start.29) | collective-permute-done | bytes 131104 | tf_op jit(solution)/shard_map/ppermute | solution.py:199
  153.2 3.7 %collective-permute-start.30 = (f32[64,512]{1,0:T(8,128)S(1)}, f32[64,512]{1,0:T(8,128)S(1)}, u32[]{:S(2)}, u32[]{:S(2)}) collective-permute-start(f32[64,512]{1,0:T(8,128)S(1)} %add.174), channel_id=1, source_target_pairs={{0,16},{8,24},{16,0},{24,8},{1,17},{9,25},{17,1},{25,9},{2,18},{10... | collective-permute-start | bytes 393224 | tf_op jit(solution)/shard_map/ppermute | solution.py:199
  157.0 12.3 %collective-permute-done.30 = f32[64,512]{1,0:T(8,128)S(1)} collective-permute-done((f32[64,512]{1,0:T(8,128)S(1)}, f32[64,512]{1,0:T(8,128)S(1)}, u32[]{:S(2)}, u32[]{:S(2)}) %collective-permute-start.30) | collective-permute-done | bytes 131104 | tf_op jit(solution)/shard_map/ppermute | solution.py:199
  169.3 1.8 collective-permute-start.32
  171.3 1.1 bitcast_dynamic-update-slice_fusion.3
  172.4 5.2 %response.3 = (f32[4,512,256]{2,1,0:T(8,128)S(1)}, f32[512,256]{1,0:T(8,128)}, f32[512,256]{1,0:T(8,128)}) fusion(f32[4,512,256]{2,1,0:T(8,128)S(1)} %bitcast_dynamic-update-slice_fusion.3, s32[]{:T(128)S(6)} %select_n.168, f32[4,512,256]{2,1,0:T(8,128)} %get-tuple-element.61.before, bf16[512,1024]{1,0:T(8,128)(2,1)S(1)} %copy-done.1, ...), kind=kCustom, calls=%fused_computation.6 | custom fusion | flops 2415919104 | bytes 9961476 | tf_op jit(solution)/shard_map/response/pallas_call | solution.py:21
  177.6 1.3 copy-done.17
  179.5 2.2 %collective-permute-start.31 = (f32[512,256]{1,0:T(8,128)}, f32[512,256]{1,0:T(8,128)S(1)}, u32[]{:S(2)}, u32[]{:S(2)}) collective-permute-start(f32[512,256]{1,0:T(8,128)} %get-tuple-element.65), channel_id=1, source_target_pairs={{0,24},{8,16},{16,8},{24,0},{1,25},{9,17},{17,9},{25,1},{2,26},{10... | collective-permute-start | bytes 1572872 | tf_op jit(solution)/shard_map/ppermute | solution.py:199
  181.7 4.3 %collective-permute-done.33 = f32[128,512]{1,0:T(8,128)S(1)} collective-permute-done((f32[128,512]{1,0:T(8,128)S(1)}, f32[128,512]{1,0:T(8,128)S(1)}, u32[]{:S(2)}, u32[]{:S(2)}) %collective-permute-start.33) | collective-permute-done | bytes 262176 | tf_op jit(solution)/shard_map/ppermute | solution.py:199
  186.2 5.4 %collective-permute-done.25 = f32[512,256]{1,0:T(8,128)S(1)} collective-permute-done((f32[512,256]{1,0:T(8,128)}, f32[512,256]{1,0:T(8,128)S(1)}, u32[]{:S(2)}, u32[]{:S(2)}) %collective-permute-start.25) | collective-permute-done | bytes 524320 | tf_op jit(solution)/shard_map/ppermute | solution.py:199
  191.6 0.8 bitcast_dynamic-update-slice_fusion.1
  192.4 12.0 %collective-permute-done.31 = f32[512,256]{1,0:T(8,128)S(1)} collective-permute-done((f32[512,256]{1,0:T(8,128)}, f32[512,256]{1,0:T(8,128)S(1)}, u32[]{:S(2)}, u32[]{:S(2)}) %collective-permute-start.31) | collective-permute-done | bytes 524320 | tf_op jit(solution)/shard_map/ppermute | solution.py:199
  204.5 0.8 bitcast_dynamic-update-slice_fusion
  205.3 1.1 maximum_select_fusion
  (98 shorter events, 8.3 us)
Async XLA Ops:
  2.1 16.0 %collective-permute-start.4 = (f32[512,256]{1,0:T(8,128)S(1)}, f32[512,256]{1,0:T(8,128)}, u32[]{:S(2)}, u32[]{:S(2)}) collective-permute-start(f32[512,256]{1,0:T(8,128)S(1)} %get-tuple-element.80.refs_0_), channel_id=1, source_target_pairs={{0,4},{1,5},{2,6},{3,7},{8,12},{9,13},{10,14},{11,15},{16,20},{17,... | collective-permute-start | bytes 1572872 | tf_op jit(solution)/shard_map/ppermute | solution.py:268
  7.8 25.6 %collective-permute-start.1 = (f32[512,256]{1,0:T(8,128)S(1)}, f32[512,256]{1,0:T(8,128)S(1)}, u32[]{:S(2)}, u32[]{:S(2)}) collective-permute-start(f32[512,256]{1,0:T(8,128)S(1)} %get-tuple-element.78), channel_id=1, source_target_pairs={{0,16},{8,24},{16,0},{24,8},{1,17},{9,25},{17,1},{25,9},{2,18},{10... | collective-permute-start | bytes 1572872 | tf_op jit(solution)/shard_map/ppermute | solution.py:199
  10.4 26.6 %collective-permute-start = (f32[512,256]{1,0:T(8,128)S(1)}, f32[512,256]{1,0:T(8,128)S(1)}, u32[]{:S(2)}, u32[]{:S(2)}) collective-permute-start(f32[512,256]{1,0:T(8,128)S(1)} %get-tuple-element.79), channel_id=1, source_target_pairs={{0,8},{8,0},{16,24},{24,16},{1,9},{9,1},{17,25},{25,17},{2,10},{10... | collective-permute-start | bytes 1572872 | tf_op jit(solution)/shard_map/ppermute | solution.py:199
  33.4 13.6 %collective-permute-start.6 = (f32[512,256]{1,0:T(8,128)S(1)}, f32[512,256]{1,0:T(8,128)}, u32[]{:S(2)}, u32[]{:S(2)}) collective-permute-start(f32[512,256]{1,0:T(8,128)S(1)} %collective-permute-done.1.refs_2_), channel_id=1, source_target_pairs={{0,4},{1,5},{2,6},{3,7},{8,12},{9,13},{10,14},{11,15},{16,20},{17,... | collective-permute-start | bytes 1572872 | tf_op jit(solution)/shard_map/ppermute | solution.py:268
  35.5 12.7 %collective-permute-start.14 = (f32[512,256]{1,0:T(8,128)S(1)}, f32[512,256]{1,0:T(8,128)S(1)}, u32[]{:S(2)}, u32[]{:S(2)}) collective-permute-start(f32[512,256]{1,0:T(8,128)S(1)} %broadcast_select_fusion.2.refs_5_), channel_id=1, source_target_pairs={{0,2},{1,3},{2,0},{3,1},{4,6},{5,7},{6,4},{7,5},{8,10},{9,11},{10,... | collective-permute-start | bytes 1572872 | tf_op jit(solution)/shard_map/ppermute | solution.py:199
  37.0 21.3 %collective-permute-start.5 = (f32[512,256]{1,0:T(8,128)S(1)}, f32[512,256]{1,0:T(8,128)}, u32[]{:S(2)}, u32[]{:S(2)}) collective-permute-start(f32[512,256]{1,0:T(8,128)S(1)} %collective-permute-done.refs_1_), channel_id=1, source_target_pairs={{0,4},{1,5},{2,6},{3,7},{8,12},{9,13},{10,14},{11,15},{16,20},{17,... | collective-permute-start | bytes 1572872 | tf_op jit(solution)/shard_map/ppermute | solution.py:268
  39.1 27.0 %copy-start.19 = (f32[32]{0:T(128)S(1)}, f32[32]{0:T(128)}, u32[]{:S(2)}) copy-start(f32[32]{0:T(128)} %param.6) | copy-start | bytes 388
  40.2 11.2 %collective-permute-start.3 = (f32[256,256]{1,0:T(8,128)S(1)}, f32[256,256]{1,0:T(8,128)S(1)}, u32[]{:S(2)}, u32[]{:S(2)}) collective-permute-start(f32[256,256]{1,0:T(8,128)S(1)} %get-tuple-element.35), channel_id=1, source_target_pairs={{0,24},{8,16},{16,8},{24,0},{1,25},{9,17},{17,9},{25,1},{2,26},{10... | collective-permute-start | bytes 786440 | tf_op jit(solution)/shard_map/ppermute | solution.py:199
  43.7 16.3 %collective-permute-start.2 = (f32[256,256]{1,0:T(8,128)S(1)}, f32[256,256]{1,0:T(8,128)}, u32[]{:S(2)}, u32[]{:S(2)}) collective-permute-start(f32[256,256]{1,0:T(8,128)S(1)} %get-tuple-element.34), channel_id=1, source_target_pairs={{0,24},{8,16},{16,8},{24,0},{1,25},{9,17},{17,9},{25,1},{2,26},{10... | collective-permute-start | bytes 786440 | tf_op jit(solution)/shard_map/ppermute | solution.py:199
  47.1 34.0 %copy-start.9 = (f32[512]{0:T(512)S(1)}, f32[512]{0:T(512)}, u32[]{:S(2)}) copy-start(f32[512]{0:T(512)} %param.7) | copy-start | bytes 6148
  48.2 6.7 %copy-start.10 = (f32[512,256]{1,0:T(8,128)}, f32[512,256]{1,0:T(8,128)S(1)}, u32[]{:S(2)}) copy-start(f32[512,256]{1,0:T(8,128)S(1)} %collective-permute-done.14.refs_0_) | copy-start | bytes 1572868
  48.3 30.4 %collective-permute-start.16 = (f32[512,256]{1,0:T(8,128)S(1)}, f32[512,256]{1,0:T(8,128)}, u32[]{:S(2)}, u32[]{:S(2)}) collective-permute-start(f32[512,256]{1,0:T(8,128)S(1)} %broadcast_select_fusion.refs_7_), channel_id=1, source_target_pairs={{0,2},{1,3},{2,0},{3,1},{4,6},{5,7},{6,4},{7,5},{8,10},{9,11},{10,... | collective-permute-start | bytes 1572872 | tf_op jit(solution)/shard_map/ppermute | solution.py:199
  51.4 29.8 %copy-start.7 = (f32[256,256]{1,0:T(8,128)}, f32[256,256]{1,0:T(8,128)S(1)}, u32[]{:S(2)}) copy-start(f32[256,256]{1,0:T(8,128)S(1)} %collective-permute-done.3.refs_4_) | copy-start | bytes 786436
  51.4 24.2 %collective-permute-start.8 = (f32[256,256]{1,0:T(8,128)S(1)}, f32[256,256]{1,0:T(8,128)}, u32[]{:S(2)}, u32[]{:S(2)}) collective-permute-start(f32[256,256]{1,0:T(8,128)S(1)} %collective-permute-done.3.refs_4_), channel_id=1, source_target_pairs={{0,4},{1,5},{2,6},{3,7},{8,12},{9,13},{10,14},{11,15},{16,20},{17,... | collective-permute-start | bytes 786440 | tf_op jit(solution)/shard_map/ppermute | solution.py:268
  58.4 20.7 %collective-permute-start.15 = (f32[512,256]{1,0:T(8,128)S(1)}, f32[512,256]{1,0:T(8,128)}, u32[]{:S(2)}, u32[]{:S(2)}) collective-permute-start(f32[512,256]{1,0:T(8,128)S(1)} %broadcast_select_fusion.1.refs_6_), channel_id=1, source_target_pairs={{0,2},{1,3},{2,0},{3,1},{4,6},{5,7},{6,4},{7,5},{8,10},{9,11},{10,... | collective-permute-start | bytes 1572872 | tf_op jit(solution)/shard_map/ppermute | solution.py:199
  59.9 17.0 %collective-permute-start.7 = (f32[256,256]{1,0:T(8,128)}, f32[256,256]{1,0:T(8,128)}, u32[]{:S(2)}, u32[]{:S(2)}) collective-permute-start(f32[256,256]{1,0:T(8,128)} %collective-permute-done.2.refs_3_), channel_id=1, source_target_pairs={{0,4},{1,5},{2,6},{3,7},{8,12},{9,13},{10,14},{11,15},{16,20},{17,... | collective-permute-start | bytes 786440 | tf_op jit(solution)/shard_map/ppermute | solution.py:268
  75.5 5.8 %collective-permute-start.9 = (f32[512,256]{1,0:T(8,128)S(1)}, f32[512,256]{1,0:T(8,128)}, u32[]{:S(2)}, u32[]{:S(2)}) collective-permute-start(f32[512,256]{1,0:T(8,128)S(1)} %broadcast_select_fusion.2.refs_5_), channel_id=1, source_target_pairs={{0,1},{1,0},{2,3},{3,2},{4,5},{5,4},{6,7},{7,6},{8,9},{9,8},{10,11... | collective-permute-start | bytes 1572872 | tf_op jit(solution)/shard_map/ppermute | solution.py:199
  75.6 6.2 %collective-permute-start.11 = (f32[512,256]{1,0:T(8,128)S(1)}, f32[512,256]{1,0:T(8,128)}, u32[]{:S(2)}, u32[]{:S(2)}) collective-permute-start(f32[512,256]{1,0:T(8,128)S(1)} %broadcast_select_fusion.refs_7_), channel_id=1, source_target_pairs={{0,1},{1,0},{2,3},{3,2},{4,5},{5,4},{6,7},{7,6},{8,9},{9,8},{10,11... | collective-permute-start | bytes 1572872 | tf_op jit(solution)/shard_map/ppermute | solution.py:199
  76.9 5.5 %collective-permute-start.10 = (f32[512,256]{1,0:T(8,128)S(1)}, f32[512,256]{1,0:T(8,128)}, u32[]{:S(2)}, u32[]{:S(2)}) collective-permute-start(f32[512,256]{1,0:T(8,128)S(1)} %broadcast_select_fusion.1.refs_6_), channel_id=1, source_target_pairs={{0,1},{1,0},{2,3},{3,2},{4,5},{5,4},{6,7},{7,6},{8,9},{9,8},{10,11... | collective-permute-start | bytes 1572872 | tf_op jit(solution)/shard_map/ppermute | solution.py:199
  78.7 5.2 %collective-permute-start.13 = (f32[256,256]{1,0:T(8,128)}, f32[256,256]{1,0:T(8,128)}, u32[]{:S(2)}, u32[]{:S(2)}) collective-permute-start(f32[256,256]{1,0:T(8,128)} %broadcast_select_fusion.3.refs_9_), channel_id=1, source_target_pairs={{0,1},{1,0},{2,3},{3,2},{4,5},{5,4},{6,7},{7,6},{8,9},{9,8},{10,11... | collective-permute-start | bytes 786440 | tf_op jit(solution)/shard_map/ppermute | solution.py:199
  79.1 4.8 %collective-permute-start.12 = (f32[256,256]{1,0:T(8,128)}, f32[256,256]{1,0:T(8,128)}, u32[]{:S(2)}, u32[]{:S(2)}) collective-permute-start(f32[256,256]{1,0:T(8,128)} %broadcast_select_fusion.4.refs_8_), channel_id=1, source_target_pairs={{0,1},{1,0},{2,3},{3,2},{4,5},{5,4},{6,7},{7,6},{8,9},{9,8},{10,11... | collective-permute-start | bytes 786440 | tf_op jit(solution)/shard_map/ppermute | solution.py:199
  81.4 20.1 %collective-permute-start.19 = (f32[512,256]{1,0:T(8,128)}, f32[512,256]{1,0:T(8,128)}, u32[]{:S(2)}, u32[]{:S(2)}) collective-permute-start(f32[512,256]{1,0:T(8,128)} %copy-done.10), channel_id=1, source_target_pairs={{0,1},{1,0},{2,3},{3,2},{4,5},{5,4},{6,7},{7,6},{8,9},{9,8},{10,11... | collective-permute-start | bytes 1572872 | tf_op jit(solution)/shard_map/ppermute | solution.py:199
  81.8 14.9 %collective-permute-start.18 = (f32[256,256]{1,0:T(8,128)}, f32[256,256]{1,0:T(8,128)}, u32[]{:S(2)}, u32[]{:S(2)}) collective-permute-start(f32[256,256]{1,0:T(8,128)} %broadcast_select_fusion.3.refs_9_), channel_id=1, source_target_pairs={{0,2},{1,3},{2,0},{3,1},{4,6},{5,7},{6,4},{7,5},{8,10},{9,11},{10,... | collective-permute-start | bytes 786440 | tf_op jit(solution)/shard_map/ppermute | solution.py:199
  82.4 14.5 %collective-permute-start.17 = (f32[256,256]{1,0:T(8,128)}, f32[256,256]{1,0:T(8,128)}, u32[]{:S(2)}, u32[]{:S(2)}) collective-permute-start(f32[256,256]{1,0:T(8,128)} %broadcast_select_fusion.4.refs_8_), channel_id=1, source_target_pairs={{0,2},{1,3},{2,0},{3,1},{4,6},{5,7},{6,4},{7,5},{8,10},{9,11},{10,... | collective-permute-start | bytes 786440 | tf_op jit(solution)/shard_map/ppermute | solution.py:199
  83.9 19.1 %collective-permute-start.21 = (f32[512,256]{1,0:T(8,128)}, f32[512,256]{1,0:T(8,128)}, u32[]{:S(2)}, u32[]{:S(2)}) collective-permute-start(f32[512,256]{1,0:T(8,128)} %collective-permute-done.16.refs_2_), channel_id=1, source_target_pairs={{0,1},{1,0},{2,3},{3,2},{4,5},{5,4},{6,7},{7,6},{8,9},{9,8},{10,11... | collective-permute-start | bytes 1572872 | tf_op jit(solution)/shard_map/ppermute | solution.py:199
  83.9 19.0 %collective-permute-start.20 = (f32[512,256]{1,0:T(8,128)}, f32[512,256]{1,0:T(8,128)}, u32[]{:S(2)}, u32[]{:S(2)}) collective-permute-start(f32[512,256]{1,0:T(8,128)} %collective-permute-done.15.refs_1_), channel_id=1, source_target_pairs={{0,1},{1,0},{2,3},{3,2},{4,5},{5,4},{6,7},{7,6},{8,9},{9,8},{10,11... | collective-permute-start | bytes 1572872 | tf_op jit(solution)/shard_map/ppermute | solution.py:199
  84.4 0.9 copy-start.8
  96.7 4.7 %collective-permute-start.23 = (f32[256,256]{1,0:T(8,128)}, f32[256,256]{1,0:T(8,128)S(1)}, u32[]{:S(2)}, u32[]{:S(2)}) collective-permute-start(f32[256,256]{1,0:T(8,128)} %collective-permute-done.18.refs_4_), channel_id=1, source_target_pairs={{0,1},{1,0},{2,3},{3,2},{4,5},{5,4},{6,7},{7,6},{8,9},{9,8},{10,11... | collective-permute-start | bytes 786440 | tf_op jit(solution)/shard_map/ppermute | solution.py:199
  96.8 5.4 %collective-permute-start.22 = (f32[256,256]{1,0:T(8,128)}, f32[256,256]{1,0:T(8,128)S(1)}, u32[]{:S(2)}, u32[]{:S(2)}) collective-permute-start(f32[256,256]{1,0:T(8,128)} %collective-permute-done.17.refs_3_), channel_id=1, source_target_pairs={{0,1},{1,0},{2,3},{3,2},{4,5},{5,4},{6,7},{7,6},{8,9},{9,8},{10,11... | collective-permute-start | bytes 786440 | tf_op jit(solution)/shard_map/ppermute | solution.py:199
  101.5 0.7 copy-start.12
  102.2 0.7 copy-start.14
  102.9 1.0 copy-start.11
  104.0 0.9 copy-start.13
  104.9 0.9 copy-start.15
  113.0 1.2 copy-start
  114.3 1.2 copy-start.2
  115.5 1.2 copy-start.4
  119.8 3.3 %copy-start.6 = (f32[512,256]{1,0:T(8,128)}, f32[512,256]{1,0:T(8,128)S(1)}, u32[]{:S(2)}) copy-start(f32[512,256]{1,0:T(8,128)S(1)} %response.2) | copy-start | bytes 1572868
  123.9 2.3 %collective-permute-start.26 = (f32[256,512]{1,0:T(8,128)}, f32[256,512]{1,0:T(8,128)}, u32[]{:S(2)}, u32[]{:S(2)}) collective-permute-start(f32[256,512]{1,0:T(8,128)} %constant_dynamic-slice_fusion.2), channel_id=1, source_target_pairs={{0,1},{1,0},{2,3},{3,2},{4,5},{5,4},{6,7},{7,6},{8,9},{9,8},{10,11... | collective-permute-start | bytes 1572872 | tf_op jit(solution)/shard_map/ppermute | solution.py:199
  127.2 0.8 copy-start.18
  128.1 8.4 %collective-permute-start.27 = (f32[128,512]{1,0:T(8,128)S(1)}, f32[128,512]{1,0:T(8,128)S(1)}, u32[]{:S(2)}, u32[]{:S(2)}) collective-permute-start(f32[128,512]{1,0:T(8,128)S(1)} %constant_dynamic-slice_fusion.1), channel_id=1, source_target_pairs={{0,2},{1,3},{2,0},{3,1},{4,6},{5,7},{6,4},{7,5},{8,10},{9,11},{10,... | collective-permute-start | bytes 786440 | tf_op jit(solution)/shard_map/ppermute | solution.py:199
  138.2 5.2 %collective-permute-start.28 = (f32[64,512]{1,0:T(8,128)}, f32[64,512]{1,0:T(8,128)S(1)}, u32[]{:S(2)}, u32[]{:S(2)}) collective-permute-start(f32[64,512]{1,0:T(8,128)} %constant_dynamic-slice_fusion), channel_id=1, source_target_pairs={{0,4},{1,5},{2,6},{3,7},{4,0},{5,1},{6,2},{7,3},{8,12},{9,13},{10,... | collective-permute-start | bytes 393224 | tf_op jit(solution)/shard_map/ppermute | solution.py:199
  138.2 32.9 %collective-permute-start.24 = (f32[512,256]{1,0:T(8,128)}, f32[512,256]{1,0:T(8,128)}, u32[]{:S(2)}, u32[]{:S(2)}) collective-permute-start(f32[512,256]{1,0:T(8,128)} %copy-done.6), channel_id=1, source_target_pairs={{0,16},{8,24},{16,0},{24,8},{1,17},{9,25},{17,1},{25,9},{2,18},{10... | collective-permute-start | bytes 1572872 | tf_op jit(solution)/shard_map/ppermute | solution.py:199
  139.5 32.9 %copy-start.1 = (bf16[512,1024]{1,0:T(8,128)(2,1)S(1)}, bf16[512,1024]{1,0:T(8,128)(2,1)}, u32[]{:S(2)}) copy-start(bf16[512,1024]{1,0:T(8,128)(2,1)} %get-tuple-element.47.refs_0_) | copy-start | bytes 3145732
  143.4 9.8 %collective-permute-start.29 = (f32[64,512]{1,0:T(8,128)S(1)}, f32[64,512]{1,0:T(8,128)S(1)}, u32[]{:S(2)}, u32[]{:S(2)}) collective-permute-start(f32[64,512]{1,0:T(8,128)S(1)} %dynamic-slice_add_fusion.2), channel_id=1, source_target_pairs={{0,8},{8,0},{16,24},{24,16},{1,9},{9,1},{17,25},{25,17},{2,10},{10... | collective-permute-start | bytes 393224 | tf_op jit(solution)/shard_map/ppermute | solution.py:199
  153.2 16.1 %collective-permute-start.30 = (f32[64,512]{1,0:T(8,128)S(1)}, f32[64,512]{1,0:T(8,128)S(1)}, u32[]{:S(2)}, u32[]{:S(2)}) collective-permute-start(f32[64,512]{1,0:T(8,128)S(1)} %add.174), channel_id=1, source_target_pairs={{0,16},{8,24},{16,0},{24,8},{1,17},{9,25},{17,1},{25,9},{2,18},{10... | collective-permute-start | bytes 393224 | tf_op jit(solution)/shard_map/ppermute | solution.py:199
  156.9 15.4 %copy-start.3 = (bf16[512,1024]{1,0:T(8,128)(2,1)S(1)}, bf16[512,1024]{1,0:T(8,128)(2,1)}, u32[]{:S(2)}) copy-start(bf16[512,1024]{1,0:T(8,128)(2,1)} %get-tuple-element.48.refs_1_) | copy-start | bytes 3145732
  156.9 15.4 %copy-start.5 = (bf16[512,1024]{1,0:T(8,128)(2,1)S(1)}, bf16[512,1024]{1,0:T(8,128)(2,1)}, u32[]{:S(2)}) copy-start(bf16[512,1024]{1,0:T(8,128)(2,1)} %get-tuple-element.51.refs_4_) | copy-start | bytes 3145732
  157.0 15.4 %copy-start.16 = (bf16[512,1024]{1,0:T(8,128)(2,1)S(1)}, bf16[512,1024]{1,0:T(8,128)(2,1)}, u32[]{:S(2)}) copy-start(bf16[512,1024]{1,0:T(8,128)(2,1)} %get-tuple-element.52.refs_5_) | copy-start | bytes 3145732
  169.3 9.6 %collective-permute-start.32 = (f32[64,512]{1,0:T(8,128)S(1)}, f32[64,512]{1,0:T(8,128)S(1)}, u32[]{:S(2)}, u32[]{:S(2)}) collective-permute-start(f32[64,512]{1,0:T(8,128)S(1)} %add.175), channel_id=1, source_target_pairs={{0,4},{1,5},{2,6},{3,7},{4,0},{5,1},{6,2},{7,3},{8,12},{9,13},{10,... | collective-permute-start | bytes 393224 | tf_op jit(solution)/shard_map/ppermute | solution.py:199
  177.6 1.3 copy-start.17
  178.9 12.7 %collective-permute-start.25 = (f32[512,256]{1,0:T(8,128)}, f32[512,256]{1,0:T(8,128)S(1)}, u32[]{:S(2)}, u32[]{:S(2)}) collective-permute-start(f32[512,256]{1,0:T(8,128)} %get-tuple-element.69), channel_id=1, source_target_pairs={{0,8},{8,0},{16,24},{24,16},{1,9},{9,1},{17,25},{25,17},{2,10},{10... | collective-permute-start | bytes 1572872 | tf_op jit(solution)/shard_map/ppermute | solution.py:199
  178.9 7.1 %collective-permute-start.33 = (f32[128,512]{1,0:T(8,128)S(1)}, f32[128,512]{1,0:T(8,128)S(1)}, u32[]{:S(2)}, u32[]{:S(2)}) collective-permute-start(f32[128,512]{1,0:T(8,128)S(1)} %maximum_select_fusion.2), channel_id=1, source_target_pairs={{0,2},{1,3},{2,0},{3,1},{4,6},{5,7},{6,4},{7,5},{8,10},{9,11},{10,... | collective-permute-start | bytes 786440 | tf_op jit(solution)/shard_map/ppermute | solution.py:199
  179.5 24.9 %collective-permute-start.31 = (f32[512,256]{1,0:T(8,128)}, f32[512,256]{1,0:T(8,128)S(1)}, u32[]{:S(2)}, u32[]{:S(2)}) collective-permute-start(f32[512,256]{1,0:T(8,128)} %get-tuple-element.65), channel_id=1, source_target_pairs={{0,24},{8,16},{16,8},{24,0},{1,25},{9,17},{17,9},{25,1},{2,26},{10... | collective-permute-start | bytes 1572872 | tf_op jit(solution)/shard_map/ppermute | solution.py:199
  186.1 19.2 %collective-permute-start.34 = (f32[256,512]{1,0:T(8,128)S(1)}, f32[256,512]{1,0:T(8,128)S(1)}, u32[]{:S(2)}, u32[]{:S(2)}) collective-permute-start(f32[256,512]{1,0:T(8,128)S(1)} %maximum_select_fusion.1), channel_id=1, source_target_pairs={{0,1},{1,0},{2,3},{3,2},{4,5},{5,4},{6,7},{7,6},{8,9},{9,8},{10,11... | collective-permute-start | bytes 1572872 | tf_op jit(solution)/shard_map/ppermute | solution.py:199

commit v2 on v1

v2 whole, which is shorter than its diff:
```python
import functools

import jax
import jax.numpy as jnp
from jax import lax
from jax.experimental import pallas as pl
from jax.experimental.pallas import tpu as pltpu
from jax.sharding import PartitionSpec as P

BLOCK = 64
NPANEL = 4
TILE = 256
VMEM_LIMIT = 24 * 1024 * 1024
SMEM = pl.BlockSpec(memory_space=pltpu.SMEM)
VMEM = pl.BlockSpec(memory_space=pltpu.VMEM)
NT = (((1,), (1,)), ((), ()))


def call(kernel, name, outs, operands, flops, scratch=(), scalars=0):
    size = sum(at.size * at.dtype.itemsize for at in [*outs, *operands])
    return pl.pallas_call(
        kernel,
        out_shape=outs,
        in_specs=[SMEM] * scalars + [VMEM] * (len(operands) - scalars),
        out_specs=[VMEM] * len(outs),
        scratch_shapes=list(scratch),
        compiler_params=pltpu.CompilerParams(vmem_limit_bytes=VMEM_LIMIT),
        cost_estimate=pl.CostEstimate(flops=flops, bytes_accessed=size, transcendentals=0),
        name=name,
    )(*operands)


def shape(*sizes, kind=jnp.float32):
    return jax.ShapeDtypeStruct(sizes, kind)


def halves(value):
    high = value.astype(jnp.bfloat16)
    return high, (value - high.astype(jnp.float32)).astype(jnp.bfloat16)


def dot(left, right):
    return jnp.dot(left, right, preferred_element_type=jnp.float32)


def dot_nt(left, right):
    return lax.dot_general(left, right, NT, preferred_element_type=jnp.float32)


def split_rows(cuts, pieces, mask, high, low):
    for (part, first, count), piece in zip(cuts, pieces):
        width = piece.shape[1]
        cols = slice(part * width, (part + 1) * width)
        for start in range(0, count, BLOCK):
            at = first + start
            kept = mask[at // BLOCK : at // BLOCK + 1, cols]
            value = piece[start : start + BLOCK, :] * kept
            high[at : at + BLOCK, cols], low[at : at + BLOCK, cols] = halves(value)


def amplitudes(energy, live, vir_col, vir_row, own, panel, amp, a_parts, w_parts):
    nvir = amp.shape[0]
    for start in range(0, nvir, TILE):
        cols = slice(start, start + TILE)
        cross = dot_nt(own[0][...], panel[0][cols, :])
        cross += dot_nt(own[0][...], panel[1][cols, :])
        cross += dot_nt(own[1][...], panel[0][cols, :])
        value = cross / (energy - vir_col[...] - vir_row[:, cols]) * live
        amp[:, cols] = value
        a_parts[0][:, cols], a_parts[1][:, cols] = halves(value)
    for above in range(0, nvir, TILE):
        rows = slice(above, above + TILE)
        for start in range(0, nvir, TILE):
            cols = slice(start, start + TILE)
            value = 2.0 * amp[rows, cols] - amp[cols, rows].T
            w_parts[0][rows, cols], w_parts[1][rows, cols] = halves(value)


def respond(rows, w_parts, panel, cols):
    value = dot(w_parts[0][rows, :], panel[0][:, cols])
    value += dot(w_parts[0][rows, :], panel[1][:, cols])
    return value + dot(w_parts[1][rows, :], panel[0][:, cols])


def density_tile(cols, w_parts, a_parts):
    value = dot_nt(w_parts[0][...], a_parts[0][cols, :])
    value += dot_nt(w_parts[0][...], a_parts[1][cols, :])
    return value + dot_nt(w_parts[1][...], a_parts[0][cols, :])


def early_kernel(cuts, parts, scalars, vir_col, vir_row, masks, *refs):
    count = len(cuts)
    own, near, twin = (refs[at * count : (at + 1) * count] for at in range(3))
    refs = refs[3 * count :]
    own_high, own_low, density = refs[:3]
    slices = refs[3 : 3 + parts]
    m_high, m_low, amp, a_high, a_low, w_high, w_low = refs[3 + parts :]
    split_rows(cuts, own, masks.at[0], own_high, own_low)
    nvir = amp.shape[0]
    panel, a_parts, w_parts = (m_high, m_low), (a_high, a_low), (w_high, w_low)
    for turn, pieces in enumerate((near, twin)):
        split_rows(cuts, pieces, masks.at[1 + turn], m_high, m_low)
        amplitudes(
            scalars[2 * turn], scalars[2 * turn + 1], vir_col, vir_row,
            (own_high, own_low), panel, amp, a_parts, w_parts,
        )
        for part, piece in enumerate(slices):
            width = piece.shape[1]
            cols = slice(part * width, (part + 1) * width)
            value = respond(slice(0, nvir), w_parts, panel, cols)
            piece[...] = value if turn == 0 else piece[...] + value
        for start in range(0, nvir, TILE):
            cols = slice(start, start + TILE)
            value = density_tile(cols, w_parts, a_parts)
            density[:, cols] = value if turn == 0 else density[:, cols] + value


def early(cuts, scalars, virtual, masks, own, near, twin):
    nvir, width = own[0].shape
    naux = masks.shape[2]
    parts = naux // width
    half = jnp.bfloat16
    outs = [shape(nvir, naux, kind=half)] * 2 + [shape(nvir, nvir)]
    outs += [shape(nvir, width)] * parts
    scratch = [pltpu.VMEM((nvir, naux), half)] * 2
    scratch += [pltpu.VMEM((nvir, nvir), jnp.float32)]
    scratch += [pltpu.VMEM((nvir, nvir), half)] * 4
    operands = [scalars, virtual[:, None], virtual[None, :], masks, *own, *near, *twin]
    flops = 2 * 3 * 2 * nvir * nvir * (2 * naux + nvir)
    kernel = functools.partial(early_kernel, cuts, parts)
    outs = call(kernel, "early", outs, operands, flops, scratch, 1)
    return outs[0], outs[1], outs[2], list(outs[3:])


def late_kernel(cuts, head, scalars, vir_col, vir_row, masks, own_high, own_low, before, *refs):
    count = len(cuts)
    sources = refs[:count], refs[count : 2 * count]
    refs = refs[2 * count :]
    amp = refs[13]
    for turn, pieces in enumerate(sources):
        m_high, m_low, a_high, a_low, w_high, w_low = refs[6 * turn : 6 * turn + 6]
        split_rows(cuts, pieces, masks.at[turn], m_high, m_low)
        amplitudes(
            scalars[2 * turn], scalars[2 * turn + 1], vir_col, vir_row,
            (own_high, own_low), (m_high, m_low), amp, (a_high, a_low), (w_high, w_low),
        )
    respond_all([head], [before], [refs[12]], refs[:12])


def late(cuts, head, scalars, virtual, masks, own, before, far, twin):
    nvir, naux = own[0].shape
    width = before.shape[1]
    half = jnp.bfloat16
    outs = ([shape(nvir, naux, kind=half)] * 2 + [shape(nvir, nvir, kind=half)] * 4) * 2
    outs += [shape(head[2], width)]
    operands = [scalars, virtual[:, None], virtual[None, :], masks, *own, before, *far, *twin]
    flops = 2 * 3 * 2 * nvir * nvir * (naux + width)
    scratch = [pltpu.VMEM((nvir, nvir), jnp.float32)]
    kernel = functools.partial(late_kernel, cuts, head)
    outs = call(kernel, "late", outs, operands, flops, scratch, 1)
    return list(outs[:12]), outs[12]


def respond_all(wanted, before, pieces, panels):
    for (part, first, count), old, piece in zip(wanted, before, pieces):
        rows = slice(first, first + count)
        width = piece.shape[1]
        cols = slice(part * width, (part + 1) * width)
        value = old[rows, :]
        for at in (0, 6):
            m_high, m_low, _, _, w_high, w_low = panels[at : at + 6]
            value += respond(rows, (w_high, w_low), (m_high, m_low), cols)
        piece[...] = value


def density_kernel(scale, before, *refs):
    panels, total = refs[:8], refs[8]
    for start in range(0, before.shape[0], TILE):
        cols = slice(start, start + TILE)
        value = before[:, cols]
        for at in (0, 4):
            a_high, a_low, w_high, w_low = panels[at : at + 4]
            value += density_tile(cols, (w_high, w_low), (a_high, a_low))
        total[:, cols] = value * scale


def densities(scale, before, panels):
    kernel = functools.partial(density_kernel, scale)
    operands = [before, *panels[2:6], *panels[8:12]]
    return call(kernel, "density", [shape(*before.shape)], operands, 0)[0]


def rest_kernel(wanted, *refs):
    count = len(wanted)
    respond_all(wanted, refs[:count], refs[count + 12 :], refs[count : count + 12])


def rest(wanted, slices, panels):
    width = slices[0].shape[1]
    outs = [shape(count, width) for _, _, count in wanted]
    operands = [slices[part] for part, _, _ in wanted] + panels
    return list(call(functools.partial(rest_kernel, wanted), "rest", outs, operands, 0))


def exchange(value, axis, bit):
    size = lax.axis_size(axis)
    return lax.ppermute(value, axis, [(at, at ^ bit) for at in range(size)])


def after(value, *others):
    return lax.optimization_barrier((value, *others))[0]


def bits(axis):
    size = lax.axis_size(axis)
    return [1 << at for at in range(size.bit_length() - 1)]


def scatter_chip(value):
    half = value.shape[0] // 2
    side = lax.axis_index("col") % 2
    kept = lax.dynamic_slice_in_dim(value, side * half, half, 0)
    sent = lax.dynamic_slice_in_dim(value, (1 - side) * half, half, 0)
    return kept + exchange(sent, "col", 1)


def scatter_plane(value):
    place = lax.axis_index("col") // 2
    chips = lax.axis_size("col") // 2
    count = value.shape[0] // chips
    total = lax.dynamic_slice_in_dim(value, place * count, count, 0)
    for turn in range(1, chips):
        sent = lax.dynamic_slice_in_dim(value, (place ^ turn) * count, count, 0)
        total = total + exchange(sent, "col", 2 * turn)
    return total


def sum_row(value, head, others):
    steps = bits("row")
    value = after(value, head)
    for bit in steps:
        if bit == steps[-1]:
            value = after(value, *others)
        value = value + exchange(value, "row", bit)
    return value


def joined(terms, place):
    if len(terms) == 1:
        return terms[0]
    half = len(terms) // 2
    low, high = joined(terms[:half], place), joined(terms[half:], place)
    side = (place // half) % 2
    return jnp.where(side == 0, jnp.concatenate([low, high]), jnp.concatenate([high, low]))


def gather_plane(value):
    col = lax.axis_index("col")
    turns = range(1, lax.axis_size("col") // 2)
    terms = [value] + [exchange(value, "col", 2 * turn) for turn in turns]
    value = joined(terms, col // 2)
    return joined([value, exchange(value, "col", 1)], col)


def cut_list(nvir, row_count):
    cuts = [(part, 0, nvir) for part in range(row_count - 1)]
    return cuts + [(row_count - 1, at, nvir // 2) for at in (0, nvir // 2)]


def on_device(three_index, occ_energy, vir_energy, block_mask, pair_list):
    row = lax.axis_index("row")
    col = lax.axis_index("col")
    row_count = lax.axis_size("row")
    col_count = lax.axis_size("col")
    position = col % NPANEL
    group = col // NPANEL
    groups = col_count // NPANEL
    nvir = three_index.shape[1]
    cuts = cut_list(nvir, row_count)

    own_orbital = col * row_count + row
    panels = [position ^ turn for turn in range(NPANEL)]
    orbitals = jnp.stack([own_orbital] + [at * row_count + row for at in panels])
    kept = block_mask[orbitals].reshape(NPANEL + 1, block_mask.shape[1], row_count, -1)
    kept = kept[:, :, row ^ jnp.arange(row_count), :].reshape(NPANEL + 1, kept.shape[1], -1)
    masks = jnp.repeat(kept.astype(jnp.float32), BLOCK, axis=-1)
    lists = pair_list[row]
    scalars = []
    for turn in range(NPANEL):
        live = jnp.any(lists == panels[turn]).astype(jnp.float32)
        scalars += [occ_energy[own_orbital] + occ_energy[orbitals[1 + turn]], live]
    small = masks[:3], masks[3:], jnp.stack(scalars[:4]), jnp.stack(scalars[4:])

    own, came, near, far = [], [], [], []

    def receive(at):
        part, first, count = cuts[at]
        rows = lax.dynamic_index_in_dim(three_index, row ^ part, 0, keepdims=False)
        rows = rows[first : first + count]
        if part == row_count - 1:
            rows = after(rows, near[0 if first == 0 else 1])
        own.append(exchange(rows, "row", part) if part else rows)

    for at in range(len(cuts)):
        while len(own) < min(at + 2, len(cuts)) and (at or len(own) < row_count - 1):
            receive(len(own))
        rows = own[at]
        if at:
            rows = after(rows, came[-1])
        if at > 1:
            rows = after(rows, *own[at + 1 : at + 2])
        reach = 1
        while reach < groups:
            span = min(reach, groups - reach) * NPANEL
            links = [(one, one + reach * NPANEL) for one in range(span)]
            got = lax.ppermute(rows, "col", links)
            rows = jnp.where((group >= reach) & (group < 2 * reach), got, rows)
            reach *= 2
        came.append(got)
        near.append(rows)
        sent = after(rows, far[-1]) if at else after(rows, *small)
        far.append(exchange(sent, "col", 2))

    near_twin = [exchange(piece, "col", 1) for piece in near]
    own_high, own_low, density, slices = early(
        cuts, small[2], vir_energy, small[0], own, near, near_twin
    )
    far_twin = [exchange(piece, "col", 1) for piece in far[:-2]]
    far_twin += [exchange(after(piece, density), "col", 1) for piece in far[-2:]]

    middle = row_count // 2
    head = (middle, 0, nvir)
    others = [(at, 0, nvir) for at in range(1, row_count - 1) if at != middle]
    wanted = others + cuts[-2:] + cuts[:1]
    last, piece = late(
        cuts, head, small[3], vir_energy, small[1], (own_high, own_low), slices[middle],
        far, far_twin,
    )
    ends = {head: exchange(piece, "row", middle)}
    scale = 1.0 / (row_count * col_count)
    total = scatter_chip(densities(scale, after(density, piece), last))
    slices[0] = after(slices[0], total)
    pieces = rest(wanted, slices, last)
    for cut, piece in zip(others, pieces):
        ends[cut] = exchange(piece, "row", cut[0])
    total = scatter_plane(total)
    ends[wanted[-3]] = exchange(after(pieces[-3], total), "row", row_count - 1)
    total = sum_row(total, ends[head], [ends[cut] for cut in others])
    ends[wanted[-2]] = exchange(after(pieces[-2], total), "row", row_count - 1)
    ends[wanted[-1]] = pieces[-1]
    total = gather_plane(after(total, ends[wanted[-3]]))

    returned = jnp.zeros_like(three_index)
    for (part, first, _), piece in ends.items():
        returned = lax.dynamic_update_slice(returned, piece[None], (row ^ part, first, 0))
    return returned, total


def solution(mesh):
    placed = (P("col", None, "row"), P(), P(), P(), P("col", None))
    return jax.shard_map(
        on_device,
        mesh=mesh,
        in_specs=placed,
        out_specs=(P("col", None, "row"), P()),
        check_vma=False,
    )
```

time: 208 us -> 193 us (0.928)
  waiting for transfers between devices: 86.5 us -> 67.2 us
  local copies, waits for them, and re-layouts: 24.7 us -> 38.2 us
  other arithmetic: 12.8 us -> 6.71 us
  Pallas kernels: 24.9 us -> 22.3 us
    ppermute x30 -> x33, waiting for transfers between devices: 74.1 us -> 54.3 us  [exchange(): return lax.ppermute(value, axis, [(at, at ^ bit) for at in range(size)])]
    unnamed x41 -> x101, local copies, waits for them, and re-layouts: 12.1 us -> 28.4 us
    pallas_call x1 -> x0, other arithmetic: 5.2 us -> none  [call(): pl.pallas_call(kernel, out_shape=outs, in_specs=[SMEM] * scalars + [VMEM]...]
    pallas_call x4, Pallas kernels: 24.9 us -> 22.3 us  [call(): pl.pallas_call(kernel, out_shape=outs, in_specs=[SMEM] * scalars + [VMEM]...]
    ppermute x30 -> x33, starting transfers between devices: 29.3 us -> 30.1 us  [exchange(): return lax.ppermute(value, axis, [(at, at ^ bit) for at in range(size)])]
  transfers between devices with their start and end apart: 35 -> 38, of which waited for: 14 -> 18; matrix products, arithmetic and copies ran while one was open for 10% -> 7% of each run, Pallas kernels for 6% -> 7%
where the time goes in v2:
time: 193 us; the launch traced here: 191 us
  waiting for transfers between devices  67.2 us (35%)
  starting transfers between devices  48.3 us (25%)
  local copies, waits for them, and re-layouts  38.2 us (20%)
  Pallas kernels  22.3 us (12%)
  between operations  8.77 us (5%)
  other arithmetic  6.71 us (3%)
    ppermute x33, waiting for transfers between devices, exchange(): return lax.ppermute(value, axis, [(at, at ^ bit) for at in range(size)])  54.3 us
    ppermute x33, starting transfers between devices, exchange(): return lax.ppermute(value, axis, [(at, at ^ bit) for at in range(size)])  30.1 us
    unnamed x101, local copies, waits for them, and re-layouts  28.4 us
    pallas_call x4, Pallas kernels, call(): pl.pallas_call(kernel, out_shape=outs, in_specs=[SMEM] * scalars + [VMEM]...  22.3 us
    ppermute x5, starting transfers between devices, on_device(): got = lax.ppermute(rows, 'col', links)  18.2 us
    ppermute x5, waiting for transfers between devices, on_device(): got = lax.ppermute(rows, 'col', links)  13 us
  transfers between devices with their start and end apart: 38, of which 18 were waited for; matrix products, arithmetic and copies ran while one was open for 7% of the time, Pallas kernels for 7%

profile of v2, /device:TPU:0, one launch (start us, length us, event | category | flops | bytes accessed | tf_op | source)
XLA Modules:
  0.0 191.5 jit_solution(11146292558114739226)
XLA Ops:
  0.7 1.5 dynamic-slice_bitcast_fusion
  2.2 5.7 %collective-permute-start.2 = (f32[512,256]{1,0:T(8,128)S(1)}, f32[512,256]{1,0:T(8,128)}, u32[]{:S(2)}, u32[]{:S(2)}) collective-permute-start(f32[512,256]{1,0:T(8,128)S(1)} %get-tuple-element.102.refs_0_), channel_id=1, source_target_pairs={{0,4},{1,5},{2,6},{3,7},{8,12},{9,13},{10,14},{11,15},{16,20},{17,... | collective-permute-start | bytes 1572872 | tf_op jit(solution)/shard_map/ppermute | solution.py:316
  7.9 1.6 collective-permute-start
  9.4 2.6 %collective-permute-start.1 = (f32[512,256]{1,0:T(8,128)S(1)}, f32[512,256]{1,0:T(8,128)S(1)}, u32[]{:S(2)}, u32[]{:S(2)}) collective-permute-start(f32[512,256]{1,0:T(8,128)S(1)} %get-tuple-element.100), channel_id=1, source_target_pairs={{0,16},{8,24},{16,0},{24,8},{1,17},{9,25},{17,1},{25,9},{2,18},{10... | collective-permute-start | bytes 1572872 | tf_op jit(solution)/shard_map/ppermute | solution.py:207
  15.2 1.4 compare_reduce_fusion.1
  23.2 1.8 dynamic-slice_bitcast_fusion.3
  25.0 7.4 %collective-permute-done.refs_1_ = f32[512,256]{1,0:T(8,128)S(1)} collective-permute-done((f32[512,256]{1,0:T(8,128)S(1)}, f32[512,256]{1,0:T(8,128)S(1)}, u32[]{:S(2)}, u32[]{:S(2)}) %collective-permute-start) | collective-permute-done | bytes 524320 | tf_op jit(solution)/shard_map/ppermute | solution.py:207
  32.4 2.1 %collective-permute-start.4 = (f32[512,256]{1,0:T(8,128)S(1)}, f32[512,256]{1,0:T(8,128)}, u32[]{:S(2)}, u32[]{:S(2)}) collective-permute-start(f32[512,256]{1,0:T(8,128)S(1)} %collective-permute-done.refs_1_), channel_id=1, source_target_pairs={{0,4},{1,5},{2,6},{3,7},{8,12},{9,13},{10,14},{11,15},{16,20},{17,... | collective-permute-start | bytes 1572872 | tf_op jit(solution)/shard_map/ppermute | solution.py:316
  34.5 2.5 %collective-permute-start.3 = (f32[256,256]{1,0:T(8,128)S(1)}, f32[256,256]{1,0:T(8,128)S(1)}, u32[]{:S(2)}, u32[]{:S(2)}) collective-permute-start(f32[256,256]{1,0:T(8,128)S(1)} %get-tuple-element.48), channel_id=1, source_target_pairs={{0,24},{8,16},{16,8},{24,0},{1,25},{9,17},{17,9},{25,1},{2,26},{10... | collective-permute-start | bytes 786440 | tf_op jit(solution)/shard_map/ppermute | solution.py:207
  38.4 1.5 collective-permute-start.14
  39.9 4.0 %collective-permute-done.4 = f32[512,256]{1,0:T(8,128)} collective-permute-done((f32[512,256]{1,0:T(8,128)S(1)}, f32[512,256]{1,0:T(8,128)}, u32[]{:S(2)}, u32[]{:S(2)}) %collective-permute-start.4) | collective-permute-done | bytes 524320 | tf_op jit(solution)/shard_map/ppermute | solution.py:316
  43.9 4.5 %collective-permute-start.6 = (f32[512,256]{1,0:T(8,128)S(1)}, f32[512,256]{1,0:T(8,128)S(1)}, u32[]{:S(2)}, u32[]{:S(2)}) collective-permute-start(f32[512,256]{1,0:T(8,128)S(1)} %collective-permute-done.1.refs_2_), channel_id=1, source_target_pairs={{0,4},{1,5},{2,6},{3,7},{8,12},{9,13},{10,14},{11,15},{16,20},{17,... | collective-permute-start | bytes 1572872 | tf_op jit(solution)/shard_map/ppermute | solution.py:316
  48.5 2.4 %collective-permute-done.14.refs_0_ = f32[512,256]{1,0:T(8,128)} collective-permute-done((f32[512,256]{1,0:T(8,128)S(1)}, f32[512,256]{1,0:T(8,128)}, u32[]{:S(2)}, u32[]{:S(2)}) %collective-permute-start.14) | collective-permute-done | bytes 524320 | tf_op jit(solution)/shard_map/ppermute | solution.py:207
  50.9 1.5 collective-permute-start.15
  52.4 1.1 collective-permute-start.5
  53.5 4.2 %collective-permute-done.6 = f32[512,256]{1,0:T(8,128)S(1)} collective-permute-done((f32[512,256]{1,0:T(8,128)S(1)}, f32[512,256]{1,0:T(8,128)S(1)}, u32[]{:S(2)}, u32[]{:S(2)}) %collective-permute-start.6) | collective-permute-done | bytes 524320 | tf_op jit(solution)/shard_map/ppermute | solution.py:316
  57.8 5.2 %collective-permute-done.15.refs_1_ = f32[512,256]{1,0:T(8,128)S(1)} collective-permute-done((f32[512,256]{1,0:T(8,128)S(1)}, f32[512,256]{1,0:T(8,128)S(1)}, u32[]{:S(2)}, u32[]{:S(2)}) %collective-permute-start.15) | collective-permute-done | bytes 524320 | tf_op jit(solution)/shard_map/ppermute | solution.py:207
  63.0 1.5 collective-permute-start.16
  64.5 1.3 collective-permute-start.7
  66.5 3.2 %collective-permute-done.7 = f32[256,256]{1,0:T(8,128)S(1)} collective-permute-done((f32[256,256]{1,0:T(8,128)S(1)}, f32[256,256]{1,0:T(8,128)S(1)}, u32[]{:S(2)}, u32[]{:S(2)}) %collective-permute-start.7) | collective-permute-done | bytes 262176 | tf_op jit(solution)/shard_map/ppermute | solution.py:316
  69.7 4.6 %collective-permute-start.8 = (f32[256,256]{1,0:T(8,128)S(1)}, f32[256,256]{1,0:T(8,128)S(1)}, u32[]{:S(2)}, u32[]{:S(2)}) collective-permute-start(f32[256,256]{1,0:T(8,128)S(1)} %collective-permute-done.5.refs_4_), channel_id=1, source_target_pairs={{0,4},{1,5},{2,6},{3,7},{8,12},{9,13},{10,14},{11,15},{16,20},{17,... | collective-permute-start | bytes 786440 | tf_op jit(solution)/shard_map/ppermute | solution.py:316
  75.0 1.4 collective-permute-start.17
  76.4 1.5 collective-permute-done.8
  78.7 3.0 %collective-permute-done.17.refs_3_ = f32[256,256]{1,0:T(8,128)} collective-permute-done((f32[256,256]{1,0:T(8,128)}, f32[256,256]{1,0:T(8,128)}, u32[]{:S(2)}, u32[]{:S(2)}) %collective-permute-start.17) | collective-permute-done | bytes 262176 | tf_op jit(solution)/shard_map/ppermute | solution.py:207
  83.0 1.4 collective-permute-start.18
  84.4 1.0 copy-done.25
  85.4 1.0 copy-done.27
  88.4 10.3 %early.1 = (bf16[512,1024]{1,0:T(8,128)(2,1)S(1)}, bf16[512,1024]{1,0:T(8,128)(2,1)S(1)}, f32[512,512]{1,0:T(8,128)S(1)}, f32[512,256]{1,0:T(8,128)S(1)}, f32[51...) custom-call(f32[4]{0:T(128)S(1)} %pad_maximum_fusion.1.scalars, f32[512,1]{1,0:T(8,128)S(1)} %copy.19.vir_col, ...), custom_call_target="tpu_custom_call" | custom-call | flops 8053063680 | bytes 11636752 | tf_op jit(solution)/shard_map/early/pallas_call | solution.py:21
  103.8 1.2 collective-permute-done.22.refs_8_
  106.2 1.0 copy-done.35
  107.2 1.2 copy-done.39
  108.5 1.2 copy-done.41
  109.7 1.0 copy-done.43
  110.7 7.3 %late.1 = (bf16[512,1024]{1,0:T(8,128)(2,1)S(1)}, bf16[512,1024]{1,0:T(8,128)(2,1)S(1)}, bf16[512,512]{1,0:T(8,128)(2,1)S(1)}, bf16[512,512]{1,0:T(8,128)(2,1)S(...) custom-call(f32[4]{0:T(128)S(1)} %pad_maximum_fusion.scalars, ...), custom_call_target="tpu_custom_call" | custom-call | flops 4026531840 | bytes 15798288 | tf_op jit(solution)/shard_map/late/pallas_call | solution.py:21
  118.1 1.0 copy-done.16
  119.1 2.0 %density.1 = f32[512,512]{1,0:T(8,128)S(1)} custom-call(f32[512,512]{1,0:T(8,128)S(1)} %copy-done.19, bf16[512,512]{1,0:T(8,128)(2,1)S(1)} %get-tuple-element.72.refs_0_.refs_6_, bf16[512,512]{1,0:T(8,128)(2,1)S(1)} %get-tuple-element.73.refs_1_.refs_7_, bf16[512,512]{1,0:T(8,128)(2,1)S(1)} %get-tuple-element.74.refs_2_.refs_8_, ...), custom_call_target="tpu_custom_call" | custom-call | bytes 6291456 | tf_op jit(solution)/shard_map/density/pallas_call | solution.py:21
  122.6 2.1 %collective-permute-done.25 = f32[256,512]{1,0:T(8,128)} collective-permute-done((f32[256,512]{1,0:T(8,128)}, f32[256,512]{1,0:T(8,128)}, u32[]{:S(2)}, u32[]{:S(2)}) %collective-permute-start.25) | collective-permute-done | bytes 524320 | tf_op jit(solution)/shard_map/ppermute | solution.py:207
  124.7 1.1 dynamic-slice_add_fusion
  125.8 1.2 copy-done.1
  127.1 1.0 copy-done.3
  128.1 1.0 copy-done.5
  129.1 1.0 copy-done.7
  130.2 1.0 copy-done.9
  131.2 1.2 copy-done.13
  132.5 1.2 copy-done.15
  133.7 1.2 copy-done.17
  134.9 1.0 copy-done.21
  135.9 1.0 copy-done.23
  137.0 2.6 %rest.1 = (f32[512,256]{1,0:T(8,128)S(1)}, f32[256,256]{1,0:T(8,128)S(1)}, f32[256,256]{1,0:T(8,128)S(1)}, f32[512,256]{1,0:T(8,128)S(1)}) custom-call(f32[512,256]{1,0:T(8,128)S(1)} %copy-done.23, f32[512,256]{1,0:T(8,128)S(1)} %get-tuple-element.69.refs_1_.refs_2_, f32[512,256]{1,0:T(8,128)S(1)} %get-tuple-element.69.refs_1_.refs_2_, ...), custom_call_target="tpu_custom_call" | custom-call | bytes 12058624 | tf_op jit(solution)/shard_map/rest/pallas_call | solution.py:21
  141.1 2.8 %collective-permute-start.29 = (f32[64,512]{1,0:T(8,128)S(1)}, f32[64,512]{1,0:T(8,128)S(1)}, u32[]{:S(2)}, u32[]{:S(2)}) collective-permute-start(f32[64,512]{1,0:T(8,128)S(1)} %get-tuple-element.104), channel_id=1, source_target_pairs={{0,6},{1,7},{2,4},{3,5},{4,2},{5,3},{6,0},{7,1},{8,14},{9,15},{10,... | collective-permute-start | bytes 393224 | tf_op jit(solution)/shard_map/ppermute | solution.py:207
  143.9 2.9 %collective-permute-done.27 = f32[64,512]{1,0:T(8,128)S(1)} collective-permute-done((f32[64,512]{1,0:T(8,128)S(1)}, f32[64,512]{1,0:T(8,128)S(1)}, u32[]{:S(2)}, u32[]{:S(2)}) %collective-permute-start.27) | collective-permute-done | bytes 131104 | tf_op jit(solution)/shard_map/ppermute | solution.py:207
  146.8 2.4 %collective-permute-done.28 = f32[64,512]{1,0:T(8,128)S(1)} collective-permute-done((f32[64,512]{1,0:T(8,128)S(1)}, f32[64,512]{1,0:T(8,128)S(1)}, u32[]{:S(2)}, u32[]{:S(2)}) %collective-permute-start.28) | collective-permute-done | bytes 131104 | tf_op jit(solution)/shard_map/ppermute | solution.py:207
  150.1 1.8 collective-permute-start.31
  151.9 1.4 collective-permute-start.30
  153.3 13.6 %collective-permute-done.31 = f32[64,512]{1,0:T(8,128)S(1)} collective-permute-done((f32[64,512]{1,0:T(8,128)S(1)}, f32[64,512]{1,0:T(8,128)S(1)}, u32[]{:S(2)}, u32[]{:S(2)}) %collective-permute-start.31) | collective-permute-done | bytes 131104 | tf_op jit(solution)/shard_map/ppermute | solution.py:207
  168.5 1.1 bitcast_dynamic-update-slice_fusion.2
  169.6 7.2 %collective-permute-done.32 = f32[64,512]{1,0:T(8,128)S(1)} collective-permute-done((f32[64,512]{1,0:T(8,128)S(1)}, f32[64,512]{1,0:T(8,128)S(1)}, u32[]{:S(2)}, u32[]{:S(2)}) %collective-permute-start.32) | collective-permute-done | bytes 131104 | tf_op jit(solution)/shard_map/ppermute | solution.py:207
  176.8 1.3 collective-permute-start.34
  178.0 2.3 %collective-permute-start.36 = (f32[64,512]{1,0:T(8,128)S(1)}, f32[64,512]{1,0:T(8,128)S(1)}, u32[]{:S(2)}, u32[]{:S(2)}) collective-permute-start(f32[64,512]{1,0:T(8,128)S(1)} %add.178), channel_id=1, source_target_pairs={{0,6},{1,7},{2,4},{3,5},{4,2},{5,3},{6,0},{7,1},{8,14},{9,15},{10,... | collective-permute-start | bytes 393224 | tf_op jit(solution)/shard_map/ppermute | solution.py:207
  180.4 1.7 collective-permute-start.33
  182.9 3.1 %collective-permute-done.35 = f32[64,512]{1,0:T(8,128)S(1)} collective-permute-done((f32[64,512]{1,0:T(8,128)S(1)}, f32[64,512]{1,0:T(8,128)S(1)}, u32[]{:S(2)}, u32[]{:S(2)}) %collective-permute-start.35) | collective-permute-done | bytes 131104 | tf_op jit(solution)/shard_map/ppermute | solution.py:207
  186.2 1.0 bitcast_dynamic-update-slice_fusion.4
  187.1 2.6 %collective-permute-done.33 = f32[256,256]{1,0:T(8,128)S(1)} collective-permute-done((f32[256,256]{1,0:T(8,128)S(1)}, f32[256,256]{1,0:T(8,128)S(1)}, u32[]{:S(2)}, u32[]{:S(2)}) %collective-permute-start.33) | collective-permute-done | bytes 262176 | tf_op jit(solution)/shard_map/ppermute | solution.py:207
  189.8 1.2 maximum_select_fusion
  (164 shorter events, 22.2 us)
Async XLA Ops:
  0.6 11.4 %copy-start.49 = (f32[32]{0:T(128)S(1)}, f32[32]{0:T(128)}, u32[]{:S(2)}) copy-start(f32[32]{0:T(128)} %param.6) | copy-start | bytes 388
  0.6 21.1 %copy-start.48 = (s32[32,8,16]{0,2,1:T(8,128)S(1)}, s32[32,8,16]{0,2,1:T(8,128)}, u32[]{:S(2)}) copy-start(s32[32,8,16]{0,2,1:T(8,128)} %param.8) | copy-start | bytes 49156
  2.2 22.8 %collective-permute-start.2 = (f32[512,256]{1,0:T(8,128)S(1)}, f32[512,256]{1,0:T(8,128)}, u32[]{:S(2)}, u32[]{:S(2)}) collective-permute-start(f32[512,256]{1,0:T(8,128)S(1)} %get-tuple-element.102.refs_0_), channel_id=1, source_target_pairs={{0,4},{1,5},{2,6},{3,7},{8,12},{9,13},{10,14},{11,15},{16,20},{17,... | collective-permute-start | bytes 1572872 | tf_op jit(solution)/shard_map/ppermute | solution.py:316
  7.9 24.5 %collective-permute-start = (f32[512,256]{1,0:T(8,128)S(1)}, f32[512,256]{1,0:T(8,128)S(1)}, u32[]{:S(2)}, u32[]{:S(2)}) collective-permute-start(f32[512,256]{1,0:T(8,128)S(1)} %get-tuple-element.101), channel_id=1, source_target_pairs={{0,8},{8,0},{16,24},{24,16},{1,9},{9,1},{17,25},{25,17},{2,10},{10... | collective-permute-start | bytes 1572872 | tf_op jit(solution)/shard_map/ppermute | solution.py:207
  9.4 30.5 %collective-permute-start.1 = (f32[512,256]{1,0:T(8,128)S(1)}, f32[512,256]{1,0:T(8,128)S(1)}, u32[]{:S(2)}, u32[]{:S(2)}) collective-permute-start(f32[512,256]{1,0:T(8,128)S(1)} %get-tuple-element.100), channel_id=1, source_target_pairs={{0,16},{8,24},{16,0},{24,8},{1,17},{9,25},{17,1},{25,9},{2,18},{10... | collective-permute-start | bytes 1572872 | tf_op jit(solution)/shard_map/ppermute | solution.py:207
  32.4 11.5 %collective-permute-start.4 = (f32[512,256]{1,0:T(8,128)S(1)}, f32[512,256]{1,0:T(8,128)}, u32[]{:S(2)}, u32[]{:S(2)}) collective-permute-start(f32[512,256]{1,0:T(8,128)S(1)} %collective-permute-done.refs_1_), channel_id=1, source_target_pairs={{0,4},{1,5},{2,6},{3,7},{8,12},{9,13},{10,14},{11,15},{16,20},{17,... | collective-permute-start | bytes 1572872 | tf_op jit(solution)/shard_map/ppermute | solution.py:316
  34.5 9.4 %collective-permute-start.3 = (f32[256,256]{1,0:T(8,128)S(1)}, f32[256,256]{1,0:T(8,128)S(1)}, u32[]{:S(2)}, u32[]{:S(2)}) collective-permute-start(f32[256,256]{1,0:T(8,128)S(1)} %get-tuple-element.48), channel_id=1, source_target_pairs={{0,24},{8,16},{16,8},{24,0},{1,25},{9,17},{17,9},{25,1},{2,26},{10... | collective-permute-start | bytes 786440 | tf_op jit(solution)/shard_map/ppermute | solution.py:207
  38.4 43.3 %copy-start.33 = (f32[512]{0:T(512)S(1)}, f32[512]{0:T(512)}, u32[]{:S(2)}) copy-start(f32[512]{0:T(512)} %param.7) | copy-start | bytes 6148
  38.4 12.5 %collective-permute-start.14 = (f32[512,256]{1,0:T(8,128)S(1)}, f32[512,256]{1,0:T(8,128)}, u32[]{:S(2)}, u32[]{:S(2)}) collective-permute-start(f32[512,256]{1,0:T(8,128)S(1)} %broadcast_select_fusion.2.refs_5_), channel_id=1, source_target_pairs={{0,2},{1,3},{2,0},{3,1},{4,6},{5,7},{6,4},{7,5},{8,10},{9,11},{10,... | collective-permute-start | bytes 1572872 | tf_op jit(solution)/shard_map/ppermute | solution.py:207
  43.9 34.8 %copy-start.28 = (f32[256,256]{1,0:T(8,128)}, f32[256,256]{1,0:T(8,128)S(1)}, u32[]{:S(2)}) copy-start(f32[256,256]{1,0:T(8,128)S(1)} %collective-permute-done.3.refs_3_) | copy-start | bytes 786436
  43.9 13.8 %collective-permute-start.6 = (f32[512,256]{1,0:T(8,128)S(1)}, f32[512,256]{1,0:T(8,128)S(1)}, u32[]{:S(2)}, u32[]{:S(2)}) collective-permute-start(f32[512,256]{1,0:T(8,128)S(1)} %collective-permute-done.1.refs_2_), channel_id=1, source_target_pairs={{0,4},{1,5},{2,6},{3,7},{8,12},{9,13},{10,14},{11,15},{16,20},{17,... | collective-permute-start | bytes 1572872 | tf_op jit(solution)/shard_map/ppermute | solution.py:316
  48.5 35.8 %copy-start.24 = (f32[512,256]{1,0:T(8,128)}, f32[512,256]{1,0:T(8,128)S(1)}, u32[]{:S(2)}) copy-start(f32[512,256]{1,0:T(8,128)S(1)} %broadcast_select_fusion.1.refs_6_) | copy-start | bytes 1572868
  50.9 12.1 %collective-permute-start.15 = (f32[512,256]{1,0:T(8,128)S(1)}, f32[512,256]{1,0:T(8,128)S(1)}, u32[]{:S(2)}, u32[]{:S(2)}) collective-permute-start(f32[512,256]{1,0:T(8,128)S(1)} %broadcast_select_fusion.1.refs_6_), channel_id=1, source_target_pairs={{0,2},{1,3},{2,0},{3,1},{4,6},{5,7},{6,4},{7,5},{8,10},{9,11},{10,... | collective-permute-start | bytes 1572872 | tf_op jit(solution)/shard_map/ppermute | solution.py:207
  52.4 12.1 %collective-permute-start.5 = (f32[256,256]{1,0:T(8,128)}, f32[256,256]{1,0:T(8,128)S(1)}, u32[]{:S(2)}, u32[]{:S(2)}) collective-permute-start(f32[256,256]{1,0:T(8,128)} %get-tuple-element.50), channel_id=1, source_target_pairs={{0,24},{8,16},{16,8},{24,0},{1,25},{9,17},{17,9},{25,1},{2,26},{10... | collective-permute-start | bytes 786440 | tf_op jit(solution)/shard_map/ppermute | solution.py:207
  57.8 26.6 %copy-start.26 = (f32[512,256]{1,0:T(8,128)}, f32[512,256]{1,0:T(8,128)S(1)}, u32[]{:S(2)}) copy-start(f32[512,256]{1,0:T(8,128)S(1)} %broadcast_select_fusion.refs_7_) | copy-start | bytes 1572868
  63.0 18.7 %copy-start.34 = (f32[512,256]{1,0:T(8,128)}, f32[512,256]{1,0:T(8,128)S(1)}, u32[]{:S(2)}) copy-start(f32[512,256]{1,0:T(8,128)S(1)} %collective-permute-done.15.refs_1_) | copy-start | bytes 1572868
  63.0 12.0 %collective-permute-start.16 = (f32[512,256]{1,0:T(8,128)S(1)}, f32[512,256]{1,0:T(8,128)}, u32[]{:S(2)}, u32[]{:S(2)}) collective-permute-start(f32[512,256]{1,0:T(8,128)S(1)} %broadcast_select_fusion.refs_7_), channel_id=1, source_target_pairs={{0,2},{1,3},{2,0},{3,1},{4,6},{5,7},{6,4},{7,5},{8,10},{9,11},{10,... | collective-permute-start | bytes 1572872 | tf_op jit(solution)/shard_map/ppermute | solution.py:207
  64.5 17.2 %copy-start.30 = (f32[256,256]{1,0:T(8,128)}, f32[256,256]{1,0:T(8,128)S(1)}, u32[]{:S(2)}) copy-start(f32[256,256]{1,0:T(8,128)S(1)} %collective-permute-done.5.refs_4_) | copy-start | bytes 786436
  64.5 5.2 %collective-permute-start.7 = (f32[256,256]{1,0:T(8,128)S(1)}, f32[256,256]{1,0:T(8,128)S(1)}, u32[]{:S(2)}, u32[]{:S(2)}) collective-permute-start(f32[256,256]{1,0:T(8,128)S(1)} %collective-permute-done.3.refs_3_), channel_id=1, source_target_pairs={{0,4},{1,5},{2,6},{3,7},{8,12},{9,13},{10,14},{11,15},{16,20},{17,... | collective-permute-start | bytes 786440 | tf_op jit(solution)/shard_map/ppermute | solution.py:316
  65.8 16.1 %collective-permute-start.9 = (f32[512,256]{1,0:T(8,128)S(1)}, f32[512,256]{1,0:T(8,128)}, u32[]{:S(2)}, u32[]{:S(2)}) collective-permute-start(f32[512,256]{1,0:T(8,128)S(1)} %broadcast_select_fusion.2.refs_5_), channel_id=1, source_target_pairs={{0,1},{1,0},{2,3},{3,2},{4,5},{5,4},{6,7},{7,6},{8,9},{9,8},{10,11... | collective-permute-start | bytes 1572872 | tf_op jit(solution)/shard_map/ppermute | solution.py:207
  65.9 16.6 %collective-permute-start.10 = (f32[512,256]{1,0:T(8,128)S(1)}, f32[512,256]{1,0:T(8,128)}, u32[]{:S(2)}, u32[]{:S(2)}) collective-permute-start(f32[512,256]{1,0:T(8,128)S(1)} %broadcast_select_fusion.1.refs_6_), channel_id=1, source_target_pairs={{0,1},{1,0},{2,3},{3,2},{4,5},{5,4},{6,7},{7,6},{8,9},{9,8},{10,11... | collective-permute-start | bytes 1572872 | tf_op jit(solution)/shard_map/ppermute | solution.py:207
  66.4 16.6 %collective-permute-start.11 = (f32[512,256]{1,0:T(8,128)S(1)}, f32[512,256]{1,0:T(8,128)}, u32[]{:S(2)}, u32[]{:S(2)}) collective-permute-start(f32[512,256]{1,0:T(8,128)S(1)} %broadcast_select_fusion.refs_7_), channel_id=1, source_target_pairs={{0,1},{1,0},{2,3},{3,2},{4,5},{5,4},{6,7},{7,6},{8,9},{9,8},{10,11... | collective-permute-start | bytes 1572872 | tf_op jit(solution)/shard_map/ppermute | solution.py:207
  69.7 8.3 %collective-permute-start.8 = (f32[256,256]{1,0:T(8,128)S(1)}, f32[256,256]{1,0:T(8,128)S(1)}, u32[]{:S(2)}, u32[]{:S(2)}) collective-permute-start(f32[256,256]{1,0:T(8,128)S(1)} %collective-permute-done.5.refs_4_), channel_id=1, source_target_pairs={{0,4},{1,5},{2,6},{3,7},{8,12},{9,13},{10,14},{11,15},{16,20},{17,... | collective-permute-start | bytes 786440 | tf_op jit(solution)/shard_map/ppermute | solution.py:316
  75.0 6.7 %collective-permute-start.17 = (f32[256,256]{1,0:T(8,128)}, f32[256,256]{1,0:T(8,128)}, u32[]{:S(2)}, u32[]{:S(2)}) collective-permute-start(f32[256,256]{1,0:T(8,128)} %broadcast_select_fusion.4.refs_8_), channel_id=1, source_target_pairs={{0,2},{1,3},{2,0},{3,1},{4,6},{5,7},{6,4},{7,5},{8,10},{9,11},{10,... | collective-permute-start | bytes 786440 | tf_op jit(solution)/shard_map/ppermute | solution.py:207
  77.9 4.6 %collective-permute-start.12 = (f32[256,256]{1,0:T(8,128)}, f32[256,256]{1,0:T(8,128)}, u32[]{:S(2)}, u32[]{:S(2)}) collective-permute-start(f32[256,256]{1,0:T(8,128)} %broadcast_select_fusion.4.refs_8_), channel_id=1, source_target_pairs={{0,1},{1,0},{2,3},{3,2},{4,5},{5,4},{6,7},{7,6},{8,9},{9,8},{10,11... | collective-permute-start | bytes 786440 | tf_op jit(solution)/shard_map/ppermute | solution.py:207
  81.7 2.6 %collective-permute-start.13 = (f32[256,256]{1,0:T(8,128)}, f32[256,256]{1,0:T(8,128)}, u32[]{:S(2)}, u32[]{:S(2)}) collective-permute-start(f32[256,256]{1,0:T(8,128)} %broadcast_select_fusion.3.refs_9_), channel_id=1, source_target_pairs={{0,1},{1,0},{2,3},{3,2},{4,5},{5,4},{6,7},{7,6},{8,9},{9,8},{10,11... | collective-permute-start | bytes 786440 | tf_op jit(solution)/shard_map/ppermute | solution.py:207
  81.9 21.8 %collective-permute-start.19 = (f32[512,256]{1,0:T(8,128)}, f32[512,256]{1,0:T(8,128)}, u32[]{:S(2)}, u32[]{:S(2)}) collective-permute-start(f32[512,256]{1,0:T(8,128)} %collective-permute-done.14.refs_0_), channel_id=1, source_target_pairs={{0,1},{1,0},{2,3},{3,2},{4,5},{5,4},{6,7},{7,6},{8,9},{9,8},{10,11... | collective-permute-start | bytes 1572872 | tf_op jit(solution)/shard_map/ppermute | solution.py:207
  82.5 21.3 %collective-permute-start.20 = (f32[512,256]{1,0:T(8,128)}, f32[512,256]{1,0:T(8,128)}, u32[]{:S(2)}, u32[]{:S(2)}) collective-permute-start(f32[512,256]{1,0:T(8,128)} %copy-done.34), channel_id=1, source_target_pairs={{0,1},{1,0},{2,3},{3,2},{4,5},{5,4},{6,7},{7,6},{8,9},{9,8},{10,11... | collective-permute-start | bytes 1572872 | tf_op jit(solution)/shard_map/ppermute | solution.py:207
  82.6 22.4 %collective-permute-start.21 = (f32[512,256]{1,0:T(8,128)}, f32[512,256]{1,0:T(8,128)}, u32[]{:S(2)}, u32[]{:S(2)}) collective-permute-start(f32[512,256]{1,0:T(8,128)} %collective-permute-done.16.refs_2_), channel_id=1, source_target_pairs={{0,1},{1,0},{2,3},{3,2},{4,5},{5,4},{6,7},{7,6},{8,9},{9,8},{10,11... | collective-permute-start | bytes 1572872 | tf_op jit(solution)/shard_map/ppermute | solution.py:207
  83.0 20.2 %collective-permute-start.18 = (f32[256,256]{1,0:T(8,128)}, f32[256,256]{1,0:T(8,128)}, u32[]{:S(2)}, u32[]{:S(2)}) collective-permute-start(f32[256,256]{1,0:T(8,128)} %broadcast_select_fusion.3.refs_9_), channel_id=1, source_target_pairs={{0,2},{1,3},{2,0},{3,1},{4,6},{5,7},{6,4},{7,5},{8,10},{9,11},{10,... | collective-permute-start | bytes 786440 | tf_op jit(solution)/shard_map/ppermute | solution.py:207
  103.2 14.8 %copy-start.22 = (f32[512,256]{1,0:T(8,128)}, f32[512,256]{1,0:T(8,128)S(1)}, u32[]{:S(2)}) copy-start(f32[512,256]{1,0:T(8,128)S(1)} %get-tuple-element.68.refs_0_) | copy-start | bytes 1572868
  103.2 1.7 collective-permute-start.22
  103.2 2.1 %collective-permute-start.23 = (f32[256,256]{1,0:T(8,128)}, f32[256,256]{1,0:T(8,128)S(1)}, u32[]{:S(2)}, u32[]{:S(2)}) collective-permute-start(f32[256,256]{1,0:T(8,128)} %collective-permute-done.18.refs_4_), channel_id=1, source_target_pairs={{0,1},{1,0},{2,3},{3,2},{4,5},{5,4},{6,7},{7,6},{8,9},{9,8},{10,11... | collective-permute-start | bytes 786440 | tf_op jit(solution)/shard_map/ppermute | solution.py:207
  107.2 1.2 copy-start.39
  108.5 1.2 copy-start.41
  110.7 8.4 %copy-start.19 = (f32[512,512]{1,0:T(8,128)S(1)}, f32[512,512]{1,0:T(8,128)}, u32[]{:S(2)}) copy-start(f32[512,512]{1,0:T(8,128)} %copy-done.18) | copy-start | bytes 3145732
  119.0 2.1 %copy-start = (bf16[512,512]{1,0:T(8,128)(2,1)}, bf16[512,512]{1,0:T(8,128)(2,1)S(1)}, u32[]{:S(2)}) copy-start(bf16[512,512]{1,0:T(8,128)(2,1)S(1)} %get-tuple-element.75.refs_3_.refs_9_) | copy-start | bytes 1572868
  119.0 2.1 %copy-start.2 = (bf16[512,512]{1,0:T(8,128)(2,1)}, bf16[512,512]{1,0:T(8,128)(2,1)S(1)}, u32[]{:S(2)}) copy-start(bf16[512,512]{1,0:T(8,128)(2,1)S(1)} %get-tuple-element.76.refs_4_.refs_12_) | copy-start | bytes 1572868
  119.0 2.1 %copy-start.4 = (bf16[512,512]{1,0:T(8,128)(2,1)}, bf16[512,512]{1,0:T(8,128)(2,1)S(1)}, u32[]{:S(2)}) copy-start(bf16[512,512]{1,0:T(8,128)(2,1)S(1)} %get-tuple-element.77.refs_5_.refs_13_) | copy-start | bytes 1572868
  119.0 2.1 %copy-start.6 = (bf16[512,512]{1,0:T(8,128)(2,1)}, bf16[512,512]{1,0:T(8,128)(2,1)S(1)}, u32[]{:S(2)}) copy-start(bf16[512,512]{1,0:T(8,128)(2,1)S(1)} %get-tuple-element.78.refs_6_.refs_14_) | copy-start | bytes 1572868
  119.0 2.2 %copy-start.8 = (bf16[512,512]{1,0:T(8,128)(2,1)}, bf16[512,512]{1,0:T(8,128)(2,1)S(1)}, u32[]{:S(2)}) copy-start(bf16[512,512]{1,0:T(8,128)(2,1)S(1)} %get-tuple-element.79.refs_7_.refs_15_) | copy-start | bytes 1572868
  119.0 2.2 %copy-start.10 = (bf16[512,1024]{1,0:T(8,128)(2,1)}, bf16[512,1024]{1,0:T(8,128)(2,1)S(1)}, u32[]{:S(2)}) copy-start(bf16[512,1024]{1,0:T(8,128)(2,1)S(1)} %get-tuple-element.81.refs_4_) | copy-start | bytes 3145732
  119.1 2.2 %copy-start.12 = (bf16[512,1024]{1,0:T(8,128)(2,1)}, bf16[512,1024]{1,0:T(8,128)(2,1)S(1)}, u32[]{:S(2)}) copy-start(bf16[512,1024]{1,0:T(8,128)(2,1)S(1)} %get-tuple-element.82.refs_5_) | copy-start | bytes 3145732
  119.1 2.5 %copy-start.14 = (bf16[512,1024]{1,0:T(8,128)(2,1)}, bf16[512,1024]{1,0:T(8,128)(2,1)S(1)}, u32[]{:S(2)}) copy-start(bf16[512,1024]{1,0:T(8,128)(2,1)S(1)} %get-tuple-element.83.refs_10_) | copy-start | bytes 3145732
  119.1 3.3 %copy-start.36 = (f32[512,256]{1,0:T(8,128)}, f32[512,256]{1,0:T(8,128)S(1)}, u32[]{:S(2)}) copy-start(f32[512,256]{1,0:T(8,128)S(1)} %get-tuple-element.67) | copy-start | bytes 1572868
  122.4 2.3 %collective-permute-start.25 = (f32[256,512]{1,0:T(8,128)}, f32[256,512]{1,0:T(8,128)}, u32[]{:S(2)}, u32[]{:S(2)}) collective-permute-start(f32[256,512]{1,0:T(8,128)} %constant_dynamic-slice_fusion.3), channel_id=1, source_target_pairs={{0,1},{1,0},{2,3},{3,2},{4,5},{5,4},{6,7},{7,6},{8,9},{9,8},{10,11... | collective-permute-start | bytes 1572872 | tf_op jit(solution)/shard_map/ppermute | solution.py:207
  122.6 3.2 %copy-start.11 = (bf16[512,1024]{1,0:T(8,128)(2,1)S(1)}, bf16[512,1024]{1,0:T(8,128)(2,1)}, u32[]{:S(2)}) copy-start(bf16[512,1024]{1,0:T(8,128)(2,1)} %copy-done.10) | copy-start | bytes 3145732
  122.6 27.5 %collective-permute-start.24 = (f32[512,256]{1,0:T(8,128)}, f32[512,256]{1,0:T(8,128)}, u32[]{:S(2)}, u32[]{:S(2)}) collective-permute-start(f32[512,256]{1,0:T(8,128)} %copy-done.36), channel_id=1, source_target_pairs={{0,16},{8,24},{16,0},{24,8},{1,17},{9,25},{17,1},{25,9},{2,18},{10... | collective-permute-start | bytes 1572872 | tf_op jit(solution)/shard_map/ppermute | solution.py:207
  125.8 14.5 %copy-start.45 = (f32[256,512]{1,0:T(8,128)}, f32[256,512]{1,0:T(8,128)S(1)}, u32[]{:S(2)}) copy-start(f32[256,512]{1,0:T(8,128)S(1)} %dynamic-slice_add_fusion) | copy-start | bytes 1572868
  125.8 1.2 copy-start.1
  140.3 26.6 %collective-permute-start.26 = (f32[512,256]{1,0:T(8,128)S(1)}, f32[512,256]{1,0:T(8,128)S(1)}, u32[]{:S(2)}, u32[]{:S(2)}) collective-permute-start(f32[512,256]{1,0:T(8,128)S(1)} %get-tuple-element.85), channel_id=1, source_target_pairs={{0,8},{8,0},{16,24},{24,16},{1,9},{9,1},{17,25},{25,17},{2,10},{10... | collective-permute-start | bytes 1572872 | tf_op jit(solution)/shard_map/ppermute | solution.py:207
  140.3 6.4 %collective-permute-start.27 = (f32[64,512]{1,0:T(8,128)S(1)}, f32[64,512]{1,0:T(8,128)S(1)}, u32[]{:S(2)}, u32[]{:S(2)}) collective-permute-start(f32[64,512]{1,0:T(8,128)S(1)} %get-tuple-element.103), channel_id=1, source_target_pairs={{0,2},{1,3},{2,0},{3,1},{4,6},{5,7},{6,4},{7,5},{8,10},{9,11},{10,... | collective-permute-start | bytes 393224 | tf_op jit(solution)/shard_map/ppermute | solution.py:207
  141.1 8.1 %collective-permute-start.28 = (f32[64,512]{1,0:T(8,128)S(1)}, f32[64,512]{1,0:T(8,128)S(1)}, u32[]{:S(2)}, u32[]{:S(2)}) collective-permute-start(f32[64,512]{1,0:T(8,128)S(1)} %get-tuple-element.105), channel_id=1, source_target_pairs={{0,4},{1,5},{2,6},{3,7},{4,0},{5,1},{6,2},{7,3},{8,12},{9,13},{10,... | collective-permute-start | bytes 393224 | tf_op jit(solution)/shard_map/ppermute | solution.py:207
  141.1 8.1 %collective-permute-start.29 = (f32[64,512]{1,0:T(8,128)S(1)}, f32[64,512]{1,0:T(8,128)S(1)}, u32[]{:S(2)}, u32[]{:S(2)}) collective-permute-start(f32[64,512]{1,0:T(8,128)S(1)} %get-tuple-element.104), channel_id=1, source_target_pairs={{0,6},{1,7},{2,4},{3,5},{4,2},{5,3},{6,0},{7,1},{8,14},{9,15},{10,... | collective-permute-start | bytes 393224 | tf_op jit(solution)/shard_map/ppermute | solution.py:207
  150.1 16.8 %collective-permute-start.31 = (f32[64,512]{1,0:T(8,128)S(1)}, f32[64,512]{1,0:T(8,128)S(1)}, u32[]{:S(2)}, u32[]{:S(2)}) collective-permute-start(f32[64,512]{1,0:T(8,128)S(1)} %add_add_fusion), channel_id=1, source_target_pairs={{0,8},{8,0},{16,24},{24,16},{1,9},{9,1},{17,25},{25,17},{2,10},{10... | collective-permute-start | bytes 393224 | tf_op jit(solution)/shard_map/ppermute | solution.py:207
  151.9 24.8 %collective-permute-start.30 = (f32[256,256]{1,0:T(8,128)}, f32[256,256]{1,0:T(8,128)}, u32[]{:S(2)}, u32[]{:S(2)}) collective-permute-start(f32[256,256]{1,0:T(8,128)} %copy-done.37), channel_id=1, source_target_pairs={{0,24},{8,16},{16,8},{24,0},{1,25},{9,17},{17,9},{25,1},{2,26},{10... | collective-permute-start | bytes 786440 | tf_op jit(solution)/shard_map/ppermute | solution.py:207
  167.7 9.0 %collective-permute-start.32 = (f32[64,512]{1,0:T(8,128)S(1)}, f32[64,512]{1,0:T(8,128)S(1)}, u32[]{:S(2)}, u32[]{:S(2)}) collective-permute-start(f32[64,512]{1,0:T(8,128)S(1)} %add.177), channel_id=1, source_target_pairs={{0,16},{8,24},{16,0},{24,8},{1,17},{9,25},{17,1},{25,9},{2,18},{10... | collective-permute-start | bytes 393224 | tf_op jit(solution)/shard_map/ppermute | solution.py:207
  168.3 12.0 %copy-start.47 = (f32[512,256]{1,0:T(8,128)S(1)}, f32[512,256]{1,0:T(8,128)}, u32[]{:S(2)}) copy-start(f32[512,256]{1,0:T(8,128)} %copy-done.46) | copy-start | bytes 1572868
  176.8 6.1 %collective-permute-start.34 = (f32[64,512]{1,0:T(8,128)S(1)}, f32[64,512]{1,0:T(8,128)S(1)}, u32[]{:S(2)}, u32[]{:S(2)}) collective-permute-start(f32[64,512]{1,0:T(8,128)S(1)} %add.178), channel_id=1, source_target_pairs={{0,2},{1,3},{2,0},{3,1},{4,6},{5,7},{6,4},{7,5},{8,10},{9,11},{10,... | collective-permute-start | bytes 393224 | tf_op jit(solution)/shard_map/ppermute | solution.py:207
  178.0 8.0 %collective-permute-start.35 = (f32[64,512]{1,0:T(8,128)S(1)}, f32[64,512]{1,0:T(8,128)S(1)}, u32[]{:S(2)}, u32[]{:S(2)}) collective-permute-start(f32[64,512]{1,0:T(8,128)S(1)} %add.178), channel_id=1, source_target_pairs={{0,4},{1,5},{2,6},{3,7},{4,0},{5,1},{6,2},{7,3},{8,12},{9,13},{10,... | collective-permute-start | bytes 393224 | tf_op jit(solution)/shard_map/ppermute | solution.py:207
  178.0 8.0 %collective-permute-start.36 = (f32[64,512]{1,0:T(8,128)S(1)}, f32[64,512]{1,0:T(8,128)S(1)}, u32[]{:S(2)}, u32[]{:S(2)}) collective-permute-start(f32[64,512]{1,0:T(8,128)S(1)} %add.178), channel_id=1, source_target_pairs={{0,6},{1,7},{2,4},{3,5},{4,2},{5,3},{6,0},{7,1},{8,14},{9,15},{10,... | collective-permute-start | bytes 393224 | tf_op jit(solution)/shard_map/ppermute | solution.py:207
  180.4 9.4 %collective-permute-start.33 = (f32[256,256]{1,0:T(8,128)S(1)}, f32[256,256]{1,0:T(8,128)S(1)}, u32[]{:S(2)}, u32[]{:S(2)}) collective-permute-start(f32[256,256]{1,0:T(8,128)S(1)} %get-tuple-element.91), channel_id=1, source_target_pairs={{0,24},{8,16},{16,8},{24,0},{1,25},{9,17},{17,9},{25,1},{2,26},{10... | collective-permute-start | bytes 786440 | tf_op jit(solution)/shard_map/ppermute | solution.py:207
  186.1 3.7 %collective-permute-start.37 = (f32[256,512]{1,0:T(8,128)S(1)}, f32[256,512]{1,0:T(8,128)S(1)}, u32[]{:S(2)}, u32[]{:S(2)}) collective-permute-start(f32[256,512]{1,0:T(8,128)S(1)} %maximum_select_fusion.1), channel_id=1, source_target_pairs={{0,1},{1,0},{2,3},{3,2},{4,5},{5,4},{6,7},{7,6},{8,9},{9,8},{10,11... | collective-permute-start | bytes 1572872 | tf_op jit(solution)/shard_map/ppermute | solution.py:207
  189.8 1.7 copy-start.44
  (24 other events, 23.8 us)

commit v3 on v2

v3 whole, which is shorter than its diff:
```python
import functools

import jax
import jax.numpy as jnp
from jax import lax
from jax.experimental import pallas as pl
from jax.experimental.pallas import tpu as pltpu
from jax.sharding import PartitionSpec as P

BLOCK = 64
NPANEL = 4
TILE = 256
VMEM_LIMIT = 60 * 1024 * 1024
NT = (((1,), (1,)), ((), ()))


def staged(kernel, smalls, bigs, count, *refs):
    small, refs = refs[:smalls], refs[smalls:]
    sources, targets, scratch = refs[:bigs], refs[bigs : bigs + count], refs[bigs + count : -2]
    in_sem, out_sem = refs[-2:]
    held, made, own = scratch[:bigs], scratch[bigs : bigs + count], scratch[bigs + count :]
    loads = [
        pltpu.make_async_copy(source, target, in_sem.at[at])
        for at, (source, target) in enumerate(zip(sources, held))
    ]
    stores = [
        pltpu.make_async_copy(source, target, out_sem.at[at])
        for at, (source, target) in enumerate(zip(made, targets))
    ]
    for load in loads:
        load.start()
    kernel(small, held, made, own, [load.wait for load in loads], [store.start for store in stores])
    for store in stores:
        store.wait()


def call(kernel, name, outs, small, big, flops, scratch):
    size = sum(at.size * at.dtype.itemsize for at in [*outs, *big])
    any_space = pl.BlockSpec(memory_space=pl.ANY)
    specs = [pl.BlockSpec(memory_space=pltpu.SMEM)]
    specs += [pl.BlockSpec(memory_space=pltpu.VMEM)] * (len(small) - 1)
    buffers = [pltpu.VMEM(at.shape, at.dtype) for at in [*big, *outs]]
    sems = [pltpu.SemaphoreType.DMA((len(big),)), pltpu.SemaphoreType.DMA((len(outs),))]
    return pl.pallas_call(
        functools.partial(staged, kernel, len(small), len(big), len(outs)),
        out_shape=outs,
        in_specs=specs + [any_space] * len(big),
        out_specs=[any_space] * len(outs),
        scratch_shapes=[*buffers, *scratch, *sems],
        compiler_params=pltpu.CompilerParams(vmem_limit_bytes=VMEM_LIMIT),
        cost_estimate=pl.CostEstimate(flops=flops, bytes_accessed=size, transcendentals=0),
        name=name,
    )(*small, *big)


def shape(*sizes, kind=jnp.float32):
    return jax.ShapeDtypeStruct(sizes, kind)


def halves(value):
    high = value.astype(jnp.bfloat16)
    return high, (value - high.astype(jnp.float32)).astype(jnp.bfloat16)


def dot(left, right):
    return jnp.dot(left, right, preferred_element_type=jnp.float32)


def dot_nt(left, right):
    return lax.dot_general(left, right, NT, preferred_element_type=jnp.float32)


def split_rows(cuts, pieces, waits, mask, high, low):
    for (part, first, count), piece, wait in zip(cuts, pieces, waits):
        wait()
        width = piece.shape[1]
        cols = slice(part * width, (part + 1) * width)
        for start in range(0, count, BLOCK):
            at = first + start
            kept = mask[at // BLOCK : at // BLOCK + 1, cols]
            value = piece[start : start + BLOCK, :] * kept
            high[at : at + BLOCK, cols], low[at : at + BLOCK, cols] = halves(value)


def amplitudes(energy, live, vir_col, vir_row, own, panel, amp, a_parts, w_parts):
    nvir = amp.shape[0]
    for start in range(0, nvir, TILE):
        cols = slice(start, start + TILE)
        cross = dot_nt(own[0][...], panel[0][cols, :])
        cross += dot_nt(own[0][...], panel[1][cols, :])
        cross += dot_nt(own[1][...], panel[0][cols, :])
        value = cross / (energy - vir_col[...] - vir_row[:, cols]) * live
        amp[:, cols] = value
        a_parts[0][:, cols], a_parts[1][:, cols] = halves(value)
    for above in range(0, nvir, TILE):
        rows = slice(above, above + TILE)
        for start in range(0, nvir, TILE):
            cols = slice(start, start + TILE)
            value = 2.0 * amp[rows, cols] - amp[cols, rows].T
            w_parts[0][rows, cols], w_parts[1][rows, cols] = halves(value)


def respond(rows, w_parts, panel, cols):
    value = dot(w_parts[0][rows, :], panel[0][:, cols])
    value += dot(w_parts[0][rows, :], panel[1][:, cols])
    return value + dot(w_parts[1][rows, :], panel[0][:, cols])


def density_tile(cols, w_parts, a_parts):
    value = dot_nt(w_parts[0][...], a_parts[0][cols, :])
    value += dot_nt(w_parts[0][...], a_parts[1][cols, :])
    return value + dot_nt(w_parts[1][...], a_parts[0][cols, :])


def early_kernel(cuts, small, held, made, own_scratch, wait, give):
    scalars, vir_col, vir_row, masks = small
    count = len(cuts)
    own_high, own_low, density, *slices = made
    m_high, m_low, amp, a_high, a_low, w_high, w_low = own_scratch
    split_rows(cuts, held[:count], wait[:count], masks.at[0], own_high, own_low)
    give[0]()
    give[1]()
    nvir = amp.shape[0]
    panel, a_parts, w_parts = (m_high, m_low), (a_high, a_low), (w_high, w_low)
    for turn in range(2):
        where = slice((1 + turn) * count, (2 + turn) * count)
        split_rows(cuts, held[where], wait[where], masks.at[1 + turn], m_high, m_low)
        amplitudes(
            scalars[2 * turn], scalars[2 * turn + 1], vir_col, vir_row,
            (own_high, own_low), panel, amp, a_parts, w_parts,
        )
        for start in range(0, nvir, TILE):
            cols = slice(start, start + TILE)
            value = density_tile(cols, w_parts, a_parts)
            density[:, cols] = value if turn == 0 else density[:, cols] + value
        if turn:
            give[2]()
        for part, piece in enumerate(slices):
            width = piece.shape[1]
            cols = slice(part * width, (part + 1) * width)
            value = respond(slice(0, nvir), w_parts, panel, cols)
            piece[...] = value if turn == 0 else piece[...] + value
            if turn:
                give[3 + part]()


def squares(nvir, naux):
    half = jnp.bfloat16
    return [pltpu.VMEM((nvir, naux), half)] * 2, [pltpu.VMEM((nvir, nvir), half)] * 4


def early(cuts, scalars, virtual, masks, own, near, twin):
    nvir, width = own[0].shape
    naux = masks.shape[2]
    parts = naux // width
    outs = [shape(nvir, naux, kind=jnp.bfloat16)] * 2 + [shape(nvir, nvir)]
    outs += [shape(nvir, width)] * parts
    wide, square = squares(nvir, naux)
    small = [scalars, virtual[:, None], virtual[None, :], masks]
    flops = 2 * 3 * 2 * nvir * nvir * (2 * naux + nvir)
    kernel = functools.partial(early_kernel, cuts)
    scratch = [*wide, pltpu.VMEM((nvir, nvir), jnp.float32), *square]
    outs = call(kernel, "early", outs, small, [*own, *near, *twin], flops, scratch)
    return outs[:2], outs[2], list(outs[3:])


def late_kernel(cuts, wanted, scale, small, held, made, own_scratch, wait, give):
    scalars, vir_col, vir_row, masks = small
    count = len(cuts)
    amp, panels = own_scratch[0], (own_scratch[1:7], own_scratch[7:])
    wait[0]()
    wait[1]()
    for turn, (m_high, m_low, a_high, a_low, w_high, w_low) in enumerate(panels):
        where = slice(2 + turn * count, 2 + (1 + turn) * count)
        split_rows(cuts, held[where], wait[where], masks.at[turn], m_high, m_low)
        amplitudes(
            scalars[2 * turn], scalars[2 * turn + 1], vir_col, vir_row,
            held[:2], (m_high, m_low), amp, (a_high, a_low), (w_high, w_low),
        )
    density, *slices = held[2 + 2 * count :]
    total, *pieces = made
    for ready in wait[2 + 2 * count :]:
        ready()
    for start in range(0, density.shape[0], TILE):
        cols = slice(start, start + TILE)
        value = density[:, cols]
        for _, _, a_high, a_low, w_high, w_low in panels:
            value += density_tile(cols, (w_high, w_low), (a_high, a_low))
        total[:, cols] = value * scale
    give[0]()
    for at, ((part, first, height), piece) in enumerate(zip(wanted, pieces)):
        rows = slice(first, first + height)
        width = piece.shape[1]
        cols = slice(part * width, (part + 1) * width)
        value = slices[part][rows, :]
        for m_high, m_low, _, _, w_high, w_low in panels:
            value += respond(rows, (w_high, w_low), (m_high, m_low), cols)
        piece[...] = value
        give[1 + at]()


def late(cuts, wanted, scale, scalars, virtual, masks, own, far, twin, density, slices):
    nvir, naux = own[0].shape
    width = slices[0].shape[1]
    outs = [shape(nvir, nvir)] + [shape(height, width) for _, _, height in wanted]
    wide, square = squares(nvir, naux)
    small = [scalars, virtual[:, None], virtual[None, :], masks]
    flops = 2 * 3 * 2 * nvir * nvir * (2 * naux + nvir)
    kernel = functools.partial(late_kernel, cuts, wanted, scale)
    scratch = [pltpu.VMEM((nvir, nvir), jnp.float32), *wide, *square, *wide, *square]
    big = [*own, *far, *twin, density, *slices]
    outs = call(kernel, "late", outs, small, big, flops, scratch)
    return outs[0], list(outs[1:])


def exchange(value, axis, bit):
    size = lax.axis_size(axis)
    return lax.ppermute(value, axis, [(at, at ^ bit) for at in range(size)])


def after(value, *others):
    return lax.optimization_barrier((value, *others))[0]


def bits(axis):
    size = lax.axis_size(axis)
    return [1 << at for at in range(size.bit_length() - 1)]


def scatter_chip(value):
    half = value.shape[0] // 2
    side = lax.axis_index("col") % 2
    kept = lax.dynamic_slice_in_dim(value, side * half, half, 0)
    sent = lax.dynamic_slice_in_dim(value, (1 - side) * half, half, 0)
    return kept + exchange(sent, "col", 1)


def scatter_plane(value):
    place = lax.axis_index("col") // 2
    chips = lax.axis_size("col") // 2
    count = value.shape[0] // chips
    total = lax.dynamic_slice_in_dim(value, place * count, count, 0)
    for turn in range(1, chips):
        sent = lax.dynamic_slice_in_dim(value, (place ^ turn) * count, count, 0)
        total = total + exchange(sent, "col", 2 * turn)
    return total


def joined(terms, place):
    if len(terms) == 1:
        return terms[0]
    half = len(terms) // 2
    low, high = joined(terms[:half], place), joined(terms[half:], place)
    side = (place // half) % 2
    return jnp.where(side == 0, jnp.concatenate([low, high]), jnp.concatenate([high, low]))


def gather_plane(value, other):
    col = lax.axis_index("col")
    turns = range(1, lax.axis_size("col") // 2)
    terms = [value] + [exchange(value, "col", 2 * turn) for turn in turns]
    value = after(joined(terms, col // 2), other)
    return joined([value, exchange(value, "col", 1)], col)


def cut_list(nvir, row_count):
    cuts = [(part, 0, nvir) for part in range(row_count - 1)]
    return cuts + [(row_count - 1, at, nvir // 2) for at in (0, nvir // 2)]


def on_device(three_index, occ_energy, vir_energy, block_mask, pair_list):
    row = lax.axis_index("row")
    col = lax.axis_index("col")
    row_count = lax.axis_size("row")
    col_count = lax.axis_size("col")
    position = col % NPANEL
    group = col // NPANEL
    groups = col_count // NPANEL
    nvir = three_index.shape[1]
    cuts = cut_list(nvir, row_count)

    own_orbital = col * row_count + row
    panels = [position ^ turn for turn in range(NPANEL)]
    orbitals = jnp.stack([own_orbital] + [at * row_count + row for at in panels])
    kept = block_mask[orbitals].reshape(NPANEL + 1, block_mask.shape[1], row_count, -1)
    kept = kept[:, :, row ^ jnp.arange(row_count), :].reshape(NPANEL + 1, kept.shape[1], -1)
    masks = jnp.repeat(kept.astype(jnp.float32), BLOCK, axis=-1)
    lists = pair_list[row]
    scalars = []
    for turn in range(NPANEL):
        live = jnp.any(lists == panels[turn]).astype(jnp.float32)
        scalars += [occ_energy[own_orbital] + occ_energy[orbitals[1 + turn]], live]
    small = masks[:3], masks[3:], jnp.stack(scalars[:4]), jnp.stack(scalars[4:])

    own, came, near, far = [], [], [], []

    def receive(at):
        part, first, count = cuts[at]
        rows = lax.dynamic_index_in_dim(three_index, row ^ part, 0, keepdims=False)
        rows = rows[first : first + count]
        if part == row_count - 1:
            rows = after(rows, near[0 if first == 0 else 1])
        elif part > 1:
            rows = after(rows, *small[2:])
        own.append(exchange(rows, "row", part) if part else rows)

    for at in range(len(cuts)):
        while len(own) < min(at + 2, len(cuts)) and (at or len(own) < row_count - 1):
            receive(len(own))
        rows = own[at]
        if at:
            rows = after(rows, came[-1])
        if at > 1:
            rows = after(rows, *own[at + 1 : at + 2])
        reach = 1
        while reach < groups:
            span = min(reach, groups - reach) * NPANEL
            links = [(one, one + reach * NPANEL) for one in range(span)]
            got = lax.ppermute(rows, "col", links)
            rows = jnp.where((group >= reach) & (group < 2 * reach), got, rows)
            reach *= 2
        came.append(got)
        near.append(rows)
        sent = after(rows, far[-1]) if at else after(rows, *small)
        far.append(exchange(sent, "col", 2))

    near_twin = [exchange(piece, "col", 1) for piece in near]
    far_twin = [exchange(piece, "col", 1) for piece in far]
    halved, density, slices = early(
        cuts, after(small[2], far[-1]), vir_energy, small[0], own, near, near_twin
    )

    middle, edge, half = row_count // 2, row_count - 1, nvir // 2
    others = [(at, 0, nvir) for at in range(1, edge) if at != middle]
    wanted = [(middle, 0, half), (middle, half, half), *others]
    wanted += [(edge, 0, half), (edge, half, half), (0, 0, nvir)]
    scale = 1.0 / (row_count * col_count)
    total, pieces = late(
        cuts, wanted, scale, small[3], vir_energy, small[1], halved, far, far_twin,
        density, slices,
    )
    ends = [exchange(piece, "row", cut[0]) for cut, piece in zip(wanted[:-3], pieces)]
    total = after(scatter_plane(scatter_chip(total)), ends[0])
    for bit in bits("row")[:-1]:
        total = total + exchange(total, "row", bit)
    ends.append(exchange(after(pieces[-3], total), "row", edge))
    total = after(total, *ends[1:-1])
    total = total + exchange(total, "row", bits("row")[-1])
    ends.append(exchange(after(pieces[-2], total), "row", edge))
    total = gather_plane(total, ends[-2])
    ends.append(pieces[-1])

    returned = jnp.zeros_like(three_index)
    for (part, first, _), piece in zip(wanted, ends):
        returned = lax.dynamic_update_slice(returned, piece[None], (row ^ part, first, 0))
    return returned, total


def solution(mesh):
    placed = (P("col", None, "row"), P(), P(), P(), P("col", None))
    return jax.shard_map(
        on_device,
        mesh=mesh,
        in_specs=placed,
        out_specs=(P("col", None, "row"), P()),
        check_vma=False,
    )
```

time: 193 us -> 197 us (1.021)
  the two profiles are of different devices: /device:TPU:0 before, /device:TPU:16 now
where the time goes in v3:
time: 197 us
  waiting for transfers between devices  105 us (53%)
  starting transfers between devices  37.5 us (19%)
  Pallas kernels  28.8 us (15%)
  local copies, waits for them, and re-layouts  11.3 us (6%)
  between operations  8.96 us (5%)
  other arithmetic  5.42 us (3%)
    ppermute x34, waiting for transfers between devices, exchange(): return lax.ppermute(value, axis, [(at, at ^ bit) for at in range(size)])  92 us
    pallas_call x2, Pallas kernels, call(): pl.pallas_call(functools.partial(staged, kernel, len(small), len(big), le...  28.8 us
    ppermute x34, starting transfers between devices, exchange(): return lax.ppermute(value, axis, [(at, at ^ bit) for at in range(size)])  24.5 us
    ppermute x5, starting transfers between devices, on_device(): got = lax.ppermute(rows, 'col', links)  13 us
    ppermute x5, waiting for transfers between devices, on_device(): got = lax.ppermute(rows, 'col', links)  12.8 us
  transfers between devices with their start and end apart: 39, of which 17 were waited for; matrix products, arithmetic and copies ran while one was open for 5% of the time, Pallas kernels for 7%

profile of v3, /device:TPU:16, one launch (start us, length us, event | category | flops | bytes accessed | tf_op | source)
XLA Modules:
  0.0 196.8 jit_solution(11058315534853390237)
XLA Ops:
  0.7 1.5 dynamic-slice_bitcast_fusion
  2.2 3.5 %collective-permute-start.1 = (f32[512,256]{1,0:T(8,128)S(1)}, f32[512,256]{1,0:T(8,128)S(1)}, u32[]{:S(2)}, u32[]{:S(2)}) collective-permute-start(f32[512,256]{1,0:T(8,128)S(1)} %get-tuple-element.76.refs_4_), channel_id=1, source_target_pairs={{0,4},{1,5},{2,6},{3,7},{8,12},{9,13},{10,14},{11,15},{16,20},{17,... | collective-permute-start | bytes 1572872 | tf_op jit(solution)/shard_map/ppermute | solution.py:319
  5.6 1.6 collective-permute-start
  7.3 0.7 fusion.2
  10.5 1.4 compare_reduce_fusion.1
  17.0 0.6 pad_maximum_fusion.1.refs_0_
  17.6 0.6 pad_maximum_fusion.refs_0_
  18.2 0.3 collective-permute-start.5
  18.8 0.6 gather_fusion
  19.4 0.6 gather_fusion.1
  20.0 1.9 dynamic-slice_bitcast_fusion.3
  21.9 2.1 %collective-permute-start.2 = (f32[512,256]{1,0:T(8,128)S(1)}, f32[512,256]{1,0:T(8,128)}, u32[]{:S(2)}, u32[]{:S(2)}) collective-permute-start(f32[512,256]{1,0:T(8,128)S(1)} %collective-permute-done.refs_5_), channel_id=1, source_target_pairs={{0,4},{1,5},{2,6},{3,7},{8,12},{9,13},{10,14},{11,15},{16,20},{17,... | collective-permute-start | bytes 1572872 | tf_op jit(solution)/shard_map/ppermute | solution.py:319
  24.1 1.6 collective-permute-start.4
  25.9 0.1 broadcast_in_dim.40
  26.0 0.8 slice.41.refs_3_
  26.9 0.7 slice.34.refs_3_
  27.6 1.5 collective-permute-start.9
  29.1 17.1 %collective-permute-done.5.refs_6_ = f32[512,256]{1,0:T(8,128)S(1)} collective-permute-done((f32[512,256]{1,0:T(8,128)S(1)}, f32[512,256]{1,0:T(8,128)S(1)}, u32[]{:S(2)}, u32[]{:S(2)}) %collective-permute-start.5) | collective-permute-done | bytes 524320 | tf_op jit(solution)/shard_map/ppermute | solution.py:218
  46.3 7.4 %collective-permute-done.4.refs_7_ = f32[256,256]{1,0:T(8,128)S(1)} collective-permute-done((f32[256,256]{1,0:T(8,128)}, f32[256,256]{1,0:T(8,128)S(1)}, u32[]{:S(2)}, u32[]{:S(2)}) %collective-permute-start.4) | collective-permute-done | bytes 262176 | tf_op jit(solution)/shard_map/ppermute | solution.py:218
  53.7 1.6 collective-permute-start.6
  55.4 4.1 %collective-permute-start.10 = (f32[512,256]{1,0:T(8,128)S(1)}, f32[512,256]{1,0:T(8,128)S(1)}, u32[]{:S(2)}, u32[]{:S(2)}) collective-permute-start(f32[512,256]{1,0:T(8,128)S(1)} %broadcast_select_fusion.2.refs_10_), channel_id=1, source_target_pairs={{0,2},{1,3},{2,0},{3,1},{4,6},{5,7},{6,4},{7,5},{8,10},{9,11},{10,... | collective-permute-start | bytes 1572872 | tf_op jit(solution)/shard_map/ppermute | solution.py:218
  59.5 6.0 %collective-permute-done.6 = f32[512,256]{1,0:T(8,128)S(1)} collective-permute-done((f32[512,256]{1,0:T(8,128)S(1)}, f32[512,256]{1,0:T(8,128)S(1)}, u32[]{:S(2)}, u32[]{:S(2)}) %collective-permute-start.6) | collective-permute-done | bytes 524320 | tf_op jit(solution)/shard_map/ppermute | solution.py:319
  65.6 3.9 %collective-permute-done.10.refs_7_ = f32[512,256]{1,0:T(8,128)S(1)} collective-permute-done((f32[512,256]{1,0:T(8,128)S(1)}, f32[512,256]{1,0:T(8,128)S(1)}, u32[]{:S(2)}, u32[]{:S(2)}) %collective-permute-start.10) | collective-permute-done | bytes 524320 | tf_op jit(solution)/shard_map/ppermute | solution.py:218
  69.5 2.1 %collective-permute-start.11 = (f32[512,256]{1,0:T(8,128)S(1)}, f32[512,256]{1,0:T(8,128)}, u32[]{:S(2)}, u32[]{:S(2)}) collective-permute-start(f32[512,256]{1,0:T(8,128)S(1)} %broadcast_select_fusion.refs_11_), channel_id=1, source_target_pairs={{0,2},{1,3},{2,0},{3,1},{4,6},{5,7},{6,4},{7,5},{8,10},{9,11},{10,... | collective-permute-start | bytes 1572872 | tf_op jit(solution)/shard_map/ppermute | solution.py:218
  71.6 1.3 collective-permute-start.7
  72.9 3.9 %collective-permute-done.7 = f32[256,256]{1,0:T(8,128)S(1)} collective-permute-done((f32[256,256]{1,0:T(8,128)S(1)}, f32[256,256]{1,0:T(8,128)S(1)}, u32[]{:S(2)}, u32[]{:S(2)}) %collective-permute-start.7) | collective-permute-done | bytes 262176 | tf_op jit(solution)/shard_map/ppermute | solution.py:319
  76.7 4.6 %collective-permute-start.8 = (f32[256,256]{1,0:T(8,128)S(1)}, f32[256,256]{1,0:T(8,128)S(1)}, u32[]{:S(2)}, u32[]{:S(2)}) collective-permute-start(f32[256,256]{1,0:T(8,128)S(1)} %collective-permute-done.3.refs_8_), channel_id=1, source_target_pairs={{0,4},{1,5},{2,6},{3,7},{8,12},{9,13},{10,14},{11,15},{16,20},{17,... | collective-permute-start | bytes 786440 | tf_op jit(solution)/shard_map/ppermute | solution.py:319
  81.5 0.5 collective-permute-start.15
  82.1 2.9 %collective-permute-done.8 = f32[256,256]{1,0:T(8,128)S(1)} collective-permute-done((f32[256,256]{1,0:T(8,128)S(1)}, f32[256,256]{1,0:T(8,128)S(1)}, u32[]{:S(2)}, u32[]{:S(2)}) %collective-permute-start.8) | collective-permute-done | bytes 262176 | tf_op jit(solution)/shard_map/ppermute | solution.py:319
  85.0 5.2 %collective-permute-done.12.refs_9_ = f32[256,256]{1,0:T(8,128)} collective-permute-done((f32[256,256]{1,0:T(8,128)S(1)}, f32[256,256]{1,0:T(8,128)}, u32[]{:S(2)}, u32[]{:S(2)}) %collective-permute-start.12) | collective-permute-done | bytes 262176 | tf_op jit(solution)/shard_map/ppermute | solution.py:218
  90.3 6.4 %collective-permute-done.13.refs_10_ = f32[256,256]{1,0:T(8,128)S(1)} collective-permute-done((f32[256,256]{1,0:T(8,128)S(1)}, f32[256,256]{1,0:T(8,128)S(1)}, u32[]{:S(2)}, u32[]{:S(2)}) %collective-permute-start.13) | collective-permute-done | bytes 262176 | tf_op jit(solution)/shard_map/ppermute | solution.py:218
  96.7 0.9 copy.19.refs_1_
  97.6 0.5 collective-permute-start.19
  98.1 0.4 collective-permute-start.21
  98.6 0.4 collective-permute-start.23
  99.1 13.4 %early.1 = (bf16[512,1024]{1,0:T(8,128)(2,1)}, bf16[512,1024]{1,0:T(8,128)(2,1)}, f32[512,512]{1,0:T(8,128)}, f32[512,256]{1,0:T(8,128)}, f32[512,256]{1,0:T(8,1...) custom-call(f32[4]{0:T(128)} %pad_maximum_fusion.1.refs_0_, f32[512,1]{1,0:T(8,128)} %copy.19.refs_1_, f32[1,512]{1,0:T(1,128)} %bitcast.49, ...), custom_call_target="tpu_custom_call" | custom-call | flops 8053063680 | bytes 11534336 | tf_op jit(solution)/shard_map/early/pallas_call | solution.py:44
  112.6 0.7 copy-done.18
  113.4 0.1 copy-done.19
  113.5 0.1 copy-done.26
  113.6 0.1 copy-done.20
  113.8 15.4 %late.1 = (f32[512,512]{1,0:T(8,128)}, f32[256,256]{1,0:T(8,128)}, f32[256,256]{1,0:T(8,128)}, f32[512,256]{1,0:T(8,128)}, f32[256,256]{1,0:T(8,128)}, /*index=5*/f32[256,256]{1,0:T(8,128)}, f32[512,256]{1,0:T(8,128)}) custom-call(f32[4]{0:T(128)} %pad_maximum_fusion.refs_0_, f32[512,1]{1,0:T(8,128)} %copy.19.refs_1_, f32[1,512]{1,0:T(1,128)} %bitcast.50, ...), custom_call_target="tpu_custom_call" | custom-call | flops 8053063680 | bytes 12582912 | tf_op jit(solution)/shard_map/late/pallas_call | solution.py:44
  129.2 1.2 constant_dynamic-slice_fusion.3
  130.3 0.1 collective-permute-start.27
  130.5 1.8 collective-permute-done.27
  132.3 1.1 dynamic-slice_add_fusion
  133.6 3.4 %collective-permute-start.30 = (f32[64,512]{1,0:T(8,128)S(1)}, f32[64,512]{1,0:T(8,128)S(1)}, u32[]{:S(2)}, u32[]{:S(2)}) collective-permute-start(f32[64,512]{1,0:T(8,128)S(1)} %get-tuple-element.80), channel_id=1, source_target_pairs={{0,6},{1,7},{2,4},{3,5},{4,2},{5,3},{6,0},{7,1},{8,14},{9,15},{10,... | collective-permute-start | bytes 393224 | tf_op jit(solution)/shard_map/ppermute | solution.py:218
  137.0 0.9 collective-permute-start.24
  137.9 2.0 %collective-permute-done.28 = f32[64,512]{1,0:T(8,128)S(1)} collective-permute-done((f32[64,512]{1,0:T(8,128)S(1)}, f32[64,512]{1,0:T(8,128)S(1)}, u32[]{:S(2)}, u32[]{:S(2)}) %collective-permute-start.28) | collective-permute-done | bytes 131104 | tf_op jit(solution)/shard_map/ppermute | solution.py:218
  139.9 0.2 collective-permute-start.25
  140.0 1.9 collective-permute-done.29
  142.0 14.4 %collective-permute-done.24 = f32[256,256]{1,0:T(8,128)S(1)} collective-permute-done((f32[256,256]{1,0:T(8,128)S(1)}, f32[256,256]{1,0:T(8,128)S(1)}, u32[]{:S(2)}, u32[]{:S(2)}) %collective-permute-start.24) | collective-permute-done | bytes 262176 | tf_op jit(solution)/shard_map/ppermute | solution.py:218
  156.5 0.6 collective-permute-start.31
  157.1 0.2 broadcast_in_dim.36
  157.3 6.9 %collective-permute-done.31 = f32[64,512]{1,0:T(8,128)S(1)} collective-permute-done((f32[64,512]{1,0:T(8,128)S(1)}, f32[64,512]{1,0:T(8,128)S(1)}, u32[]{:S(2)}, u32[]{:S(2)}) %collective-permute-start.31) | collective-permute-done | bytes 131104 | tf_op jit(solution)/shard_map/ppermute | solution.py:218
  164.4 5.9 %collective-permute-done.33 = f32[64,512]{1,0:T(8,128)S(1)} collective-permute-done((f32[64,512]{1,0:T(8,128)S(1)}, f32[64,512]{1,0:T(8,128)S(1)}, u32[]{:S(2)}, u32[]{:S(2)}) %collective-permute-start.33) | collective-permute-done | bytes 131104 | tf_op jit(solution)/shard_map/ppermute | solution.py:218
  170.3 0.4 collective-permute-start.35
  170.7 0.5 collective-permute-start.36
  171.2 2.6 %collective-permute-start.37 = (f32[64,512]{1,0:T(8,128)S(1)}, f32[64,512]{1,0:T(8,128)S(1)}, u32[]{:S(2)}, u32[]{:S(2)}) collective-permute-start(f32[64,512]{1,0:T(8,128)S(1)} %add.179), channel_id=1, source_target_pairs={{0,6},{1,7},{2,4},{3,5},{4,2},{5,3},{6,0},{7,1},{8,14},{9,15},{10,... | collective-permute-start | bytes 393224 | tf_op jit(solution)/shard_map/ppermute | solution.py:218
  174.0 2.0 %collective-permute-start.34 = (f32[256,256]{1,0:T(8,128)S(1)}, f32[256,256]{1,0:T(8,128)S(1)}, u32[]{:S(2)}, u32[]{:S(2)}) collective-permute-start(f32[256,256]{1,0:T(8,128)S(1)} %copy-done.21), channel_id=1, source_target_pairs={{0,24},{8,16},{16,8},{24,0},{1,25},{9,17},{17,9},{25,1},{2,26},{10... | collective-permute-start | bytes 786440 | tf_op jit(solution)/shard_map/ppermute | solution.py:218
  176.1 1.1 collective-permute-done.37
  177.2 13.2 %collective-permute-done.32 = f32[256,256]{1,0:T(8,128)S(1)} collective-permute-done((f32[256,256]{1,0:T(8,128)S(1)}, f32[256,256]{1,0:T(8,128)S(1)}, u32[]{:S(2)}, u32[]{:S(2)}) %collective-permute-start.32) | collective-permute-done | bytes 262176 | tf_op jit(solution)/shard_map/ppermute | solution.py:218
  190.4 4.7 %collective-permute-done.34 = f32[256,256]{1,0:T(8,128)S(1)} collective-permute-done((f32[256,256]{1,0:T(8,128)S(1)}, f32[256,256]{1,0:T(8,128)S(1)}, u32[]{:S(2)}, u32[]{:S(2)}) %collective-permute-start.34) | collective-permute-done | bytes 262176 | tf_op jit(solution)/shard_map/ppermute | solution.py:218
  195.1 1.2 maximum_select_fusion
  196.3 0.4 copy-done.1
  (119 shorter events, 2.0 us)
Async XLA Ops:
  0.6 6.7 %copy-start.14 = (f32[32]{0:T(128)S(1)}, f32[32]{0:T(128)}, u32[]{:S(2)}) copy-start(f32[32]{0:T(128)} %param.6) | copy-start | bytes 388
  0.6 18.0 %copy-start.13 = (s32[32,8,16]{0,2,1:T(8,128)S(1)}, s32[32,8,16]{0,2,1:T(8,128)}, u32[]{:S(2)}) copy-start(s32[32,8,16]{0,2,1:T(8,128)} %param.8) | copy-start | bytes 49156
  2.2 24.8 %copy-start = (f32[512,256]{1,0:T(8,128)}, f32[512,256]{1,0:T(8,128)S(1)}, u32[]{:S(2)}) copy-start(f32[512,256]{1,0:T(8,128)S(1)} %get-tuple-element.76.refs_4_) | copy-start | bytes 1572868
  2.2 19.7 %collective-permute-start.1 = (f32[512,256]{1,0:T(8,128)S(1)}, f32[512,256]{1,0:T(8,128)S(1)}, u32[]{:S(2)}, u32[]{:S(2)}) collective-permute-start(f32[512,256]{1,0:T(8,128)S(1)} %get-tuple-element.76.refs_4_), channel_id=1, source_target_pairs={{0,4},{1,5},{2,6},{3,7},{8,12},{9,13},{10,14},{11,15},{16,20},{17,... | collective-permute-start | bytes 1572872 | tf_op jit(solution)/shard_map/ppermute | solution.py:319
  5.6 16.3 %collective-permute-start = (f32[512,256]{1,0:T(8,128)S(1)}, f32[512,256]{1,0:T(8,128)S(1)}, u32[]{:S(2)}, u32[]{:S(2)}) collective-permute-start(f32[512,256]{1,0:T(8,128)S(1)} %get-tuple-element.75), channel_id=1, source_target_pairs={{0,8},{8,0},{16,24},{24,16},{1,9},{9,1},{17,25},{25,17},{2,10},{10... | collective-permute-start | bytes 1572872 | tf_op jit(solution)/shard_map/ppermute | solution.py:218
  18.2 28.0 %collective-permute-start.5 = (f32[512,256]{1,0:T(8,128)S(1)}, f32[512,256]{1,0:T(8,128)S(1)}, u32[]{:S(2)}, u32[]{:S(2)}) collective-permute-start(f32[512,256]{1,0:T(8,128)S(1)} %get-tuple-element.39), channel_id=1, source_target_pairs={{0,16},{8,24},{16,0},{24,8},{1,17},{9,25},{17,1},{25,9},{2,18},{10... | collective-permute-start | bytes 1572872 | tf_op jit(solution)/shard_map/ppermute | solution.py:218
  21.9 33.4 %copy-start.2 = (f32[512,256]{1,0:T(8,128)}, f32[512,256]{1,0:T(8,128)S(1)}, u32[]{:S(2)}) copy-start(f32[512,256]{1,0:T(8,128)S(1)} %collective-permute-done.refs_5_) | copy-start | bytes 1572868
  21.9 24.4 %collective-permute-start.2 = (f32[512,256]{1,0:T(8,128)S(1)}, f32[512,256]{1,0:T(8,128)}, u32[]{:S(2)}, u32[]{:S(2)}) collective-permute-start(f32[512,256]{1,0:T(8,128)S(1)} %collective-permute-done.refs_5_), channel_id=1, source_target_pairs={{0,4},{1,5},{2,6},{3,7},{8,12},{9,13},{10,14},{11,15},{16,20},{17,... | collective-permute-start | bytes 1572872 | tf_op jit(solution)/shard_map/ppermute | solution.py:319
  24.1 57.4 %copy-start.4 = (f32[512,256]{1,0:T(8,128)}, f32[512,256]{1,0:T(8,128)S(1)}, u32[]{:S(2)}) copy-start(f32[512,256]{1,0:T(8,128)S(1)} %broadcast_select_fusion.1.refs_9_) | copy-start | bytes 1572868
  24.1 35.4 %copy-start.8 = (f32[256,256]{1,0:T(8,128)S(1)}, f32[256,256]{1,0:T(8,128)}, u32[]{:S(2)}) copy-start(f32[256,256]{1,0:T(8,128)} %get-tuple-element.37) | copy-start | bytes 786436
  24.1 29.6 %collective-permute-start.4 = (f32[256,256]{1,0:T(8,128)}, f32[256,256]{1,0:T(8,128)S(1)}, u32[]{:S(2)}, u32[]{:S(2)}) collective-permute-start(f32[256,256]{1,0:T(8,128)} %get-tuple-element.38), channel_id=1, source_target_pairs={{0,24},{8,16},{16,8},{24,0},{1,25},{9,17},{17,9},{25,1},{2,26},{10... | collective-permute-start | bytes 786440 | tf_op jit(solution)/shard_map/ppermute | solution.py:218
  27.6 69.0 %copy-start.15 = (f32[512]{0:T(512)S(1)}, f32[512]{0:T(512)}, u32[]{:S(2)}) copy-start(f32[512]{0:T(512)} %param.7) | copy-start | bytes 6148
  27.6 27.7 %collective-permute-start.9 = (f32[512,256]{1,0:T(8,128)S(1)}, f32[512,256]{1,0:T(8,128)}, u32[]{:S(2)}, u32[]{:S(2)}) collective-permute-start(f32[512,256]{1,0:T(8,128)S(1)} %broadcast_select_fusion.1.refs_9_), channel_id=1, source_target_pairs={{0,2},{1,3},{2,0},{3,1},{4,6},{5,7},{6,4},{7,5},{8,10},{9,11},{10,... | collective-permute-start | bytes 1572872 | tf_op jit(solution)/shard_map/ppermute | solution.py:218
  46.3 38.8 %copy-start.3 = (f32[512,256]{1,0:T(8,128)}, f32[512,256]{1,0:T(8,128)S(1)}, u32[]{:S(2)}) copy-start(f32[512,256]{1,0:T(8,128)S(1)} %collective-permute-done.5.refs_6_) | copy-start | bytes 1572868
  53.7 31.4 %copy-start.9 = (f32[256,256]{1,0:T(8,128)}, f32[256,256]{1,0:T(8,128)S(1)}, u32[]{:S(2)}) copy-start(f32[256,256]{1,0:T(8,128)S(1)} %collective-permute-done.4.refs_7_) | copy-start | bytes 786436
  53.7 11.8 %collective-permute-start.6 = (f32[512,256]{1,0:T(8,128)S(1)}, f32[512,256]{1,0:T(8,128)S(1)}, u32[]{:S(2)}, u32[]{:S(2)}) collective-permute-start(f32[512,256]{1,0:T(8,128)S(1)} %collective-permute-done.5.refs_6_), channel_id=1, source_target_pairs={{0,4},{1,5},{2,6},{3,7},{8,12},{9,13},{10,14},{11,15},{16,20},{17,... | collective-permute-start | bytes 1572872 | tf_op jit(solution)/shard_map/ppermute | solution.py:319
  55.3 43.7 %copy-start.5 = (f32[512,256]{1,0:T(8,128)}, f32[512,256]{1,0:T(8,128)S(1)}, u32[]{:S(2)}) copy-start(f32[512,256]{1,0:T(8,128)S(1)} %broadcast_select_fusion.2.refs_10_) | copy-start | bytes 1572868
  55.4 14.1 %collective-permute-start.10 = (f32[512,256]{1,0:T(8,128)S(1)}, f32[512,256]{1,0:T(8,128)S(1)}, u32[]{:S(2)}, u32[]{:S(2)}) collective-permute-start(f32[512,256]{1,0:T(8,128)S(1)} %broadcast_select_fusion.2.refs_10_), channel_id=1, source_target_pairs={{0,2},{1,3},{2,0},{3,1},{4,6},{5,7},{6,4},{7,5},{8,10},{9,11},{10,... | collective-permute-start | bytes 1572872 | tf_op jit(solution)/shard_map/ppermute | solution.py:218
  59.5 12.1 %collective-permute-start.3 = (f32[256,256]{1,0:T(8,128)S(1)}, f32[256,256]{1,0:T(8,128)S(1)}, u32[]{:S(2)}, u32[]{:S(2)}) collective-permute-start(f32[256,256]{1,0:T(8,128)S(1)} %copy-done.8), channel_id=1, source_target_pairs={{0,24},{8,16},{16,8},{24,0},{1,25},{9,17},{17,9},{25,1},{2,26},{10... | collective-permute-start | bytes 786440 | tf_op jit(solution)/shard_map/ppermute | solution.py:218
  65.6 33.5 %copy-start.6 = (f32[512,256]{1,0:T(8,128)}, f32[512,256]{1,0:T(8,128)S(1)}, u32[]{:S(2)}) copy-start(f32[512,256]{1,0:T(8,128)S(1)} %broadcast_select_fusion.refs_11_) | copy-start | bytes 1572868
  69.5 27.2 %copy-start.17 = (f32[512,256]{1,0:T(8,128)}, f32[512,256]{1,0:T(8,128)S(1)}, u32[]{:S(2)}) copy-start(f32[512,256]{1,0:T(8,128)S(1)} %collective-permute-done.10.refs_7_) | copy-start | bytes 1572868
  69.5 11.9 %collective-permute-start.11 = (f32[512,256]{1,0:T(8,128)S(1)}, f32[512,256]{1,0:T(8,128)}, u32[]{:S(2)}, u32[]{:S(2)}) collective-permute-start(f32[512,256]{1,0:T(8,128)S(1)} %broadcast_select_fusion.refs_11_), channel_id=1, source_target_pairs={{0,2},{1,3},{2,0},{3,1},{4,6},{5,7},{6,4},{7,5},{8,10},{9,11},{10,... | collective-permute-start | bytes 1572872 | tf_op jit(solution)/shard_map/ppermute | solution.py:218
  71.6 18.7 %copy-start.10 = (f32[256,256]{1,0:T(8,128)}, f32[256,256]{1,0:T(8,128)S(1)}, u32[]{:S(2)}) copy-start(f32[256,256]{1,0:T(8,128)S(1)} %collective-permute-done.3.refs_8_) | copy-start | bytes 786436
  71.6 5.2 %collective-permute-start.7 = (f32[256,256]{1,0:T(8,128)S(1)}, f32[256,256]{1,0:T(8,128)S(1)}, u32[]{:S(2)}, u32[]{:S(2)}) collective-permute-start(f32[256,256]{1,0:T(8,128)S(1)} %collective-permute-done.4.refs_7_), channel_id=1, source_target_pairs={{0,4},{1,5},{2,6},{3,7},{8,12},{9,13},{10,14},{11,15},{16,20},{17,... | collective-permute-start | bytes 786440 | tf_op jit(solution)/shard_map/ppermute | solution.py:319
  76.7 8.3 %collective-permute-start.8 = (f32[256,256]{1,0:T(8,128)S(1)}, f32[256,256]{1,0:T(8,128)S(1)}, u32[]{:S(2)}, u32[]{:S(2)}) collective-permute-start(f32[256,256]{1,0:T(8,128)S(1)} %collective-permute-done.3.refs_8_), channel_id=1, source_target_pairs={{0,4},{1,5},{2,6},{3,7},{8,12},{9,13},{10,14},{11,15},{16,20},{17,... | collective-permute-start | bytes 786440 | tf_op jit(solution)/shard_map/ppermute | solution.py:319
  81.3 17.7 %copy-start.11 = (f32[256,256]{1,0:T(8,128)}, f32[256,256]{1,0:T(8,128)S(1)}, u32[]{:S(2)}) copy-start(f32[256,256]{1,0:T(8,128)S(1)} %broadcast_select_fusion.3.refs_12_) | copy-start | bytes 786436
  81.4 8.9 %collective-permute-start.12 = (f32[256,256]{1,0:T(8,128)S(1)}, f32[256,256]{1,0:T(8,128)}, u32[]{:S(2)}, u32[]{:S(2)}) collective-permute-start(f32[256,256]{1,0:T(8,128)S(1)} %broadcast_select_fusion.3.refs_12_), channel_id=1, source_target_pairs={{0,2},{1,3},{2,0},{3,1},{4,6},{5,7},{6,4},{7,5},{8,10},{9,11},{10,... | collective-permute-start | bytes 786440 | tf_op jit(solution)/shard_map/ppermute | solution.py:218
  81.5 16.1 %collective-permute-start.14 = (f32[512,256]{1,0:T(8,128)S(1)}, f32[512,256]{1,0:T(8,128)}, u32[]{:S(2)}, u32[]{:S(2)}) collective-permute-start(f32[512,256]{1,0:T(8,128)S(1)} %broadcast_select_fusion.1.refs_9_), channel_id=1, source_target_pairs={{0,1},{1,0},{2,3},{3,2},{4,5},{5,4},{6,7},{7,6},{8,9},{9,8},{10,11... | collective-permute-start | bytes 1572872 | tf_op jit(solution)/shard_map/ppermute | solution.py:218
  81.5 16.5 %collective-permute-start.15 = (f32[512,256]{1,0:T(8,128)S(1)}, f32[512,256]{1,0:T(8,128)}, u32[]{:S(2)}, u32[]{:S(2)}) collective-permute-start(f32[512,256]{1,0:T(8,128)S(1)} %broadcast_select_fusion.2.refs_10_), channel_id=1, source_target_pairs={{0,1},{1,0},{2,3},{3,2},{4,5},{5,4},{6,7},{7,6},{8,9},{9,8},{10,11... | collective-permute-start | bytes 1572872 | tf_op jit(solution)/shard_map/ppermute | solution.py:218
  82.0 16.5 %collective-permute-start.16 = (f32[512,256]{1,0:T(8,128)S(1)}, f32[512,256]{1,0:T(8,128)}, u32[]{:S(2)}, u32[]{:S(2)}) collective-permute-start(f32[512,256]{1,0:T(8,128)S(1)} %broadcast_select_fusion.refs_11_), channel_id=1, source_target_pairs={{0,1},{1,0},{2,3},{3,2},{4,5},{5,4},{6,7},{7,6},{8,9},{9,8},{10,11... | collective-permute-start | bytes 1572872 | tf_op jit(solution)/shard_map/ppermute | solution.py:218
  85.0 14.1 %copy-start.12 = (f32[256,256]{1,0:T(8,128)}, f32[256,256]{1,0:T(8,128)S(1)}, u32[]{:S(2)}) copy-start(f32[256,256]{1,0:T(8,128)S(1)} %broadcast_select_fusion.4.refs_13_) | copy-start | bytes 786436
  90.3 6.4 %collective-permute-start.13 = (f32[256,256]{1,0:T(8,128)S(1)}, f32[256,256]{1,0:T(8,128)S(1)}, u32[]{:S(2)}, u32[]{:S(2)}) collective-permute-start(f32[256,256]{1,0:T(8,128)S(1)} %broadcast_select_fusion.4.refs_13_), channel_id=1, source_target_pairs={{0,2},{1,3},{2,0},{3,1},{4,6},{5,7},{6,4},{7,5},{8,10},{9,11},{10,... | collective-permute-start | bytes 786440 | tf_op jit(solution)/shard_map/ppermute | solution.py:218
  90.3 7.8 %collective-permute-start.17 = (f32[256,256]{1,0:T(8,128)S(1)}, f32[256,256]{1,0:T(8,128)}, u32[]{:S(2)}, u32[]{:S(2)}) collective-permute-start(f32[256,256]{1,0:T(8,128)S(1)} %broadcast_select_fusion.3.refs_12_), channel_id=1, source_target_pairs={{0,1},{1,0},{2,3},{3,2},{4,5},{5,4},{6,7},{7,6},{8,9},{9,8},{10,11... | collective-permute-start | bytes 786440 | tf_op jit(solution)/shard_map/ppermute | solution.py:218
  96.7 15.9 %copy-start.25 = (f32[256,256]{1,0:T(8,128)}, f32[256,256]{1,0:T(8,128)S(1)}, u32[]{:S(2)}) copy-start(f32[256,256]{1,0:T(8,128)S(1)} %collective-permute-done.13.refs_10_) | copy-start | bytes 786436
  96.7 2.0 %collective-permute-start.18 = (f32[256,256]{1,0:T(8,128)S(1)}, f32[256,256]{1,0:T(8,128)}, u32[]{:S(2)}, u32[]{:S(2)}) collective-permute-start(f32[256,256]{1,0:T(8,128)S(1)} %broadcast_select_fusion.4.refs_13_), channel_id=1, source_target_pairs={{0,1},{1,0},{2,3},{3,2},{4,5},{5,4},{6,7},{7,6},{8,9},{9,8},{10,11... | collective-permute-start | bytes 786440 | tf_op jit(solution)/shard_map/ppermute | solution.py:218
  97.6 15.0 %collective-permute-start.19 = (f32[512,256]{1,0:T(8,128)}, f32[512,256]{1,0:T(8,128)S(1)}, u32[]{:S(2)}, u32[]{:S(2)}) collective-permute-start(f32[512,256]{1,0:T(8,128)} %collective-permute-done.9.refs_6_), channel_id=1, source_target_pairs={{0,1},{1,0},{2,3},{3,2},{4,5},{5,4},{6,7},{7,6},{8,9},{9,8},{10,11... | collective-permute-start | bytes 1572872 | tf_op jit(solution)/shard_map/ppermute | solution.py:218
  98.0 14.5 %collective-permute-start.20 = (f32[512,256]{1,0:T(8,128)}, f32[512,256]{1,0:T(8,128)S(1)}, u32[]{:S(2)}, u32[]{:S(2)}) collective-permute-start(f32[512,256]{1,0:T(8,128)} %copy-done.17), channel_id=1, source_target_pairs={{0,1},{1,0},{2,3},{3,2},{4,5},{5,4},{6,7},{7,6},{8,9},{9,8},{10,11... | collective-permute-start | bytes 1572872 | tf_op jit(solution)/shard_map/ppermute | solution.py:218
  98.1 14.5 %collective-permute-start.21 = (f32[512,256]{1,0:T(8,128)}, f32[512,256]{1,0:T(8,128)S(1)}, u32[]{:S(2)}, u32[]{:S(2)}) collective-permute-start(f32[512,256]{1,0:T(8,128)} %collective-permute-done.11.refs_8_), channel_id=1, source_target_pairs={{0,1},{1,0},{2,3},{3,2},{4,5},{5,4},{6,7},{7,6},{8,9},{9,8},{10,11... | collective-permute-start | bytes 1572872 | tf_op jit(solution)/shard_map/ppermute | solution.py:218
  98.6 14.0 %collective-permute-start.22 = (f32[256,256]{1,0:T(8,128)}, f32[256,256]{1,0:T(8,128)S(1)}, u32[]{:S(2)}, u32[]{:S(2)}) collective-permute-start(f32[256,256]{1,0:T(8,128)} %collective-permute-done.12.refs_9_), channel_id=1, source_target_pairs={{0,1},{1,0},{2,3},{3,2},{4,5},{5,4},{6,7},{7,6},{8,9},{9,8},{10,11... | collective-permute-start | bytes 786440 | tf_op jit(solution)/shard_map/ppermute | solution.py:218
  98.6 14.0 %collective-permute-start.23 = (f32[256,256]{1,0:T(8,128)S(1)}, f32[256,256]{1,0:T(8,128)}, u32[]{:S(2)}, u32[]{:S(2)}) collective-permute-start(f32[256,256]{1,0:T(8,128)S(1)} %collective-permute-done.13.refs_10_), channel_id=1, source_target_pairs={{0,1},{1,0},{2,3},{3,2},{4,5},{5,4},{6,7},{7,6},{8,9},{9,8},{10,11... | collective-permute-start | bytes 786440 | tf_op jit(solution)/shard_map/ppermute | solution.py:218
  112.6 1.0 copy-start.26
  112.6 1.2 copy-start.20
  129.1 7.9 %copy-start.16 = (f32[512,256]{1,0:T(8,128)S(1)}, f32[512,256]{1,0:T(8,128)}, u32[]{:S(2)}) copy-start(f32[512,256]{1,0:T(8,128)} %get-tuple-element.60) | copy-start | bytes 1572868
  129.2 7.9 %copy-start.24 = (f32[256,256]{1,0:T(8,128)S(1)}, f32[256,256]{1,0:T(8,128)}, u32[]{:S(2)}) copy-start(f32[256,256]{1,0:T(8,128)} %get-tuple-element.58) | copy-start | bytes 786436
  129.2 10.7 %copy-start.23 = (f32[256,256]{1,0:T(8,128)S(1)}, f32[256,256]{1,0:T(8,128)}, u32[]{:S(2)}) copy-start(f32[256,256]{1,0:T(8,128)} %get-tuple-element.59) | copy-start | bytes 786436
  130.3 2.0 %collective-permute-start.27 = (f32[256,512]{1,0:T(8,128)S(1)}, f32[256,512]{1,0:T(8,128)S(1)}, u32[]{:S(2)}, u32[]{:S(2)}) collective-permute-start(f32[256,512]{1,0:T(8,128)S(1)} %constant_dynamic-slice_fusion.3), channel_id=1, source_target_pairs={{0,1},{1,0},{2,3},{3,2},{4,5},{5,4},{6,7},{7,6},{8,9},{9,8},{10,11... | collective-permute-start | bytes 1572872 | tf_op jit(solution)/shard_map/ppermute | solution.py:218
  133.5 6.4 %collective-permute-start.28 = (f32[64,512]{1,0:T(8,128)S(1)}, f32[64,512]{1,0:T(8,128)S(1)}, u32[]{:S(2)}, u32[]{:S(2)}) collective-permute-start(f32[64,512]{1,0:T(8,128)S(1)} %get-tuple-element.79), channel_id=1, source_target_pairs={{0,2},{1,3},{2,0},{3,1},{4,6},{5,7},{6,4},{7,5},{8,10},{9,11},{10,... | collective-permute-start | bytes 393224 | tf_op jit(solution)/shard_map/ppermute | solution.py:218
  133.6 8.4 %collective-permute-start.29 = (f32[64,512]{1,0:T(8,128)S(1)}, f32[64,512]{1,0:T(8,128)S(1)}, u32[]{:S(2)}, u32[]{:S(2)}) collective-permute-start(f32[64,512]{1,0:T(8,128)S(1)} %get-tuple-element.81), channel_id=1, source_target_pairs={{0,4},{1,5},{2,6},{3,7},{4,0},{5,1},{6,2},{7,3},{8,12},{9,13},{10,... | collective-permute-start | bytes 393224 | tf_op jit(solution)/shard_map/ppermute | solution.py:218
  133.6 8.3 %collective-permute-start.30 = (f32[64,512]{1,0:T(8,128)S(1)}, f32[64,512]{1,0:T(8,128)S(1)}, u32[]{:S(2)}, u32[]{:S(2)}) collective-permute-start(f32[64,512]{1,0:T(8,128)S(1)} %get-tuple-element.80), channel_id=1, source_target_pairs={{0,6},{1,7},{2,4},{3,5},{4,2},{5,3},{6,0},{7,1},{8,14},{9,15},{10,... | collective-permute-start | bytes 393224 | tf_op jit(solution)/shard_map/ppermute | solution.py:218
  137.0 27.2 %collective-permute-start.26 = (f32[512,256]{1,0:T(8,128)S(1)}, f32[512,256]{1,0:T(8,128)S(1)}, u32[]{:S(2)}, u32[]{:S(2)}) collective-permute-start(f32[512,256]{1,0:T(8,128)S(1)} %copy-done.16), channel_id=1, source_target_pairs={{0,8},{8,0},{16,24},{24,16},{1,9},{9,1},{17,25},{25,17},{2,10},{10... | collective-permute-start | bytes 1572872 | tf_op jit(solution)/shard_map/ppermute | solution.py:218
  137.0 19.4 %collective-permute-start.24 = (f32[256,256]{1,0:T(8,128)S(1)}, f32[256,256]{1,0:T(8,128)S(1)}, u32[]{:S(2)}, u32[]{:S(2)}) collective-permute-start(f32[256,256]{1,0:T(8,128)S(1)} %copy-done.24), channel_id=1, source_target_pairs={{0,16},{8,24},{16,0},{24,8},{1,17},{9,25},{17,1},{25,9},{2,18},{10... | collective-permute-start | bytes 786440 | tf_op jit(solution)/shard_map/ppermute | solution.py:218
  139.9 24.3 %collective-permute-start.25 = (f32[256,256]{1,0:T(8,128)S(1)}, f32[256,256]{1,0:T(8,128)S(1)}, u32[]{:S(2)}, u32[]{:S(2)}) collective-permute-start(f32[256,256]{1,0:T(8,128)S(1)} %copy-done.23), channel_id=1, source_target_pairs={{0,16},{8,24},{16,0},{24,8},{1,17},{9,25},{17,1},{25,9},{2,18},{10... | collective-permute-start | bytes 786440 | tf_op jit(solution)/shard_map/ppermute | solution.py:218
  142.0 31.9 %copy-start.22 = (f32[256,256]{1,0:T(8,128)S(1)}, f32[256,256]{1,0:T(8,128)}, u32[]{:S(2)}) copy-start(f32[256,256]{1,0:T(8,128)} %get-tuple-element.64) | copy-start | bytes 786436
  142.0 32.0 %copy-start.21 = (f32[256,256]{1,0:T(8,128)S(1)}, f32[256,256]{1,0:T(8,128)}, u32[]{:S(2)}) copy-start(f32[256,256]{1,0:T(8,128)} %get-tuple-element.67) | copy-start | bytes 786436
  156.5 7.7 %collective-permute-start.31 = (f32[64,512]{1,0:T(8,128)S(1)}, f32[64,512]{1,0:T(8,128)S(1)}, u32[]{:S(2)}, u32[]{:S(2)}) collective-permute-start(f32[64,512]{1,0:T(8,128)S(1)} %add_add_fusion), channel_id=1, source_target_pairs={{0,8},{8,0},{16,24},{24,16},{1,9},{9,1},{17,25},{25,17},{2,10},{10... | collective-permute-start | bytes 393224 | tf_op jit(solution)/shard_map/ppermute | solution.py:218
  164.3 6.0 %collective-permute-start.33 = (f32[64,512]{1,0:T(8,128)S(1)}, f32[64,512]{1,0:T(8,128)S(1)}, u32[]{:S(2)}, u32[]{:S(2)}) collective-permute-start(f32[64,512]{1,0:T(8,128)S(1)} %add.178), channel_id=1, source_target_pairs={{0,16},{8,24},{16,0},{24,8},{1,17},{9,25},{17,1},{25,9},{2,18},{10... | collective-permute-start | bytes 393224 | tf_op jit(solution)/shard_map/ppermute | solution.py:218
  170.3 24.8 %copy-start.7 = (f32[512,256]{1,0:T(8,128)S(1)}, f32[512,256]{1,0:T(8,128)}, u32[]{:S(2)}) copy-start(f32[512,256]{1,0:T(8,128)} %get-tuple-element.68) | copy-start | bytes 1572868
  170.3 5.7 %collective-permute-start.35 = (f32[64,512]{1,0:T(8,128)S(1)}, f32[64,512]{1,0:T(8,128)S(1)}, u32[]{:S(2)}, u32[]{:S(2)}) collective-permute-start(f32[64,512]{1,0:T(8,128)S(1)} %add.179), channel_id=1, source_target_pairs={{0,2},{1,3},{2,0},{3,1},{4,6},{5,7},{6,4},{7,5},{8,10},{9,11},{10,... | collective-permute-start | bytes 393224 | tf_op jit(solution)/shard_map/ppermute | solution.py:218
  170.7 5.3 %collective-permute-start.36 = (f32[64,512]{1,0:T(8,128)S(1)}, f32[64,512]{1,0:T(8,128)S(1)}, u32[]{:S(2)}, u32[]{:S(2)}) collective-permute-start(f32[64,512]{1,0:T(8,128)S(1)} %add.179), channel_id=1, source_target_pairs={{0,4},{1,5},{2,6},{3,7},{4,0},{5,1},{6,2},{7,3},{8,12},{9,13},{10,... | collective-permute-start | bytes 393224 | tf_op jit(solution)/shard_map/ppermute | solution.py:218
  171.2 5.9 %collective-permute-start.37 = (f32[64,512]{1,0:T(8,128)S(1)}, f32[64,512]{1,0:T(8,128)S(1)}, u32[]{:S(2)}, u32[]{:S(2)}) collective-permute-start(f32[64,512]{1,0:T(8,128)S(1)} %add.179), channel_id=1, source_target_pairs={{0,6},{1,7},{2,4},{3,5},{4,2},{5,3},{6,0},{7,1},{8,14},{9,15},{10,... | collective-permute-start | bytes 393224 | tf_op jit(solution)/shard_map/ppermute | solution.py:218
  173.9 16.4 %collective-permute-start.32 = (f32[256,256]{1,0:T(8,128)S(1)}, f32[256,256]{1,0:T(8,128)S(1)}, u32[]{:S(2)}, u32[]{:S(2)}) collective-permute-start(f32[256,256]{1,0:T(8,128)S(1)} %copy-done.22), channel_id=1, source_target_pairs={{0,24},{8,16},{16,8},{24,0},{1,25},{9,17},{17,9},{25,1},{2,26},{10... | collective-permute-start | bytes 786440 | tf_op jit(solution)/shard_map/ppermute | solution.py:218
  174.0 21.0 %collective-permute-start.34 = (f32[256,256]{1,0:T(8,128)S(1)}, f32[256,256]{1,0:T(8,128)S(1)}, u32[]{:S(2)}, u32[]{:S(2)}) collective-permute-start(f32[256,256]{1,0:T(8,128)S(1)} %copy-done.21), channel_id=1, source_target_pairs={{0,24},{8,16},{16,8},{24,0},{1,25},{9,17},{17,9},{25,1},{2,26},{10... | collective-permute-start | bytes 786440 | tf_op jit(solution)/shard_map/ppermute | solution.py:218
  190.4 4.8 %collective-permute-start.38 = (f32[256,512]{1,0:T(8,128)S(1)}, f32[256,512]{1,0:T(8,128)S(1)}, u32[]{:S(2)}, u32[]{:S(2)}) collective-permute-start(f32[256,512]{1,0:T(8,128)S(1)} %maximum_select_fusion.1), channel_id=1, source_target_pairs={{0,1},{1,0},{2,3},{3,2},{4,5},{5,4},{6,7},{7,6},{8,9},{9,8},{10,11... | collective-permute-start | bytes 1572872 | tf_op jit(solution)/shard_map/ppermute | solution.py:218
  195.1 1.7 copy-start.1
  (2 other events, 1.8 us)

commit v4 on v3

--- a/solution.py
+++ b/solution.py
@@ -34,8 +34,7 @@
         store.wait()
 
 
-def call(kernel, name, outs, small, big, flops, scratch):
-    size = sum(at.size * at.dtype.itemsize for at in [*outs, *big])
+def call(kernel, name, outs, small, big, scratch):
     any_space = pl.BlockSpec(memory_space=pl.ANY)
     specs = [pl.BlockSpec(memory_space=pltpu.SMEM)]
     specs += [pl.BlockSpec(memory_space=pltpu.VMEM)] * (len(small) - 1)
@@ -48,7 +47,7 @@
         out_specs=[any_space] * len(outs),
         scratch_shapes=[*buffers, *scratch, *sems],
         compiler_params=pltpu.CompilerParams(vmem_limit_bytes=VMEM_LIMIT),
-        cost_estimate=pl.CostEstimate(flops=flops, bytes_accessed=size, transcendentals=0),
+        cost_estimate=pl.CostEstimate(flops=0, bytes_accessed=0, transcendentals=0),
         name=name,
     )(*small, *big)
 
@@ -157,10 +156,9 @@
     outs += [shape(nvir, width)] * parts
     wide, square = squares(nvir, naux)
     small = [scalars, virtual[:, None], virtual[None, :], masks]
-    flops = 2 * 3 * 2 * nvir * nvir * (2 * naux + nvir)
     kernel = functools.partial(early_kernel, cuts)
     scratch = [*wide, pltpu.VMEM((nvir, nvir), jnp.float32), *square]
-    outs = call(kernel, "early", outs, small, [*own, *near, *twin], flops, scratch)
+    outs = call(kernel, "early", outs, small, [*own, *near, *twin], scratch)
     return outs[:2], outs[2], list(outs[3:])
 
 
@@ -205,11 +203,10 @@
     outs = [shape(nvir, nvir)] + [shape(height, width) for _, _, height in wanted]
     wide, square = squares(nvir, naux)
     small = [scalars, virtual[:, None], virtual[None, :], masks]
-    flops = 2 * 3 * 2 * nvir * nvir * (2 * naux + nvir)
     kernel = functools.partial(late_kernel, cuts, wanted, scale)
     scratch = [pltpu.VMEM((nvir, nvir), jnp.float32), *wide, *square, *wide, *square]
     big = [*own, *far, *twin, density, *slices]
-    outs = call(kernel, "late", outs, small, big, flops, scratch)
+    outs = call(kernel, "late", outs, small, big, scratch)
     return outs[0], list(outs[1:])
 
 
@@ -255,11 +252,11 @@
     return jnp.where(side == 0, jnp.concatenate([low, high]), jnp.concatenate([high, low]))
 
 
-def gather_plane(value, other):
+def gather_plane(value):
     col = lax.axis_index("col")
     turns = range(1, lax.axis_size("col") // 2)
     terms = [value] + [exchange(value, "col", 2 * turn) for turn in turns]
-    value = after(joined(terms, col // 2), other)
+    value = joined(terms, col // 2)
     return joined([value, exchange(value, "col", 1)], col)
 
 
@@ -300,8 +297,6 @@
         rows = rows[first : first + count]
         if part == row_count - 1:
             rows = after(rows, near[0 if first == 0 else 1])
-        elif part > 1:
-            rows = after(rows, *small[2:])
         own.append(exchange(rows, "row", part) if part else rows)
 
     for at in range(len(cuts)):
@@ -325,14 +320,15 @@
         far.append(exchange(sent, "col", 2))
 
     near_twin = [exchange(piece, "col", 1) for piece in near]
-    far_twin = [exchange(piece, "col", 1) for piece in far]
     halved, density, slices = early(
-        cuts, after(small[2], far[-1]), vir_energy, small[0], own, near, near_twin
+        cuts, small[2], vir_energy, small[0], own, near, near_twin
     )
+    far_twin = [exchange(piece, "col", 1) for piece in far[:-2]]
+    far_twin += [exchange(after(piece, density), "col", 1) for piece in far[-2:]]
 
     middle, edge, half = row_count // 2, row_count - 1, nvir // 2
     others = [(at, 0, nvir) for at in range(1, edge) if at != middle]
-    wanted = [(middle, 0, half), (middle, half, half), *others]
+    wanted = [(middle, 0, nvir), *others]
     wanted += [(edge, 0, half), (edge, half, half), (0, 0, nvir)]
     scale = 1.0 / (row_count * col_count)
     total, pieces = late(
@@ -340,14 +336,14 @@
         density, slices,
     )
     ends = [exchange(piece, "row", cut[0]) for cut, piece in zip(wanted[:-3], pieces)]
-    total = after(scatter_plane(scatter_chip(total)), ends[0])
+    total = scatter_plane(scatter_chip(total))
     for bit in bits("row")[:-1]:
         total = total + exchange(total, "row", bit)
     ends.append(exchange(after(pieces[-3], total), "row", edge))
-    total = after(total, *ends[1:-1])
+    total = after(total, *ends[:-1])
     total = total + exchange(total, "row", bits("row")[-1])
     ends.append(exchange(after(pieces[-2], total), "row", edge))
-    total = gather_plane(total, ends[-2])
+    total = gather_plane(after(total, ends[-2]))
     ends.append(pieces[-1])
 
     returned = jnp.zeros_like(three_index)

time: 197 us -> 182 us (0.924)
  the two profiles are of different devices: /device:TPU:16 before, /device:TPU:0 now
where the time goes in v4:
time: 182 us; the launch traced here: 181 us
  waiting for transfers between devices  79.3 us (44%)
  starting transfers between devices  47.8 us (26%)
  Pallas kernels  28.7 us (16%)
  local copies, waits for them, and re-layouts  11.1 us (6%)
  between operations  8.82 us (5%)
  other arithmetic  5.48 us (3%)
    ppermute x33, waiting for transfers between devices, exchange(): return lax.ppermute(value, axis, [(at, at ^ bit) for at in range(size)])  67.6 us
    ppermute x33, starting transfers between devices, exchange(): return lax.ppermute(value, axis, [(at, at ^ bit) for at in range(size)])  29.6 us
    pallas_call x2, Pallas kernels, call(): pl.pallas_call(functools.partial(staged, kernel, len(small), len(big), le...  28.7 us
    ppermute x5, starting transfers between devices, on_device(): got = lax.ppermute(rows, 'col', links)  18.2 us
    ppermute x5, waiting for transfers between devices, on_device(): got = lax.ppermute(rows, 'col', links)  11.7 us
  transfers between devices with their start and end apart: 38, of which 17 were waited for; matrix products, arithmetic and copies ran while one was open for 6% of the time, Pallas kernels for 7%

profile of v4, /device:TPU:0, one launch (start us, length us, event | category | flops | bytes accessed | tf_op | source)
XLA Modules:
  0.0 181.2 jit_solution(14795342363553131035)
XLA Ops:
  0.7 1.5 dynamic-slice_bitcast_fusion
  2.2 5.7 %collective-permute-start.2 = (f32[512,256]{1,0:T(8,128)S(1)}, f32[512,256]{1,0:T(8,128)}, u32[]{:S(2)}, u32[]{:S(2)}) collective-permute-start(f32[512,256]{1,0:T(8,128)S(1)} %get-tuple-element.74.refs_4_), channel_id=1, source_target_pairs={{0,4},{1,5},{2,6},{3,7},{8,12},{9,13},{10,14},{11,15},{16,20},{17,... | collective-permute-start | bytes 1572872 | tf_op jit(solution)/shard_map/ppermute | solution.py:314
  7.9 1.6 collective-permute-start
  9.4 2.6 %collective-permute-start.1 = (f32[512,256]{1,0:T(8,128)S(1)}, f32[512,256]{1,0:T(8,128)S(1)}, u32[]{:S(2)}, u32[]{:S(2)}) collective-permute-start(f32[512,256]{1,0:T(8,128)S(1)} %get-tuple-element.72), channel_id=1, source_target_pairs={{0,16},{8,24},{16,0},{24,8},{1,17},{9,25},{17,1},{25,9},{2,18},{10... | collective-permute-start | bytes 1572872 | tf_op jit(solution)/shard_map/ppermute | solution.py:215
  12.0 0.7 fusion.2
  15.3 1.4 compare_reduce_fusion.1
  22.0 0.6 gather_fusion
  22.6 0.6 gather_fusion.1
  23.2 0.6 pad_maximum_fusion.1.refs_0_
  23.8 1.8 dynamic-slice_bitcast_fusion.3
  25.6 6.8 %collective-permute-done.refs_5_ = f32[512,256]{1,0:T(8,128)S(1)} collective-permute-done((f32[512,256]{1,0:T(8,128)S(1)}, f32[512,256]{1,0:T(8,128)S(1)}, u32[]{:S(2)}, u32[]{:S(2)}) %collective-permute-start) | collective-permute-done | bytes 524320 | tf_op jit(solution)/shard_map/ppermute | solution.py:215
  32.4 2.1 %collective-permute-start.4 = (f32[512,256]{1,0:T(8,128)S(1)}, f32[512,256]{1,0:T(8,128)}, u32[]{:S(2)}, u32[]{:S(2)}) collective-permute-start(f32[512,256]{1,0:T(8,128)S(1)} %collective-permute-done.refs_5_), channel_id=1, source_target_pairs={{0,4},{1,5},{2,6},{3,7},{8,12},{9,13},{10,14},{11,15},{16,20},{17,... | collective-permute-start | bytes 1572872 | tf_op jit(solution)/shard_map/ppermute | solution.py:314
  34.5 2.5 %collective-permute-start.3 = (f32[256,256]{1,0:T(8,128)}, f32[256,256]{1,0:T(8,128)S(1)}, u32[]{:S(2)}, u32[]{:S(2)}) collective-permute-start(f32[256,256]{1,0:T(8,128)} %get-tuple-element.34), channel_id=1, source_target_pairs={{0,24},{8,16},{16,8},{24,0},{1,25},{9,17},{17,9},{25,1},{2,26},{10... | collective-permute-start | bytes 786440 | tf_op jit(solution)/shard_map/ppermute | solution.py:215
  37.1 0.7 pad_maximum_fusion.refs_0_
  37.9 0.8 slice.37.refs_3_
  38.9 0.7 slice.34.refs_3_
  39.6 1.5 collective-permute-start.14
  41.1 2.8 %collective-permute-done.4 = f32[512,256]{1,0:T(8,128)} collective-permute-done((f32[512,256]{1,0:T(8,128)S(1)}, f32[512,256]{1,0:T(8,128)}, u32[]{:S(2)}, u32[]{:S(2)}) %collective-permute-start.4) | collective-permute-done | bytes 524320 | tf_op jit(solution)/shard_map/ppermute | solution.py:314
  43.9 4.5 %collective-permute-start.6 = (f32[512,256]{1,0:T(8,128)S(1)}, f32[512,256]{1,0:T(8,128)S(1)}, u32[]{:S(2)}, u32[]{:S(2)}) collective-permute-start(f32[512,256]{1,0:T(8,128)S(1)} %collective-permute-done.1.refs_6_), channel_id=1, source_target_pairs={{0,4},{1,5},{2,6},{3,7},{8,12},{9,13},{10,14},{11,15},{16,20},{17,... | collective-permute-start | bytes 1572872 | tf_op jit(solution)/shard_map/ppermute | solution.py:314
  48.6 3.6 %collective-permute-done.14.refs_6_ = f32[512,256]{1,0:T(8,128)} collective-permute-done((f32[512,256]{1,0:T(8,128)S(1)}, f32[512,256]{1,0:T(8,128)}, u32[]{:S(2)}, u32[]{:S(2)}) %collective-permute-start.14) | collective-permute-done | bytes 524320 | tf_op jit(solution)/shard_map/ppermute | solution.py:215
  52.2 1.5 collective-permute-start.15
  53.7 1.1 collective-permute-start.5
  54.8 3.0 %collective-permute-done.6 = f32[512,256]{1,0:T(8,128)S(1)} collective-permute-done((f32[512,256]{1,0:T(8,128)S(1)}, f32[512,256]{1,0:T(8,128)S(1)}, u32[]{:S(2)}, u32[]{:S(2)}) %collective-permute-start.6) | collective-permute-done | bytes 524320 | tf_op jit(solution)/shard_map/ppermute | solution.py:314
  57.8 6.4 %collective-permute-done.15.refs_7_ = f32[512,256]{1,0:T(8,128)} collective-permute-done((f32[512,256]{1,0:T(8,128)S(1)}, f32[512,256]{1,0:T(8,128)}, u32[]{:S(2)}, u32[]{:S(2)}) %collective-permute-start.15) | collective-permute-done | bytes 524320 | tf_op jit(solution)/shard_map/ppermute | solution.py:215
  64.3 1.5 collective-permute-start.16
  65.8 1.3 collective-permute-start.7
  67.2 0.5 collective-permute-start.10
  67.7 3.3 %collective-permute-done.7 = f32[256,256]{1,0:T(8,128)S(1)} collective-permute-done((f32[256,256]{1,0:T(8,128)S(1)}, f32[256,256]{1,0:T(8,128)S(1)}, u32[]{:S(2)}, u32[]{:S(2)}) %collective-permute-start.7) | collective-permute-done | bytes 262176 | tf_op jit(solution)/shard_map/ppermute | solution.py:314
  70.9 4.6 %collective-permute-start.8 = (f32[256,256]{1,0:T(8,128)S(1)}, f32[256,256]{1,0:T(8,128)S(1)}, u32[]{:S(2)}, u32[]{:S(2)}) collective-permute-start(f32[256,256]{1,0:T(8,128)S(1)} %collective-permute-done.5.refs_8_), channel_id=1, source_target_pairs={{0,4},{1,5},{2,6},{3,7},{8,12},{9,13},{10,14},{11,15},{16,20},{17,... | collective-permute-start | bytes 786440 | tf_op jit(solution)/shard_map/ppermute | solution.py:314
  75.7 0.9 collective-permute-start.17
  76.5 2.7 %collective-permute-done.8 = f32[256,256]{1,0:T(8,128)S(1)} collective-permute-done((f32[256,256]{1,0:T(8,128)S(1)}, f32[256,256]{1,0:T(8,128)S(1)}, u32[]{:S(2)}, u32[]{:S(2)}) %collective-permute-start.8) | collective-permute-done | bytes 262176 | tf_op jit(solution)/shard_map/ppermute | solution.py:314
  79.3 5.2 %collective-permute-done.17.refs_9_ = f32[256,256]{1,0:T(8,128)S(1)} collective-permute-done((f32[256,256]{1,0:T(8,128)S(1)}, f32[256,256]{1,0:T(8,128)S(1)}, u32[]{:S(2)}, u32[]{:S(2)}) %collective-permute-start.17) | collective-permute-done | bytes 262176 | tf_op jit(solution)/shard_map/ppermute | solution.py:215
  84.4 0.5 collective-permute-start.19
  84.9 0.5 collective-permute-start.18
  85.5 0.5 collective-permute-start.21
  86.2 0.2 copy-done.15
  86.4 0.9 copy.19.refs_1_
  87.3 13.4 %early.1 = (bf16[512,1024]{1,0:T(8,128)(2,1)}, bf16[512,1024]{1,0:T(8,128)(2,1)}, f32[512,512]{1,0:T(8,128)}, f32[512,256]{1,0:T(8,128)}, f32[512,256]{1,0:T(8,1...) custom-call(f32[4]{0:T(128)} %pad_maximum_fusion.1.refs_0_, f32[512,1]{1,0:T(8,128)} %copy.19.refs_1_, f32[1,512]{1,0:T(1,128)} %bitcast.47, ...), custom_call_target="tpu_custom_call" | custom-call | tf_op jit(solution)/shard_map/early/pallas_call | solution.py:43
  100.7 0.5 collective-permute-start.22
  101.3 1.0 collective-permute-done.22.refs_14_
  102.4 0.4 collective-permute-done.23.refs_15_
  102.8 0.3 copy-done.19
  103.1 0.4 copy-done.20
  103.5 15.3 %late.1 = (f32[512,512]{1,0:T(8,128)}, f32[512,256]{1,0:T(8,128)}, f32[512,256]{1,0:T(8,128)}, f32[256,256]{1,0:T(8,128)}, f32[256,256]{1,0:T(8,128)}, /*index=5*/f32[512,256]{1,0:T(8,128)}) custom-call(f32[4]{0:T(128)} %pad_maximum_fusion.refs_0_, f32[512,1]{1,0:T(8,128)} %copy.19.refs_1_, f32[1,512]{1,0:T(1,128)} %bitcast.48, ...), custom_call_target="tpu_custom_call" | custom-call | tf_op jit(solution)/shard_map/late/pallas_call | solution.py:43
  118.8 1.1 constant_dynamic-slice_fusion.3
  119.9 0.4 collective-permute-start.26
  120.4 1.8 collective-permute-start.25
  122.1 1.1 dynamic-slice_add_fusion
  123.3 1.6 collective-permute-start.27
  124.9 2.0 %collective-permute-start.29 = (f32[64,512]{1,0:T(8,128)S(1)}, f32[64,512]{1,0:T(8,128)S(1)}, u32[]{:S(2)}, u32[]{:S(2)}) collective-permute-start(f32[64,512]{1,0:T(8,128)S(1)} %get-tuple-element.76), channel_id=1, source_target_pairs={{0,6},{1,7},{2,4},{3,5},{4,2},{5,3},{6,0},{7,1},{8,14},{9,15},{10,... | collective-permute-start | bytes 393224 | tf_op jit(solution)/shard_map/ppermute | solution.py:215
  126.9 2.4 %collective-permute-done.27 = f32[64,512]{1,0:T(8,128)S(1)} collective-permute-done((f32[64,512]{1,0:T(8,128)S(1)}, f32[64,512]{1,0:T(8,128)S(1)}, u32[]{:S(2)}, u32[]{:S(2)}) %collective-permute-start.27) | collective-permute-done | bytes 131104 | tf_op jit(solution)/shard_map/ppermute | solution.py:215
  129.2 3.7 %collective-permute-done.28 = f32[64,512]{1,0:T(8,128)S(1)} collective-permute-done((f32[64,512]{1,0:T(8,128)S(1)}, f32[64,512]{1,0:T(8,128)S(1)}, u32[]{:S(2)}, u32[]{:S(2)}) %collective-permute-start.28) | collective-permute-done | bytes 131104 | tf_op jit(solution)/shard_map/ppermute | solution.py:215
  133.1 15.6 %collective-permute-done.30 = f32[64,512]{1,0:T(8,128)S(1)} collective-permute-done((f32[64,512]{1,0:T(8,128)S(1)}, f32[64,512]{1,0:T(8,128)S(1)}, u32[]{:S(2)}, u32[]{:S(2)}) %collective-permute-start.30) | collective-permute-done | bytes 131104 | tf_op jit(solution)/shard_map/ppermute | solution.py:215
  148.7 2.4 %collective-permute-start.31 = (f32[256,256]{1,0:T(8,128)S(1)}, f32[256,256]{1,0:T(8,128)S(1)}, u32[]{:S(2)}, u32[]{:S(2)}) collective-permute-start(f32[256,256]{1,0:T(8,128)S(1)} %copy-done.26), channel_id=1, source_target_pairs={{0,24},{8,16},{16,8},{24,0},{1,25},{9,17},{17,9},{25,1},{2,26},{10... | collective-permute-start | bytes 786440 | tf_op jit(solution)/shard_map/ppermute | solution.py:215
  151.1 0.2 broadcast_in_dim.33
  151.3 16.2 %collective-permute-done.32 = f32[64,512]{1,0:T(8,128)S(1)} collective-permute-done((f32[64,512]{1,0:T(8,128)S(1)}, f32[64,512]{1,0:T(8,128)S(1)}, u32[]{:S(2)}, u32[]{:S(2)}) %collective-permute-start.32) | collective-permute-done | bytes 131104 | tf_op jit(solution)/shard_map/ppermute | solution.py:215
  167.6 1.6 collective-permute-start.34
  169.1 2.0 %collective-permute-start.36 = (f32[64,512]{1,0:T(8,128)S(1)}, f32[64,512]{1,0:T(8,128)S(1)}, u32[]{:S(2)}, u32[]{:S(2)}) collective-permute-start(f32[64,512]{1,0:T(8,128)S(1)} %add.178), channel_id=1, source_target_pairs={{0,6},{1,7},{2,4},{3,5},{4,2},{5,3},{6,0},{7,1},{8,14},{9,15},{10,... | collective-permute-start | bytes 393224 | tf_op jit(solution)/shard_map/ppermute | solution.py:215
  171.2 1.7 collective-permute-start.33
  172.9 1.0 collective-permute-done.34
  173.8 1.9 %collective-permute-done.35 = f32[64,512]{1,0:T(8,128)S(1)} collective-permute-done((f32[64,512]{1,0:T(8,128)S(1)}, f32[64,512]{1,0:T(8,128)S(1)}, u32[]{:S(2)}, u32[]{:S(2)}) %collective-permute-start.35) | collective-permute-done | bytes 131104 | tf_op jit(solution)/shard_map/ppermute | solution.py:215
  176.0 3.5 %collective-permute-done.33 = f32[256,256]{1,0:T(8,128)S(1)} collective-permute-done((f32[256,256]{1,0:T(8,128)S(1)}, f32[256,256]{1,0:T(8,128)S(1)}, u32[]{:S(2)}, u32[]{:S(2)}) %collective-permute-start.33) | collective-permute-done | bytes 262176 | tf_op jit(solution)/shard_map/ppermute | solution.py:215
  179.6 1.2 maximum_select_fusion
  180.8 0.4 copy-done.6
  (116 shorter events, 2.1 us)
Async XLA Ops:
  0.6 11.4 %copy-start.24 = (f32[32]{0:T(128)S(1)}, f32[32]{0:T(128)}, u32[]{:S(2)}) copy-start(f32[32]{0:T(128)} %param.6) | copy-start | bytes 388
  0.6 21.2 %copy-start.22 = (s32[32,8,16]{0,2,1:T(8,128)S(1)}, s32[32,8,16]{0,2,1:T(8,128)}, u32[]{:S(2)}) copy-start(s32[32,8,16]{0,2,1:T(8,128)} %param.8) | copy-start | bytes 49156
  2.2 36.7 %copy-start = (f32[512,256]{1,0:T(8,128)}, f32[512,256]{1,0:T(8,128)S(1)}, u32[]{:S(2)}) copy-start(f32[512,256]{1,0:T(8,128)S(1)} %get-tuple-element.74.refs_4_) | copy-start | bytes 1572868
  2.2 23.4 %collective-permute-start.2 = (f32[512,256]{1,0:T(8,128)S(1)}, f32[512,256]{1,0:T(8,128)}, u32[]{:S(2)}, u32[]{:S(2)}) collective-permute-start(f32[512,256]{1,0:T(8,128)S(1)} %get-tuple-element.74.refs_4_), channel_id=1, source_target_pairs={{0,4},{1,5},{2,6},{3,7},{8,12},{9,13},{10,14},{11,15},{16,20},{17,... | collective-permute-start | bytes 1572872 | tf_op jit(solution)/shard_map/ppermute | solution.py:314
  7.9 24.5 %collective-permute-start = (f32[512,256]{1,0:T(8,128)S(1)}, f32[512,256]{1,0:T(8,128)S(1)}, u32[]{:S(2)}, u32[]{:S(2)}) collective-permute-start(f32[512,256]{1,0:T(8,128)S(1)} %get-tuple-element.73), channel_id=1, source_target_pairs={{0,8},{8,0},{16,24},{24,16},{1,9},{9,1},{17,25},{25,17},{2,10},{10... | collective-permute-start | bytes 1572872 | tf_op jit(solution)/shard_map/ppermute | solution.py:215
  9.4 31.7 %collective-permute-start.1 = (f32[512,256]{1,0:T(8,128)S(1)}, f32[512,256]{1,0:T(8,128)S(1)}, u32[]{:S(2)}, u32[]{:S(2)}) collective-permute-start(f32[512,256]{1,0:T(8,128)S(1)} %get-tuple-element.72), channel_id=1, source_target_pairs={{0,16},{8,24},{16,0},{24,8},{1,17},{9,25},{17,1},{25,9},{2,18},{10... | collective-permute-start | bytes 1572872 | tf_op jit(solution)/shard_map/ppermute | solution.py:215
  32.4 16.2 %copy-start.1 = (f32[512,256]{1,0:T(8,128)}, f32[512,256]{1,0:T(8,128)S(1)}, u32[]{:S(2)}) copy-start(f32[512,256]{1,0:T(8,128)S(1)} %collective-permute-done.refs_5_) | copy-start | bytes 1572868
  32.4 11.5 %collective-permute-start.4 = (f32[512,256]{1,0:T(8,128)S(1)}, f32[512,256]{1,0:T(8,128)}, u32[]{:S(2)}, u32[]{:S(2)}) collective-permute-start(f32[512,256]{1,0:T(8,128)S(1)} %collective-permute-done.refs_5_), channel_id=1, source_target_pairs={{0,4},{1,5},{2,6},{3,7},{8,12},{9,13},{10,14},{11,15},{16,20},{17,... | collective-permute-start | bytes 1572872 | tf_op jit(solution)/shard_map/ppermute | solution.py:314
  34.5 32.5 %copy-start.3 = (f32[512,256]{1,0:T(8,128)}, f32[512,256]{1,0:T(8,128)S(1)}, u32[]{:S(2)}) copy-start(f32[512,256]{1,0:T(8,128)S(1)} %broadcast_select_fusion.2.refs_9_) | copy-start | bytes 1572868
  34.5 9.4 %collective-permute-start.3 = (f32[256,256]{1,0:T(8,128)}, f32[256,256]{1,0:T(8,128)S(1)}, u32[]{:S(2)}, u32[]{:S(2)}) collective-permute-start(f32[256,256]{1,0:T(8,128)} %get-tuple-element.34), channel_id=1, source_target_pairs={{0,24},{8,16},{16,8},{24,0},{1,25},{9,17},{17,9},{25,1},{2,26},{10... | collective-permute-start | bytes 786440 | tf_op jit(solution)/shard_map/ppermute | solution.py:215
  39.6 46.8 %copy-start.23 = (f32[512]{0:T(512)S(1)}, f32[512]{0:T(512)}, u32[]{:S(2)}) copy-start(f32[512]{0:T(512)} %param.7) | copy-start | bytes 6148
  39.6 12.5 %collective-permute-start.14 = (f32[512,256]{1,0:T(8,128)S(1)}, f32[512,256]{1,0:T(8,128)}, u32[]{:S(2)}, u32[]{:S(2)}) collective-permute-start(f32[512,256]{1,0:T(8,128)S(1)} %broadcast_select_fusion.2.refs_9_), channel_id=1, source_target_pairs={{0,2},{1,3},{2,0},{3,1},{4,6},{5,7},{6,4},{7,5},{8,10},{9,11},{10,... | collective-permute-start | bytes 1572872 | tf_op jit(solution)/shard_map/ppermute | solution.py:215
  41.1 38.1 %copy-start.2 = (f32[512,256]{1,0:T(8,128)}, f32[512,256]{1,0:T(8,128)S(1)}, u32[]{:S(2)}) copy-start(f32[512,256]{1,0:T(8,128)S(1)} %collective-permute-done.1.refs_6_) | copy-start | bytes 1572868
  43.9 35.3 %copy-start.7 = (f32[256,256]{1,0:T(8,128)}, f32[256,256]{1,0:T(8,128)S(1)}, u32[]{:S(2)}) copy-start(f32[256,256]{1,0:T(8,128)S(1)} %collective-permute-done.3.refs_7_) | copy-start | bytes 786436
  43.9 13.8 %collective-permute-start.6 = (f32[512,256]{1,0:T(8,128)S(1)}, f32[512,256]{1,0:T(8,128)S(1)}, u32[]{:S(2)}, u32[]{:S(2)}) collective-permute-start(f32[512,256]{1,0:T(8,128)S(1)} %collective-permute-done.1.refs_6_), channel_id=1, source_target_pairs={{0,4},{1,5},{2,6},{3,7},{8,12},{9,13},{10,14},{11,15},{16,20},{17,... | collective-permute-start | bytes 1572872 | tf_op jit(solution)/shard_map/ppermute | solution.py:314
  48.5 38.7 %copy-start.4 = (f32[512,256]{1,0:T(8,128)}, f32[512,256]{1,0:T(8,128)S(1)}, u32[]{:S(2)}) copy-start(f32[512,256]{1,0:T(8,128)S(1)} %broadcast_select_fusion.1.refs_10_) | copy-start | bytes 1572868
  52.2 12.1 %collective-permute-start.15 = (f32[512,256]{1,0:T(8,128)S(1)}, f32[512,256]{1,0:T(8,128)}, u32[]{:S(2)}, u32[]{:S(2)}) collective-permute-start(f32[512,256]{1,0:T(8,128)S(1)} %broadcast_select_fusion.1.refs_10_), channel_id=1, source_target_pairs={{0,2},{1,3},{2,0},{3,1},{4,6},{5,7},{6,4},{7,5},{8,10},{9,11},{10,... | collective-permute-start | bytes 1572872 | tf_op jit(solution)/shard_map/ppermute | solution.py:215
  53.7 12.1 %collective-permute-start.5 = (f32[256,256]{1,0:T(8,128)S(1)}, f32[256,256]{1,0:T(8,128)S(1)}, u32[]{:S(2)}, u32[]{:S(2)}) collective-permute-start(f32[256,256]{1,0:T(8,128)S(1)} %get-tuple-element.36), channel_id=1, source_target_pairs={{0,24},{8,16},{16,8},{24,0},{1,25},{9,17},{17,9},{25,1},{2,26},{10... | collective-permute-start | bytes 786440 | tf_op jit(solution)/shard_map/ppermute | solution.py:215
  57.8 29.4 %copy-start.5 = (f32[512,256]{1,0:T(8,128)}, f32[512,256]{1,0:T(8,128)S(1)}, u32[]{:S(2)}) copy-start(f32[512,256]{1,0:T(8,128)S(1)} %broadcast_select_fusion.refs_11_) | copy-start | bytes 1572868
  64.3 11.4 %collective-permute-start.16 = (f32[512,256]{1,0:T(8,128)S(1)}, f32[512,256]{1,0:T(8,128)}, u32[]{:S(2)}, u32[]{:S(2)}) collective-permute-start(f32[512,256]{1,0:T(8,128)S(1)} %broadcast_select_fusion.refs_11_), channel_id=1, source_target_pairs={{0,2},{1,3},{2,0},{3,1},{4,6},{5,7},{6,4},{7,5},{8,10},{9,11},{10,... | collective-permute-start | bytes 1572872 | tf_op jit(solution)/shard_map/ppermute | solution.py:215
  65.8 21.5 %copy-start.8 = (f32[256,256]{1,0:T(8,128)}, f32[256,256]{1,0:T(8,128)S(1)}, u32[]{:S(2)}) copy-start(f32[256,256]{1,0:T(8,128)S(1)} %collective-permute-done.5.refs_8_) | copy-start | bytes 786436
  65.8 5.2 %collective-permute-start.7 = (f32[256,256]{1,0:T(8,128)S(1)}, f32[256,256]{1,0:T(8,128)S(1)}, u32[]{:S(2)}, u32[]{:S(2)}) collective-permute-start(f32[256,256]{1,0:T(8,128)S(1)} %collective-permute-done.3.refs_7_), channel_id=1, source_target_pairs={{0,4},{1,5},{2,6},{3,7},{8,12},{9,13},{10,14},{11,15},{16,20},{17,... | collective-permute-start | bytes 786440 | tf_op jit(solution)/shard_map/ppermute | solution.py:314
  67.1 17.3 %collective-permute-start.9 = (f32[512,256]{1,0:T(8,128)S(1)}, f32[512,256]{1,0:T(8,128)S(1)}, u32[]{:S(2)}, u32[]{:S(2)}) collective-permute-start(f32[512,256]{1,0:T(8,128)S(1)} %broadcast_select_fusion.2.refs_9_), channel_id=1, source_target_pairs={{0,1},{1,0},{2,3},{3,2},{4,5},{5,4},{6,7},{7,6},{8,9},{9,8},{10,11... | collective-permute-start | bytes 1572872 | tf_op jit(solution)/shard_map/ppermute | solution.py:215
  67.2 17.8 %collective-permute-start.10 = (f32[512,256]{1,0:T(8,128)S(1)}, f32[512,256]{1,0:T(8,128)S(1)}, u32[]{:S(2)}, u32[]{:S(2)}) collective-permute-start(f32[512,256]{1,0:T(8,128)S(1)} %broadcast_select_fusion.1.refs_10_), channel_id=1, source_target_pairs={{0,1},{1,0},{2,3},{3,2},{4,5},{5,4},{6,7},{7,6},{8,9},{9,8},{10,11... | collective-permute-start | bytes 1572872 | tf_op jit(solution)/shard_map/ppermute | solution.py:215
  70.9 8.3 %collective-permute-start.8 = (f32[256,256]{1,0:T(8,128)S(1)}, f32[256,256]{1,0:T(8,128)S(1)}, u32[]{:S(2)}, u32[]{:S(2)}) collective-permute-start(f32[256,256]{1,0:T(8,128)S(1)} %collective-permute-done.5.refs_8_), channel_id=1, source_target_pairs={{0,4},{1,5},{2,6},{3,7},{8,12},{9,13},{10,14},{11,15},{16,20},{17,... | collective-permute-start | bytes 786440 | tf_op jit(solution)/shard_map/ppermute | solution.py:314
  75.5 10.0 %collective-permute-start.11 = (f32[512,256]{1,0:T(8,128)S(1)}, f32[512,256]{1,0:T(8,128)S(1)}, u32[]{:S(2)}, u32[]{:S(2)}) collective-permute-start(f32[512,256]{1,0:T(8,128)S(1)} %broadcast_select_fusion.refs_11_), channel_id=1, source_target_pairs={{0,1},{1,0},{2,3},{3,2},{4,5},{5,4},{6,7},{7,6},{8,9},{9,8},{10,11... | collective-permute-start | bytes 1572872 | tf_op jit(solution)/shard_map/ppermute | solution.py:215
  75.6 11.6 %copy-start.9 = (f32[256,256]{1,0:T(8,128)}, f32[256,256]{1,0:T(8,128)S(1)}, u32[]{:S(2)}) copy-start(f32[256,256]{1,0:T(8,128)S(1)} %broadcast_select_fusion.4.refs_12_) | copy-start | bytes 786436
  75.7 8.8 %collective-permute-start.17 = (f32[256,256]{1,0:T(8,128)S(1)}, f32[256,256]{1,0:T(8,128)S(1)}, u32[]{:S(2)}, u32[]{:S(2)}) collective-permute-start(f32[256,256]{1,0:T(8,128)S(1)} %broadcast_select_fusion.4.refs_12_), channel_id=1, source_target_pairs={{0,2},{1,3},{2,0},{3,1},{4,6},{5,7},{6,4},{7,5},{8,10},{9,11},{10,... | collective-permute-start | bytes 786440 | tf_op jit(solution)/shard_map/ppermute | solution.py:215
  79.2 6.3 %collective-permute-start.12 = (f32[256,256]{1,0:T(8,128)S(1)}, f32[256,256]{1,0:T(8,128)S(1)}, u32[]{:S(2)}, u32[]{:S(2)}) collective-permute-start(f32[256,256]{1,0:T(8,128)S(1)} %broadcast_select_fusion.4.refs_12_), channel_id=1, source_target_pairs={{0,1},{1,0},{2,3},{3,2},{4,5},{5,4},{6,7},{7,6},{8,9},{9,8},{10,11... | collective-permute-start | bytes 786440 | tf_op jit(solution)/shard_map/ppermute | solution.py:215
  79.3 8.0 %copy-start.10 = (f32[256,256]{1,0:T(8,128)}, f32[256,256]{1,0:T(8,128)S(1)}, u32[]{:S(2)}) copy-start(f32[256,256]{1,0:T(8,128)S(1)} %broadcast_select_fusion.3.refs_13_) | copy-start | bytes 786436
  84.4 18.3 %copy-start.17 = (f32[256,256]{1,0:T(8,128)}, f32[256,256]{1,0:T(8,128)S(1)}, u32[]{:S(2)}) copy-start(f32[256,256]{1,0:T(8,128)S(1)} %collective-permute-done.17.refs_9_) | copy-start | bytes 786436
  84.4 2.8 %collective-permute-start.13 = (f32[256,256]{1,0:T(8,128)S(1)}, f32[256,256]{1,0:T(8,128)}, u32[]{:S(2)}, u32[]{:S(2)}) collective-permute-start(f32[256,256]{1,0:T(8,128)S(1)} %broadcast_select_fusion.3.refs_13_), channel_id=1, source_target_pairs={{0,1},{1,0},{2,3},{3,2},{4,5},{5,4},{6,7},{7,6},{8,9},{9,8},{10,11... | collective-permute-start | bytes 786440 | tf_op jit(solution)/shard_map/ppermute | solution.py:215
  84.4 1.1 copy-start.13
  84.4 16.9 %collective-permute-start.19 = (f32[512,256]{1,0:T(8,128)}, f32[512,256]{1,0:T(8,128)S(1)}, u32[]{:S(2)}, u32[]{:S(2)}) collective-permute-start(f32[512,256]{1,0:T(8,128)} %collective-permute-done.14.refs_6_), channel_id=1, source_target_pairs={{0,1},{1,0},{2,3},{3,2},{4,5},{5,4},{6,7},{7,6},{8,9},{9,8},{10,11... | collective-permute-start | bytes 1572872 | tf_op jit(solution)/shard_map/ppermute | solution.py:215
  84.9 1.1 copy-start.14
  84.9 16.3 %collective-permute-start.18 = (f32[256,256]{1,0:T(8,128)S(1)}, f32[256,256]{1,0:T(8,128)S(1)}, u32[]{:S(2)}, u32[]{:S(2)}) collective-permute-start(f32[256,256]{1,0:T(8,128)S(1)} %broadcast_select_fusion.3.refs_13_), channel_id=1, source_target_pairs={{0,2},{1,3},{2,0},{3,1},{4,6},{5,7},{6,4},{7,5},{8,10},{9,11},{10,... | collective-permute-start | bytes 786440 | tf_op jit(solution)/shard_map/ppermute | solution.py:215
  85.5 0.7 copy-start.21
  85.5 15.8 %collective-permute-start.20 = (f32[512,256]{1,0:T(8,128)}, f32[512,256]{1,0:T(8,128)S(1)}, u32[]{:S(2)}, u32[]{:S(2)}) collective-permute-start(f32[512,256]{1,0:T(8,128)} %collective-permute-done.15.refs_7_), channel_id=1, source_target_pairs={{0,1},{1,0},{2,3},{3,2},{4,5},{5,4},{6,7},{7,6},{8,9},{9,8},{10,11... | collective-permute-start | bytes 1572872 | tf_op jit(solution)/shard_map/ppermute | solution.py:215
  85.5 0.9 copy-start.15
  85.5 16.8 %collective-permute-start.21 = (f32[512,256]{1,0:T(8,128)}, f32[512,256]{1,0:T(8,128)}, u32[]{:S(2)}, u32[]{:S(2)}) collective-permute-start(f32[512,256]{1,0:T(8,128)} %collective-permute-done.16.refs_8_), channel_id=1, source_target_pairs={{0,1},{1,0},{2,3},{3,2},{4,5},{5,4},{6,7},{7,6},{8,9},{9,8},{10,11... | collective-permute-start | bytes 1572872 | tf_op jit(solution)/shard_map/ppermute | solution.py:215
  100.7 1.7 collective-permute-start.22
  101.2 1.5 copy-start.18
  101.2 1.5 collective-permute-start.23
  101.3 1.4 copy-start.11
  101.3 1.4 copy-start.12
  102.7 0.7 copy-start.20
  118.8 29.9 %copy-start.26 = (f32[256,256]{1,0:T(8,128)S(1)}, f32[256,256]{1,0:T(8,128)}, u32[]{:S(2)}) copy-start(f32[256,256]{1,0:T(8,128)} %get-tuple-element.60) | copy-start | bytes 786436
  119.9 2.2 %collective-permute-start.26 = (f32[256,512]{1,0:T(8,128)S(1)}, f32[256,512]{1,0:T(8,128)S(1)}, u32[]{:S(2)}, u32[]{:S(2)}) collective-permute-start(f32[256,512]{1,0:T(8,128)S(1)} %constant_dynamic-slice_fusion.3), channel_id=1, source_target_pairs={{0,1},{1,0},{2,3},{3,2},{4,5},{5,4},{6,7},{7,6},{8,9},{9,8},{10,11... | collective-permute-start | bytes 1572872 | tf_op jit(solution)/shard_map/ppermute | solution.py:215
  120.3 30.7 %collective-permute-start.24 = (f32[512,256]{1,0:T(8,128)}, f32[512,256]{1,0:T(8,128)S(1)}, u32[]{:S(2)}, u32[]{:S(2)}) collective-permute-start(f32[512,256]{1,0:T(8,128)} %get-tuple-element.56), channel_id=1, source_target_pairs={{0,16},{8,24},{16,0},{24,8},{1,17},{9,25},{17,1},{25,9},{2,18},{10... | collective-permute-start | bytes 1572872 | tf_op jit(solution)/shard_map/ppermute | solution.py:215
  120.4 30.7 %collective-permute-start.25 = (f32[512,256]{1,0:T(8,128)}, f32[512,256]{1,0:T(8,128)S(1)}, u32[]{:S(2)}, u32[]{:S(2)}) collective-permute-start(f32[512,256]{1,0:T(8,128)} %get-tuple-element.57), channel_id=1, source_target_pairs={{0,8},{8,0},{16,24},{24,16},{1,9},{9,1},{17,25},{25,17},{2,10},{10... | collective-permute-start | bytes 1572872 | tf_op jit(solution)/shard_map/ppermute | solution.py:215
  123.3 5.9 %collective-permute-start.27 = (f32[64,512]{1,0:T(8,128)S(1)}, f32[64,512]{1,0:T(8,128)S(1)}, u32[]{:S(2)}, u32[]{:S(2)}) collective-permute-start(f32[64,512]{1,0:T(8,128)S(1)} %get-tuple-element.75), channel_id=1, source_target_pairs={{0,2},{1,3},{2,0},{3,1},{4,6},{5,7},{6,4},{7,5},{8,10},{9,11},{10,... | collective-permute-start | bytes 393224 | tf_op jit(solution)/shard_map/ppermute | solution.py:215
  124.9 8.0 %collective-permute-start.28 = (f32[64,512]{1,0:T(8,128)S(1)}, f32[64,512]{1,0:T(8,128)S(1)}, u32[]{:S(2)}, u32[]{:S(2)}) collective-permute-start(f32[64,512]{1,0:T(8,128)S(1)} %get-tuple-element.77), channel_id=1, source_target_pairs={{0,4},{1,5},{2,6},{3,7},{4,0},{5,1},{6,2},{7,3},{8,12},{9,13},{10,... | collective-permute-start | bytes 393224 | tf_op jit(solution)/shard_map/ppermute | solution.py:215
  124.9 8.0 %collective-permute-start.29 = (f32[64,512]{1,0:T(8,128)S(1)}, f32[64,512]{1,0:T(8,128)S(1)}, u32[]{:S(2)}, u32[]{:S(2)}) collective-permute-start(f32[64,512]{1,0:T(8,128)S(1)} %get-tuple-element.76), channel_id=1, source_target_pairs={{0,6},{1,7},{2,4},{3,5},{4,2},{5,3},{6,0},{7,1},{8,14},{9,15},{10,... | collective-permute-start | bytes 393224 | tf_op jit(solution)/shard_map/ppermute | solution.py:215
  133.0 15.7 %collective-permute-start.30 = (f32[64,512]{1,0:T(8,128)S(1)}, f32[64,512]{1,0:T(8,128)S(1)}, u32[]{:S(2)}, u32[]{:S(2)}) collective-permute-start(f32[64,512]{1,0:T(8,128)S(1)} %add_add_fusion), channel_id=1, source_target_pairs={{0,8},{8,0},{16,24},{24,16},{1,9},{9,1},{17,25},{25,17},{2,10},{10... | collective-permute-start | bytes 393224 | tf_op jit(solution)/shard_map/ppermute | solution.py:215
  148.7 18.9 %collective-permute-start.31 = (f32[256,256]{1,0:T(8,128)S(1)}, f32[256,256]{1,0:T(8,128)S(1)}, u32[]{:S(2)}, u32[]{:S(2)}) collective-permute-start(f32[256,256]{1,0:T(8,128)S(1)} %copy-done.26), channel_id=1, source_target_pairs={{0,24},{8,16},{16,8},{24,0},{1,25},{9,17},{17,9},{25,1},{2,26},{10... | collective-permute-start | bytes 786440 | tf_op jit(solution)/shard_map/ppermute | solution.py:215
  151.0 20.1 %copy-start.25 = (f32[256,256]{1,0:T(8,128)S(1)}, f32[256,256]{1,0:T(8,128)}, u32[]{:S(2)}) copy-start(f32[256,256]{1,0:T(8,128)} %get-tuple-element.63) | copy-start | bytes 786436
  151.0 16.5 %collective-permute-start.32 = (f32[64,512]{1,0:T(8,128)S(1)}, f32[64,512]{1,0:T(8,128)S(1)}, u32[]{:S(2)}, u32[]{:S(2)}) collective-permute-start(f32[64,512]{1,0:T(8,128)S(1)} %add.177), channel_id=1, source_target_pairs={{0,16},{8,24},{16,0},{24,8},{1,17},{9,25},{17,1},{25,9},{2,18},{10... | collective-permute-start | bytes 393224 | tf_op jit(solution)/shard_map/ppermute | solution.py:215
  167.5 11.9 %copy-start.16 = (f32[512,256]{1,0:T(8,128)S(1)}, f32[512,256]{1,0:T(8,128)}, u32[]{:S(2)}) copy-start(f32[512,256]{1,0:T(8,128)} %get-tuple-element.64) | copy-start | bytes 1572868
  167.6 6.3 %collective-permute-start.34 = (f32[64,512]{1,0:T(8,128)S(1)}, f32[64,512]{1,0:T(8,128)S(1)}, u32[]{:S(2)}, u32[]{:S(2)}) collective-permute-start(f32[64,512]{1,0:T(8,128)S(1)} %add.178), channel_id=1, source_target_pairs={{0,2},{1,3},{2,0},{3,1},{4,6},{5,7},{6,4},{7,5},{8,10},{9,11},{10,... | collective-permute-start | bytes 393224 | tf_op jit(solution)/shard_map/ppermute | solution.py:215
  169.1 6.7 %collective-permute-start.35 = (f32[64,512]{1,0:T(8,128)S(1)}, f32[64,512]{1,0:T(8,128)S(1)}, u32[]{:S(2)}, u32[]{:S(2)}) collective-permute-start(f32[64,512]{1,0:T(8,128)S(1)} %add.178), channel_id=1, source_target_pairs={{0,4},{1,5},{2,6},{3,7},{4,0},{5,1},{6,2},{7,3},{8,12},{9,13},{10,... | collective-permute-start | bytes 393224 | tf_op jit(solution)/shard_map/ppermute | solution.py:215
  169.1 6.7 %collective-permute-start.36 = (f32[64,512]{1,0:T(8,128)S(1)}, f32[64,512]{1,0:T(8,128)S(1)}, u32[]{:S(2)}, u32[]{:S(2)}) collective-permute-start(f32[64,512]{1,0:T(8,128)S(1)} %add.178), channel_id=1, source_target_pairs={{0,6},{1,7},{2,4},{3,5},{4,2},{5,3},{6,0},{7,1},{8,14},{9,15},{10,... | collective-permute-start | bytes 393224 | tf_op jit(solution)/shard_map/ppermute | solution.py:215
  171.2 8.3 %collective-permute-start.33 = (f32[256,256]{1,0:T(8,128)S(1)}, f32[256,256]{1,0:T(8,128)S(1)}, u32[]{:S(2)}, u32[]{:S(2)}) collective-permute-start(f32[256,256]{1,0:T(8,128)S(1)} %copy-done.25), channel_id=1, source_target_pairs={{0,24},{8,16},{16,8},{24,0},{1,25},{9,17},{17,9},{25,1},{2,26},{10... | collective-permute-start | bytes 786440 | tf_op jit(solution)/shard_map/ppermute | solution.py:215
  175.9 3.7 %collective-permute-start.37 = (f32[256,512]{1,0:T(8,128)S(1)}, f32[256,512]{1,0:T(8,128)S(1)}, u32[]{:S(2)}, u32[]{:S(2)}) collective-permute-start(f32[256,512]{1,0:T(8,128)S(1)} %maximum_select_fusion.1), channel_id=1, source_target_pairs={{0,1},{1,0},{2,3},{3,2},{4,5},{5,4},{6,7},{7,6},{8,9},{9,8},{10,11... | collective-permute-start | bytes 1572872 | tf_op jit(solution)/shard_map/ppermute | solution.py:215
  179.5 1.7 copy-start.6
  (1 other events, 0.7 us)
